TPU v7x, 512 devices: a whole 4x8x8 slice. The times are simulated.
512 devices in a mesh: lat: 16 (over x, z_lo), lon: 32 (over z_hi, y, core).
Axes of the slice: x: 4, y: 8, z: 8 (z_hi: 2, z_lo: 4; z = z_hi * 4 + z_lo), core: 2. Of those that a mesh axis runs over, the one named last changes fastest.
Arguments:
- frame_one: bfloat16 [256, 1024, 256], P('lat', 'lon'), may hold values from -6 to 6
- frame_two: bfloat16 [256, 1024, 256], P('lat', 'lon'), may hold values from -6 to 6
- enc_weight: bfloat16 [3, 3, 256, 256], replicated, may hold values from -0.125 to 0.125
- mask_weight: bfloat16 [256, 576], replicated, may hold values from -0.375 to 0.375
Outputs:
- up_flow: float32 [2, 2048, 8192], P(None, 'lat', 'lon')
All inputs are finite; a program needn't handle non-finite values.
Results may differ from a plain program's by a relative error of at most 0.0011.
Values may be sent and summed in bfloat16 or wider, within the bound.
No kernel may reach another device: no remote copies, remote signals or barrier semaphores. Data moves between devices by JAX's collectives and lax.ppermute only.
A program may use at most 64 MiB of HBM per device.

v0:
```python
import functools
import math

import jax
import jax.numpy as jnp
from jax import lax
from jax.experimental import pallas as pl
from jax.experimental.pallas import tpu as pltpu
from jax.sharding import PartitionSpec as P

CH = 256
BR = 8
BC = 16
UP = 8
F32 = jnp.float32
BF16 = jnp.bfloat16
VMEM = pl.BlockSpec(memory_space=pltpu.VMEM)


def params(mib):
    return pltpu.CompilerParams(vmem_limit_bytes=mib * 1024 * 1024)


def pair_perm(size, first, wrap):
    out = []
    for i in range(first, size, 2):
        j = i + 1
        if j >= size:
            if not wrap:
                continue
            j -= size
        out += [(i, j), (j, i)]
    return out


def pack_kernel(rows, cols, f1, f2, ra, rb, m_in, m_x, ext, col):
    lat_odd = lax.axis_index("lat") % 2 == 1
    lon_odd = lax.axis_index("lon") % 2 == 1

    def halo(north, south):
        ext[0 : BR + 1] = north[0 : BR + 1]
        ext[BR + 1 : BR + 1 + rows] = f2[...]
        ext[BR + 1 + rows : 2 * BR + 2 + rows] = south[0 : BR + 1]
        ext[2 * BR + 2 + rows] = north[BR + 1]
        ext[2 * BR + 3 + rows : 2 * BR + 3 + 2 * rows] = f1[...]
        ext[2 * BR + 3 + 2 * rows] = south[BR + 1]

    @pl.when(lat_odd)
    def _():
        halo(rb, ra)

    @pl.when(jnp.logical_not(lat_odd))
    def _():
        halo(ra, rb)

    n2 = rows + 2 * BR + 2
    n1 = rows + 2
    slots2 = -(-n2 // BC)
    slots1 = -(-n1 // BC)

    def edge(msg, main, extra, one):
        msg[0:n2] = ext[0:n2, main : main + BC]
        lo = extra // BC * BC
        slab = ext[0:n2, lo : lo + BC].astype(F32)
        col[0:n2] = slab[:, extra - lo, :]
        msg[n2 : n2 + slots2] = col[0 : slots2 * BC].astype(BF16).reshape(slots2, BC, CH)
        lo = one // BC * BC
        slab = ext[n2 : n2 + n1, lo : lo + BC].astype(F32)
        col[0:n1] = slab[:, one - lo, :]
        msg[n2 + slots2 :] = col[0 : slots1 * BC].astype(BF16).reshape(slots1, BC, CH)

    def right(msg):
        edge(msg, cols - BC, cols - BC - 1, cols - 1)

    def left(msg):
        edge(msg, 0, BC, 0)

    @pl.when(lon_odd)
    def _():
        right(m_x)
        left(m_in)

    @pl.when(jnp.logical_not(lon_odd))
    def _():
        left(m_x)
        right(m_in)


def flow_kernel(rows, cols, f1, f2, ra, rb, c_in, c_x, w, flow, enc_one, s2, s1, x2, x1, e2):
    lat = lax.axis_index("lat")
    lat_odd = lat % 2 == 1
    lon_odd = lax.axis_index("lon") % 2 == 1
    n2 = rows + 2 * BR + 2
    n1 = rows + 2
    wide = cols + 2 * BC
    slots2 = -(-n2 // BC)
    slots1 = -(-n1 // BC)
    own = BR + BC

    def put_rows(north, south):
        s2[0 : BR + 1, own : own + cols] = north[0 : BR + 1].astype(F32)
        s2[BR + 1 + rows :, own : own + cols] = south[0 : BR + 1].astype(F32)
        s1[0, BR : BR + cols] = north[BR + 1].astype(F32)
        s1[n1 - 1, BR : BR + cols] = south[BR + 1].astype(F32)

    def put_cols(left, right):
        s2[:, BR : BR + BC] = left[0:n2].astype(F32)
        s2[:, own + cols : own + cols + BC] = right[0:n2].astype(F32)
        extra = left[n2 : n2 + slots2].astype(F32).reshape(slots2 * BC, CH)
        s2[:, BR - 1 : BR] = extra[0:n2][:, None, :]
        extra = right[n2 : n2 + slots2].astype(F32).reshape(slots2 * BC, CH)
        s2[:, BR + wide : BR + wide + 1] = extra[0:n2][:, None, :]
        one = left[n2 + slots2 :].astype(F32).reshape(slots1 * BC, CH)
        s1[:, BR - 1 : BR] = one[0:n1][:, None, :]
        one = right[n2 + slots2 :].astype(F32).reshape(slots1 * BC, CH)
        s1[:, BR + cols : BR + cols + 1] = one[0:n1][:, None, :]

    s2[BR + 1 : BR + 1 + rows, own : own + cols] = f2[...].astype(F32)
    s1[1 : 1 + rows, BR : BR + cols] = f1[...].astype(F32)

    @pl.when(lat_odd)
    def _():
        put_rows(rb, ra)

    @pl.when(jnp.logical_not(lat_odd))
    def _():
        put_rows(ra, rb)

    @pl.when(lon_odd)
    def _():
        put_cols(c_in, c_x)

    @pl.when(jnp.logical_not(lon_odd))
    def _():
        put_cols(c_x, c_in)

    for b in range(3):
        x2[b] = s2[:, BR - 1 + b : BR - 1 + b + wide].astype(BF16)
        x1[b] = s1[:, BR - 1 + b : BR - 1 + b + cols].astype(BF16)

    def conv(x, row, count, width):
        lhs = jnp.concatenate(
            [
                x[b, pl.ds(row + a, count)].reshape(count * width, CH)
                for a in range(3)
                for b in range(3)
            ],
            axis=1,
        )
        return jnp.dot(lhs, w[...], preferred_element_type=F32)

    half = BR // 2
    for g in range(rows // BR):
        enc_one[g * BR : g * BR + BR] = (
            conv(x1, g * BR, BR, cols).astype(BF16).reshape(BR, cols, CH)
        )
    for g in range((rows + 2 * BR) // half):
        e2[g * half : g * half + half] = (
            conv(x2, g * half, half, wide).astype(BF16).reshape(half, wide, CH)
        )

    bands = rows // BR
    queries = BR * cols
    lane = lax.broadcasted_iota(jnp.int32, (BR, queries), 1)
    sub = lax.broadcasted_iota(jnp.int32, (BR, queries), 0).astype(F32)
    q_col = lane % cols
    on_left = q_col < BC
    lefts = jnp.broadcast_to(on_left[None], (2, BR, queries))
    last = lax.axis_size("lat") - 1
    for g in range(bands):
        query = (enc_one[g * BR : g * BR + BR].reshape(queries, CH).astype(F32) * (1.0 / math.sqrt(CH))).astype(BF16)
        sums = [jnp.zeros((BR, queries), F32) for _ in range(6)]
        sum_y = jnp.zeros((BR, queries), F32)
        for kb in range(3):
            part = [jnp.zeros((BR, queries), F32) for _ in range(6)]
            part_y = jnp.zeros((BR, queries), F32)
            for kr in range(BR):
                keys = e2[(g + kb) * BR + kr]
                score = lax.dot_general(
                    keys, query, (((1,), (1,)), ((), ())), preferred_element_type=F32
                ).reshape(wide // BR, BR, queries)
                mid = jnp.exp(score[2:6])
                rim = jnp.exp(jnp.where(lefts, score[0:2], score[6:8]))
                pieces = [mid[0], mid[1], mid[2], mid[3], rim[0], rim[1]]
                total = (pieces[0] + pieces[1]) + (pieces[2] + pieces[3]) + (pieces[4] + pieces[5])
                part = [p + e for p, e in zip(part, pieces)]
                part_y = part_y + total * float((kb - 1) * BR + kr)
            if kb == 0 and g == 0:
                fits = lat > 0
            elif kb == 2 and g == bands - 1:
                fits = lat < last
            else:
                fits = None
            if fits is not None:
                part = [jnp.where(fits, p, 0.0) for p in part]
                part_y = jnp.where(fits, part_y, 0.0)
            sums = [s + p for s, p in zip(sums, part)]
            sum_y = sum_y + part_y
        mass = (sums[0] + sums[1]) + (sums[2] + sums[3]) + (sums[4] + sums[5])
        at_four = jnp.where(on_left, -2.0, 4.0)
        at_five = jnp.where(on_left, -1.0, 5.0)
        octs = sums[1] + 2.0 * sums[2] + 3.0 * sums[3] + at_four * sums[4] + at_five * sums[5]
        sum_x = octs * 8.0 + mass * sub
        mass = jnp.sum(mass, axis=0, keepdims=True)
        sum_x = jnp.sum(sum_x, axis=0, keepdims=True)
        sum_y = jnp.sum(sum_y, axis=0, keepdims=True)
        row = (lane // cols)[0:1].astype(F32)
        column = q_col[0:1].astype(F32)
        flow[0:1, g * queries : (g + 1) * queries] = sum_y / mass - row
        flow[1:2, g * queries : (g + 1) * queries] = sum_x / mass - column


def mix_kernel(cells, enc_one, wt, mix):
    feats = enc_one[...].reshape(cells, CH)
    step = 256
    for c0 in range(0, cells, step):
        for k in range(UP):
            wk = jnp.concatenate(
                [wt[n * 64 + k * UP : n * 64 + k * UP + UP] for n in range(9)], axis=0
            )
            logits = lax.dot_general(
                wk, feats[c0 : c0 + step], (((1,), (1,)), ((), ())), preferred_element_type=F32
            )
            expo = jnp.exp(logits).reshape(9, UP, step)
            total = jnp.sum(expo, axis=0)
            mix[:, k, :, c0 : c0 + step] = expo / total[None]


def up_kernel(rows, cols, mix, own, lat_a, lat_b, lon_in, lon_x, out, pad):
    lat_odd = lax.axis_index("lat") % 2 == 1
    lon_odd = lax.axis_index("lon") % 2 == 1
    cells = rows * cols
    width = cells + 2 * cols

    def place(slot, mine, a, b):
        def at(north, south):
            pad[slot, :, 0:cols] = north[:, cells - cols : cells]
            pad[slot, :, cols + cells : width] = south[:, 0:cols]

        pad[slot, :, cols : cols + cells] = mine[...]

        @pl.when(lat_odd)
        def _():
            at(b, a)

        @pl.when(jnp.logical_not(lat_odd))
        def _():
            at(a, b)

    place(0, own, lat_a, lat_b)

    @pl.when(lon_odd)
    def _():
        place(1, lon_in.at[0], lon_in.at[1], lon_in.at[2])
        place(2, lon_x.at[0], lon_x.at[1], lon_x.at[2])

    @pl.when(jnp.logical_not(lon_odd))
    def _():
        place(1, lon_x.at[0], lon_x.at[1], lon_x.at[2])
        place(2, lon_in.at[0], lon_in.at[1], lon_in.at[2])

    total_lanes = pad.shape[2]
    mid, left, right = pad[0] * UP, pad[1] * UP, pad[2] * UP
    column = lax.broadcasted_iota(jnp.int32, mid.shape, 1) % cols
    west = jnp.where(
        column == 0, pltpu.roll(left, total_lanes - (cols - 1), 1), pltpu.roll(mid, 1, 1)
    )
    east = jnp.where(
        column == cols - 1, pltpu.roll(right, cols - 1, 1), pltpu.roll(mid, total_lanes - 1, 1)
    )
    shifted = []
    for a in range(3):
        for field in (west, mid, east):
            moved = field if a == 0 else pltpu.roll(field, total_lanes - a * cols, 1)
            shifted.append(moved[:, 0:cells])
    src = lax.broadcasted_iota(jnp.int32, (UP * cols, UP * cols), 0)
    dst = lax.broadcasted_iota(jnp.int32, (UP * cols, UP * cols), 1)
    order = jnp.where((dst // UP == src % cols) & (dst % UP == src // cols), 1.0, 0.0).astype(BF16)
    tile = 128
    group = tile // cols
    lane = lax.broadcasted_iota(jnp.int32, (UP, tile), 1)
    bits = []
    span = 1
    while span < group:
        bits.append((span, (lane // (span * cols)) % 2 == 1))
        span *= 2
    for d in range(2):
        lanes_of = [[None] * (UP // group) for _ in range(rows)]
        for t in range(cells // tile):
            flows = [
                jnp.broadcast_to(s[d : d + 1, t * tile : (t + 1) * tile], (UP, tile))
                for s in shifted
            ]
            for u in range(UP // group):
                block = []
                for k in range(group):
                    acc = None
                    for n in range(9):
                        term = mix[n, u * group + k, :, t * tile : (t + 1) * tile] * flows[n]
                        acc = term if acc is None else acc + term
                    block.append(acc)
                for span, high in bits:
                    shift = span * cols
                    done = list(block)
                    for k in range(group):
                        if k & span:
                            continue
                        lo_v, hi_v = block[k], block[k | span]
                        done[k] = jnp.where(high, pltpu.roll(hi_v, shift, 1), lo_v)
                        done[k | span] = jnp.where(
                            high, hi_v, pltpu.roll(lo_v, tile - shift, 1)
                        )
                    block = done
                for k in range(group):
                    lanes_of[t * group + k][u] = block[k]
        value = jnp.concatenate([jnp.concatenate(v, axis=1) for v in lanes_of], axis=0)
        high_part = value.astype(BF16)
        low_part = (value - high_part.astype(F32)).astype(BF16)
        out[d] = jnp.dot(high_part, order, preferred_element_type=F32) + jnp.dot(
            low_part, order, preferred_element_type=F32
        )


def body(frame_one, frame_two, enc_weight, mask_weight):
    rows, cols = frame_one.shape[0], frame_one.shape[1]
    cells = rows * cols
    n2, n1 = rows + 2 * BR + 2, rows + 2
    slots = n2 + -(-n2 // BC) + -(-n1 // BC)
    wide = cols + 2 * BC
    lats, lons = lax.axis_size("lat"), lax.axis_size("lon")
    lat_odd = lax.axis_index("lat") % 2 == 1
    far_lat = pair_perm(lats, 1, False)
    near_lat = pair_perm(lats, 0, False)
    far_lon = pair_perm(lons, 1, True)
    near_lon = pair_perm(lons, 0, True)

    def edge_rows(bottom):
        two = lax.dynamic_slice_in_dim(frame_two, jnp.where(bottom, rows - BR - 1, 0), BR + 1, 0)
        one = lax.dynamic_slice_in_dim(frame_one, jnp.where(bottom, rows - 1, 0), 1, 0)
        return jnp.concatenate([two, one], axis=0)

    row_a = lax.ppermute(edge_rows(lat_odd), "lat", far_lat)
    row_b = lax.ppermute(edge_rows(jnp.logical_not(lat_odd)), "lat", near_lat)

    msg = jax.ShapeDtypeStruct((slots, BC, CH), BF16)
    m_in, m_x = pl.pallas_call(
        functools.partial(pack_kernel, rows, cols),
        out_shape=(msg, msg),
        in_specs=[VMEM] * 4,
        out_specs=(VMEM, VMEM),
        scratch_shapes=[
            pltpu.VMEM((n2 + n1, cols, CH), BF16),
            pltpu.VMEM((-(-n2 // BC) * BC, CH), F32),
        ],
        compiler_params=params(16),
        name="pack",
    )(frame_one, frame_two, row_a, row_b)
    col_x = lax.ppermute(m_x, "lon", far_lon)
    col_in = lax.ppermute(m_in, "lon", near_lon)

    flow, enc_one = pl.pallas_call(
        functools.partial(flow_kernel, rows, cols),
        out_shape=(
            jax.ShapeDtypeStruct((2, cells), F32),
            jax.ShapeDtypeStruct((rows, cols, CH), BF16),
        ),
        in_specs=[VMEM] * 7,
        out_specs=(VMEM, VMEM),
        scratch_shapes=[
            pltpu.VMEM((n2, wide + 2 * BR, CH), F32),
            pltpu.VMEM((n1, cols + 2 * BR, CH), F32),
            pltpu.VMEM((3, n2, wide, CH), BF16),
            pltpu.VMEM((3, n1, cols, CH), BF16),
            pltpu.VMEM((rows + 2 * BR, wide, CH), BF16),
        ],
        compiler_params=params(32),
        name="flow",
    )(frame_one, frame_two, row_a, row_b, col_in, col_x, enc_weight.reshape(9 * CH, CH))

    flow_a = lax.ppermute(flow, "lat", far_lat)
    flow_b = lax.ppermute(flow, "lat", near_lat)

    wt = mask_weight.reshape(CH, 9, UP, UP).transpose(1, 3, 2, 0).reshape(9 * UP * UP, CH)
    mix = pl.pallas_call(
        functools.partial(mix_kernel, cells),
        out_shape=jax.ShapeDtypeStruct((9, UP, UP, cells), F32),
        in_specs=[VMEM] * 2,
        out_specs=VMEM,
        compiler_params=params(16),
        cost_estimate=pl.CostEstimate(
            flops=2 * 576 * CH * cells, bytes_accessed=4 * 576 * cells, transcendentals=576 * cells
        ),
        name="mix",
    )(enc_one, wt)

    trio = jnp.stack([flow, flow_a, flow_b])
    lon_x = lax.ppermute(trio, "lon", far_lon)
    lon_in = lax.ppermute(trio, "lon", near_lon)
    lanes = -(-(cells + 2 * cols) // 128) * 128
    return pl.pallas_call(
        functools.partial(up_kernel, rows, cols),
        out_shape=jax.ShapeDtypeStruct((2, rows * UP, cols * UP), F32),
        in_specs=[VMEM] * 6,
        out_specs=VMEM,
        scratch_shapes=[pltpu.VMEM((3, 2, lanes), F32)],
        compiler_params=params(16),
        name="upsample",
    )(mix, flow, flow_a, flow_b, lon_in, lon_x)


def solution(mesh):
    in_specs = (P("lat", "lon", None), P("lat", "lon", None), P(), P())
    return jax.shard_map(
        body, mesh=mesh, in_specs=in_specs, out_specs=P(None, "lat", "lon"), check_vma=False
    )
```

profile of v0, /device:TPU:6, one launch (start us, length us, event | category | flops | bytes accessed | tf_op | source)
XLA Modules:
  0.0 69.4 jit_solution(4995485422669093214)
XLA Ops:
  0.0 0.0 copy-start.1
  0.0 0.0 copy-start
  0.0 0.0 copy-start.2
  0.0 0.9 %constant_dynamic-slice_fusion = (bf16[1,32,256]{2,1,0:T(8,128)(2,1)S(1)}, bf16[1,32,256]{2,1,0:T(8,128)(2,1)S(1)}) fusion(bf16[16,32,256]{2,1,0:T(8,128)(2,1)} %f1.3, s32[]{:T(128)S(6)} %select_n.28, s32[]{:T(128)S(6)} %select_n.26), kind=kLoop, calls=%fused_computation.3 | loop fusion | bytes 65544 | tf_op jit(solution)/shard_map/dynamic_slice | solution.py:339
  0.9 1.0 %constant_dynamic-slice_fusion.1 = (bf16[9,32,256]{2,1,0:T(8,128)(2,1)S(1)}, bf16[9,32,256]{2,1,0:T(8,128)(2,1)S(1)}) fusion(bf16[16,32,256]{2,1,0:T(8,128)(2,1)} %f2.3, s32[]{:T(128)S(6)} %select_n.27, s32[]{:T(128)S(6)} %select_n.25), kind=kLoop, calls=%fused_computation.4 | loop fusion | bytes 589832 | tf_op jit(solution)/shard_map/dynamic_slice | solution.py:338
  1.9 8.2 %collective-permute-start = (bf16[10,32,256]{2,1,0:T(8,128)(2,1)S(1)}, bf16[10,32,256]{2,1,0:T(8,128)(2,1)S(1)}, u32[]{:S(2)}, u32[]{:S(2)}) collective-permute-start(bf16[10,32,256]{2,1,0:T(8,128)(2,1)S(1)} %pad_maximum_fusion), channel_id=1, source_target_pairs={{32,64},{64,32},{96,128},{128,96},{160,192},{192,160},{224,256},{2... | collective-permute-start | bytes 491528 | tf_op jit(solution)/shard_map/ppermute | solution.py:342
  10.1 1.9 %collective-permute-start.1 = (bf16[10,32,256]{2,1,0:T(8,128)(2,1)S(1)}, bf16[10,32,256]{2,1,0:T(8,128)(2,1)S(1)}, u32[]{:S(2)}, u32[]{:S(2)}) collective-permute-start(bf16[10,32,256]{2,1,0:T(8,128)(2,1)S(1)} %pad_maximum_fusion.1), channel_id=1, source_target_pairs={{0,32},{32,0},{64,96},{96,64},{128,160},{160,128},{192,224},{224,1... | collective-permute-start | bytes 491528 | tf_op jit(solution)/shard_map/ppermute | solution.py:343
  12.1 3.1 %collective-permute-done.ra = bf16[10,32,256]{2,1,0:T(8,128)(2,1)S(1)} collective-permute-done((bf16[10,32,256]{2,1,0:T(8,128)(2,1)S(1)}, bf16[10,32,256]{2,1,0:T(8,128)(2,1)S(1)}, u32[]{:S(2)}, u32[]{:S(2)}) %collective-permute-start) | collective-permute-done | bytes 163872 | tf_op jit(solution)/shard_map/ppermute | solution.py:342
  15.2 2.5 %collective-permute-done.1.rb = bf16[10,32,256]{2,1,0:T(8,128)(2,1)S(1)} collective-permute-done((bf16[10,32,256]{2,1,0:T(8,128)(2,1)S(1)}, bf16[10,32,256]{2,1,0:T(8,128)(2,1)S(1)}, u32[]{:S(2)}, u32[]{:S(2)}) %collective-permute-start.1) | collective-permute-done | bytes 163872 | tf_op jit(solution)/shard_map/ppermute | solution.py:343
  17.7 0.0 copy-done.1
  17.7 0.0 copy-done
  17.7 0.2 pack.1
  17.8 1.9 %collective-permute-start.2 = (bf16[39,16,256]{2,1,0:T(8,128)(2,1)S(1)}, bf16[39,16,256]{2,1,0:T(8,128)(2,1)S(1)}, u32[]{:S(2)}, u32[]{:S(2)}) collective-permute-start(bf16[39,16,256]{2,1,0:T(8,128)(2,1)S(1)} %get-tuple-element.9), channel_id=1, source_target_pairs={{0,1},{1,0},{2,3},{3,2},{4,5},{5,4},{6,7},{7,6},{8,9},{9,8},{10,11... | collective-permute-start | bytes 958472 | tf_op jit(solution)/shard_map/ppermute | solution.py:359
  19.8 11.2 %collective-permute-start.3 = (bf16[39,16,256]{2,1,0:T(8,128)(2,1)S(1)}, bf16[39,16,256]{2,1,0:T(8,128)(2,1)S(1)}, u32[]{:S(2)}, u32[]{:S(2)}) collective-permute-start(bf16[39,16,256]{2,1,0:T(8,128)(2,1)S(1)} %get-tuple-element.10), channel_id=1, source_target_pairs={{1,2},{2,1},{3,4},{4,3},{5,6},{6,5},{7,8},{8,7},{9,10},{10,9},{11,... | collective-permute-start | bytes 958472 | tf_op jit(solution)/shard_map/ppermute | solution.py:358
  31.0 0.0 collective-permute-done.2.c_in
  31.0 6.7 %collective-permute-done.3.c_x = bf16[39,16,256]{2,1,0:T(8,128)(2,1)S(1)} collective-permute-done((bf16[39,16,256]{2,1,0:T(8,128)(2,1)S(1)}, bf16[39,16,256]{2,1,0:T(8,128)(2,1)S(1)}, u32[]{:S(2)}, u32[]{:S(2)}) %collective-permute-start.3) | collective-permute-done | bytes 319520 | tf_op jit(solution)/shard_map/ppermute | solution.py:358
  37.7 0.0 copy-done.2
  37.7 0.0 copy-start.3
  37.7 5.3 %flow.1 = (f32[2,512]{1,0:T(2,128)S(1)}, bf16[16,32,256]{2,1,0:T(8,128)(2,1)S(1)}) custom-call(bf16[16,32,256]{2,1,0:T(8,128)(2,1)S(1)} %copy-done.1, bf16[16,32,256]{2,1,0:T(8,128)(2,1)S(1)} %copy-done, bf16[10,32,256]{2,1,0:T(8,128)(2,1)S(1)} %collective-permute-done.ra, bf16[10,32,256]{2,1,0:T(8,128)(2,1)S(1)} %collective-permute-done.1.rb, ...), custom_call_target="tpu_custom_call" | custom-call | tf_op jit(solution)/shard_map/flow/pallas_call | solution.py:361
  43.1 6.2 %collective-permute-start.4 = (f32[2,512]{1,0:T(2,128)S(1)}, f32[2,512]{1,0:T(2,128)S(1)}, u32[]{:S(2)}, u32[]{:S(2)}) collective-permute-start(f32[2,512]{1,0:T(2,128)S(1)} %get-tuple-element.12.own), channel_id=1, source_target_pairs={{32,64},{64,32},{96,128},{128,96},{160,192},{192,160},{224,256},{2... | collective-permute-start | bytes 12296 | tf_op jit(solution)/shard_map/ppermute | solution.py:380
  49.2 1.9 %collective-permute-start.5 = (f32[2,512]{1,0:T(2,128)S(1)}, f32[2,512]{1,0:T(2,128)S(1)}, u32[]{:S(2)}, u32[]{:S(2)}) collective-permute-start(f32[2,512]{1,0:T(2,128)S(1)} %get-tuple-element.12.own), channel_id=1, source_target_pairs={{0,32},{32,0},{64,96},{96,64},{128,160},{160,128},{192,224},{224,1... | collective-permute-start | bytes 12296 | tf_op jit(solution)/shard_map/ppermute | solution.py:381
  51.2 0.0 copy-done.3
  51.2 0.1 copy.5
  51.2 0.0 collective-permute-done.4.lat_a
  51.3 3.5 %collective-permute-done.5.lat_b = f32[2,512]{1,0:T(2,128)S(1)} collective-permute-done((f32[2,512]{1,0:T(2,128)S(1)}, f32[2,512]{1,0:T(2,128)S(1)}, u32[]{:S(2)}, u32[]{:S(2)}) %collective-permute-start.5) | collective-permute-done | bytes 4128 | tf_op jit(solution)/shard_map/ppermute | solution.py:381
  54.7 1.9 %collective-permute-start.6 = (f32[3,2,512]{2,1,0:T(2,128)S(1)}, f32[3,2,512]{2,1,0:T(2,128)S(1)}, u32[]{:S(2)}, u32[]{:S(2)}) collective-permute-start(f32[3,2,512]{2,1,0:T(2,128)S(1)} %pad_maximum_fusion.2), channel_id=1, source_target_pairs={{0,1},{1,0},{2,3},{3,2},{4,5},{5,4},{6,7},{7,6},{8,9},{9,8},{10,11... | collective-permute-start | bytes 36872 | tf_op jit(solution)/shard_map/ppermute | solution.py:398
  56.7 7.9 %collective-permute-start.7 = (f32[3,2,512]{2,1,0:T(2,128)S(1)}, f32[3,2,512]{2,1,0:T(2,128)S(1)}, u32[]{:S(2)}, u32[]{:S(2)}) collective-permute-start(f32[3,2,512]{2,1,0:T(2,128)S(1)} %pad_maximum_fusion.2), channel_id=1, source_target_pairs={{1,2},{2,1},{3,4},{4,3},{5,6},{6,5},{7,8},{8,7},{9,10},{10,9},{11,... | collective-permute-start | bytes 36872 | tf_op jit(solution)/shard_map/ppermute | solution.py:397
  64.6 0.8 %mix.1 = f32[9,8,8,512]{3,2,1,0:T(8,128)S(1)} custom-call(bf16[16,32,256]{2,1,0:T(8,128)(2,1)S(1)} %get-tuple-element.11.enc_one, bf16[576,256]{1,0:T(8,128)(2,1)S(1)} %bitcast.8), custom_call_target="tpu_custom_call" | custom-call | flops 150994944 | bytes 1179648 | tf_op jit(solution)/shard_map/mix/pallas_call | solution.py:384
  65.4 0.0 collective-permute-done.6.lon_in
  65.4 2.3 %collective-permute-done.7.lon_x = f32[3,2,512]{2,1,0:T(2,128)S(1)} collective-permute-done((f32[3,2,512]{2,1,0:T(2,128)S(1)}, f32[3,2,512]{2,1,0:T(2,128)S(1)}, u32[]{:S(2)}, u32[]{:S(2)}) %collective-permute-start.7) | collective-permute-done | bytes 12320 | tf_op jit(solution)/shard_map/ppermute | solution.py:397
  67.7 1.7 %upsample.1 = f32[2,128,256]{2,1,0:T(8,128)} custom-call(f32[9,8,8,512]{3,2,1,0:T(8,128)S(1)} %mix.1, f32[2,512]{1,0:T(2,128)S(1)} %get-tuple-element.12.own, f32[2,512]{1,0:T(2,128)S(1)} %collective-permute-done.4.lat_a, f32[2,512]{1,0:T(2,128)S(1)} %collective-permute-done.5.lat_b, f32[3,2,512]{2,1,0:T(2,128)S(1)} %collective-permute-done.6.lon_in, ...), custom_call_target="tpu_custom_call" | custom-call | tf_op jit(solution)/shard_map/upsample/pallas_call | solution.py:400
  (3 shorter events, 0.0 us)
Async XLA Ops:
  0.0 17.7 %copy-start.1 = (bf16[16,32,256]{2,1,0:T(8,128)(2,1)S(1)}, bf16[16,32,256]{2,1,0:T(8,128)(2,1)}, u32[]{:S(2)}) copy-start(bf16[16,32,256]{2,1,0:T(8,128)(2,1)} %f1.3) | copy-start | bytes 786436
  0.0 17.7 %copy-start = (bf16[16,32,256]{2,1,0:T(8,128)(2,1)S(1)}, bf16[16,32,256]{2,1,0:T(8,128)(2,1)}, u32[]{:S(2)}) copy-start(bf16[16,32,256]{2,1,0:T(8,128)(2,1)} %f2.3) | copy-start | bytes 786436
  0.0 37.7 %copy-start.2 = (bf16[3,3,256,256]{3,2,1,0:T(8,128)(2,1)S(1)}, bf16[3,3,256,256]{3,2,1,0:T(8,128)(2,1)}, u32[]{:S(2)}) copy-start(bf16[3,3,256,256]{3,2,1,0:T(8,128)(2,1)} %param.6) | copy-start | bytes 3538948
  1.9 13.2 %collective-permute-start = (bf16[10,32,256]{2,1,0:T(8,128)(2,1)S(1)}, bf16[10,32,256]{2,1,0:T(8,128)(2,1)S(1)}, u32[]{:S(2)}, u32[]{:S(2)}) collective-permute-start(bf16[10,32,256]{2,1,0:T(8,128)(2,1)S(1)} %pad_maximum_fusion), channel_id=1, source_target_pairs={{32,64},{64,32},{96,128},{128,96},{160,192},{192,160},{224,256},{2... | collective-permute-start | bytes 491528 | tf_op jit(solution)/shard_map/ppermute | solution.py:342
  10.1 7.6 %collective-permute-start.1 = (bf16[10,32,256]{2,1,0:T(8,128)(2,1)S(1)}, bf16[10,32,256]{2,1,0:T(8,128)(2,1)S(1)}, u32[]{:S(2)}, u32[]{:S(2)}) collective-permute-start(bf16[10,32,256]{2,1,0:T(8,128)(2,1)S(1)} %pad_maximum_fusion.1), channel_id=1, source_target_pairs={{0,32},{32,0},{64,96},{96,64},{128,160},{160,128},{192,224},{224,1... | collective-permute-start | bytes 491528 | tf_op jit(solution)/shard_map/ppermute | solution.py:343
  17.8 13.2 %collective-permute-start.2 = (bf16[39,16,256]{2,1,0:T(8,128)(2,1)S(1)}, bf16[39,16,256]{2,1,0:T(8,128)(2,1)S(1)}, u32[]{:S(2)}, u32[]{:S(2)}) collective-permute-start(bf16[39,16,256]{2,1,0:T(8,128)(2,1)S(1)} %get-tuple-element.9), channel_id=1, source_target_pairs={{0,1},{1,0},{2,3},{3,2},{4,5},{5,4},{6,7},{7,6},{8,9},{9,8},{10,11... | collective-permute-start | bytes 958472 | tf_op jit(solution)/shard_map/ppermute | solution.py:359
  19.8 18.0 %collective-permute-start.3 = (bf16[39,16,256]{2,1,0:T(8,128)(2,1)S(1)}, bf16[39,16,256]{2,1,0:T(8,128)(2,1)S(1)}, u32[]{:S(2)}, u32[]{:S(2)}) collective-permute-start(bf16[39,16,256]{2,1,0:T(8,128)(2,1)S(1)} %get-tuple-element.10), channel_id=1, source_target_pairs={{1,2},{2,1},{3,4},{4,3},{5,6},{6,5},{7,8},{8,7},{9,10},{10,9},{11,... | collective-permute-start | bytes 958472 | tf_op jit(solution)/shard_map/ppermute | solution.py:358
  37.7 13.4 %copy-start.3 = (bf16[256,576]{0,1:T(8,128)(2,1)S(1)}, bf16[256,576]{0,1:T(8,128)(2,1)}, u32[]{:S(2)}) copy-start(bf16[256,576]{0,1:T(8,128)(2,1)} %param.7) | copy-start | bytes 884740
  43.1 8.2 %collective-permute-start.4 = (f32[2,512]{1,0:T(2,128)S(1)}, f32[2,512]{1,0:T(2,128)S(1)}, u32[]{:S(2)}, u32[]{:S(2)}) collective-permute-start(f32[2,512]{1,0:T(2,128)S(1)} %get-tuple-element.12.own), channel_id=1, source_target_pairs={{32,64},{64,32},{96,128},{128,96},{160,192},{192,160},{224,256},{2... | collective-permute-start | bytes 12296 | tf_op jit(solution)/shard_map/ppermute | solution.py:380
  49.2 5.5 %collective-permute-start.5 = (f32[2,512]{1,0:T(2,128)S(1)}, f32[2,512]{1,0:T(2,128)S(1)}, u32[]{:S(2)}, u32[]{:S(2)}) collective-permute-start(f32[2,512]{1,0:T(2,128)S(1)} %get-tuple-element.12.own), channel_id=1, source_target_pairs={{0,32},{32,0},{64,96},{96,64},{128,160},{160,128},{192,224},{224,1... | collective-permute-start | bytes 12296 | tf_op jit(solution)/shard_map/ppermute | solution.py:381
  54.7 10.7 %collective-permute-start.6 = (f32[3,2,512]{2,1,0:T(2,128)S(1)}, f32[3,2,512]{2,1,0:T(2,128)S(1)}, u32[]{:S(2)}, u32[]{:S(2)}) collective-permute-start(f32[3,2,512]{2,1,0:T(2,128)S(1)} %pad_maximum_fusion.2), channel_id=1, source_target_pairs={{0,1},{1,0},{2,3},{3,2},{4,5},{5,4},{6,7},{7,6},{8,9},{9,8},{10,11... | collective-permute-start | bytes 36872 | tf_op jit(solution)/shard_map/ppermute | solution.py:398
  56.7 11.0 %collective-permute-start.7 = (f32[3,2,512]{2,1,0:T(2,128)S(1)}, f32[3,2,512]{2,1,0:T(2,128)S(1)}, u32[]{:S(2)}, u32[]{:S(2)}) collective-permute-start(f32[3,2,512]{2,1,0:T(2,128)S(1)} %pad_maximum_fusion.2), channel_id=1, source_target_pairs={{1,2},{2,1},{3,4},{4,3},{5,6},{6,5},{7,8},{8,7},{9,10},{10,9},{11,... | collective-permute-start | bytes 36872 | tf_op jit(solution)/shard_map/ppermute | solution.py:397
where the time goes:
time: 69.8 us; the launch traced here: 69.4 us
  starting transfers between devices  41.2 us (59%)
  waiting for transfers between devices  18.1 us (26%)
  Pallas kernels  8.01 us (11%)
  local copies, waits for them, and re-layouts  1.94 us (3%)
    ppermute x1, starting transfers between devices, body(): col_x = lax.ppermute(m_x, 'lon', far_lon)  11.2 us
    ppermute x1, starting transfers between devices, body(): row_a = lax.ppermute(edge_rows(lat_odd), 'lat', far_lat)  8.16 us
    ppermute x1, starting transfers between devices, body(): lon_x = lax.ppermute(trio, 'lon', far_lon)  7.92 us
    ppermute x1, waiting for transfers between devices, body(): col_x = lax.ppermute(m_x, 'lon', far_lon)  6.71 us
    ppermute x1, starting transfers between devices, body(): flow_a = lax.ppermute(flow, 'lat', far_lat)  6.16 us
    pallas_call x1, Pallas kernels, body(): pl.pallas_call(functools.partial(flow_kernel, rows, cols), out_shape=(jax...  5.32 us
    ppermute x1, waiting for transfers between devices, body(): flow_b = lax.ppermute(flow, 'lat', near_lat)  3.48 us
    ppermute x1, waiting for transfers between devices, body(): row_a = lax.ppermute(edge_rows(lat_odd), 'lat', far_lat)  3.11 us
  transfers between devices with their start and end apart: 8, of which 5 were waited for; matrix products, arithmetic and copies ran while one was open for 0% of the time, Pallas kernels for 1%

commit v1 on v0

--- a/solution.py
+++ b/solution.py
@@ -33,30 +33,54 @@
     return out
 
 
-def pack_kernel(rows, cols, f1, f2, ra, rb, m_in, m_x, ext, col):
+def edge_kernel(rows, f1, f2, m_a, m_b, sems):
+    odd = lax.axis_index("lat") % 2
+    copies = []
+    for k, (msg, low) in enumerate(((m_a, odd), (m_b, 1 - odd))):
+        copies.append(
+            pltpu.make_async_copy(
+                f2.at[pl.ds(low * (rows - BR - 1), BR + 1)], msg.at[pl.ds(0, BR + 1)], sems.at[2 * k]
+            )
+        )
+        copies.append(
+            pltpu.make_async_copy(
+                f1.at[pl.ds(low * (rows - 1), 1)], msg.at[pl.ds(BR + 1, 1)], sems.at[2 * k + 1]
+            )
+        )
+    for copy in copies:
+        copy.start()
+    for copy in copies:
+        copy.wait()
+
+
+def pack_kernel(rows, cols, f1, f2, ra, rb, m_x, m_in, ends, ext, col):
     lat_odd = lax.axis_index("lat") % 2 == 1
     lon_odd = lax.axis_index("lon") % 2 == 1
-
-    def halo(north, south):
-        ext[0 : BR + 1] = north[0 : BR + 1]
-        ext[BR + 1 : BR + 1 + rows] = f2[...]
-        ext[BR + 1 + rows : 2 * BR + 2 + rows] = south[0 : BR + 1]
-        ext[2 * BR + 2 + rows] = north[BR + 1]
-        ext[2 * BR + 3 + rows : 2 * BR + 3 + 2 * rows] = f1[...]
-        ext[2 * BR + 3 + 2 * rows] = south[BR + 1]
-
-    @pl.when(lat_odd)
-    def _():
-        halo(rb, ra)
-
-    @pl.when(jnp.logical_not(lat_odd))
-    def _():
-        halo(ra, rb)
-
     n2 = rows + 2 * BR + 2
     n1 = rows + 2
     slots2 = -(-n2 // BC)
     slots1 = -(-n1 // BC)
+
+    def halo(north, south):
+        ext[0 : BR + 1] = north[0 : BR + 1]
+        ext[BR + 1 : BR + 1 + rows] = f2[...]
+        ext[BR + 1 + rows : n2] = south[0 : BR + 1]
+        ext[n2] = north[BR + 1]
+        ext[n2 + 1 : n2 + 1 + rows] = f1[...]
+        ext[n2 + 1 + rows] = south[BR + 1]
+
+    @pl.when(lat_odd)
+    def _():
+        halo(rb, ra)
+
+    @pl.when(jnp.logical_not(lat_odd))
+    def _():
+        halo(ra, rb)
+
+    first = ext[0:n2, 0:BC].astype(F32)
+    ends[0, 0:n2] = first[:, 0, :]
+    final = ext[0:n2, cols - BC : cols].astype(F32)
+    ends[1, 0:n2] = final[:, BC - 1, :]
 
     def edge(msg, main, extra, one):
         msg[0:n2] = ext[0:n2, main : main + BC]
@@ -86,78 +110,113 @@
         right(m_in)
 
 
-def flow_kernel(rows, cols, f1, f2, ra, rb, c_in, c_x, w, flow, enc_one, s2, s1, x2, x1, e2):
+def conv(x, w, row, count, width):
+    lhs = jnp.concatenate(
+        [
+            x[b, row + a : row + a + count].reshape(count * width, CH)
+            for a in range(3)
+            for b in range(3)
+        ],
+        axis=1,
+    )
+    return jnp.dot(lhs, w[...], preferred_element_type=F32)
+
+
+def own_kernel(rows, cols, f1, f2, ra, rb, w, e2, e1, ends2, ends1, s2, s1, x2, x1):
+    lat_odd = lax.axis_index("lat") % 2 == 1
+    n2 = rows + 2 * BR + 2
+    n1 = rows + 2
+
+    def put_rows(north, south):
+        s2[0 : BR + 1, BR : BR + cols] = north[0 : BR + 1].astype(F32)
+        s2[BR + 1 + rows :, BR : BR + cols] = south[0 : BR + 1].astype(F32)
+        s1[0, BR : BR + cols] = north[BR + 1].astype(F32)
+        s1[n1 - 1, BR : BR + cols] = south[BR + 1].astype(F32)
+
+    s2[BR + 1 : BR + 1 + rows, BR : BR + cols] = f2[...].astype(F32)
+    s1[1 : 1 + rows, BR : BR + cols] = f1[...].astype(F32)
+
+    @pl.when(lat_odd)
+    def _():
+        put_rows(rb, ra)
+
+    @pl.when(jnp.logical_not(lat_odd))
+    def _():
+        put_rows(ra, rb)
+
+    for s in (s2, s1):
+        s[:, 0:BR] = jnp.zeros((s.shape[0], BR, CH), F32)
+        s[:, BR + cols :] = jnp.zeros((s.shape[0], BR, CH), F32)
+    for b in range(3):
+        x2[b] = s2[:, BR - 1 + b : BR - 1 + b + cols].astype(BF16)
+        x1[b] = s1[:, BR - 1 + b : BR - 1 + b + cols].astype(BF16)
+
+    def run(x, out, ends, total):
+        step = 2 * BR
+        for r in range(0, total, step):
+            acc = conv(x, w, r, step, cols).reshape(step, cols, CH)
+            out[r : r + step] = acc.astype(BF16)
+            ends[0, r : r + step] = acc[:, 0, :]
+            ends[1, r : r + step] = acc[:, cols - 1, :]
+
+    run(x1, e1, ends1, rows)
+    run(x2, e2, ends2, rows + 2 * BR)
+
+
+def flow_kernel(rows, cols, o2, o1, ends2, ends1, edges, c_x, c_in, w, flow, enc_one, ext, xs, e2):
     lat = lax.axis_index("lat")
-    lat_odd = lat % 2 == 1
     lon_odd = lax.axis_index("lon") % 2 == 1
     n2 = rows + 2 * BR + 2
     n1 = rows + 2
     wide = cols + 2 * BC
+    tall = rows + 2 * BR
     slots2 = -(-n2 // BC)
     slots1 = -(-n1 // BC)
-    own = BR + BC
-
-    def put_rows(north, south):
-        s2[0 : BR + 1, own : own + cols] = north[0 : BR + 1].astype(F32)
-        s2[BR + 1 + rows :, own : own + cols] = south[0 : BR + 1].astype(F32)
-        s1[0, BR : BR + cols] = north[BR + 1].astype(F32)
-        s1[n1 - 1, BR : BR + cols] = south[BR + 1].astype(F32)
-
-    def put_cols(left, right):
-        s2[:, BR : BR + BC] = left[0:n2].astype(F32)
-        s2[:, own + cols : own + cols + BC] = right[0:n2].astype(F32)
-        extra = left[n2 : n2 + slots2].astype(F32).reshape(slots2 * BC, CH)
-        s2[:, BR - 1 : BR] = extra[0:n2][:, None, :]
-        extra = right[n2 : n2 + slots2].astype(F32).reshape(slots2 * BC, CH)
-        s2[:, BR + wide : BR + wide + 1] = extra[0:n2][:, None, :]
-        one = left[n2 + slots2 :].astype(F32).reshape(slots1 * BC, CH)
-        s1[:, BR - 1 : BR] = one[0:n1][:, None, :]
-        one = right[n2 + slots2 :].astype(F32).reshape(slots1 * BC, CH)
-        s1[:, BR + cols : BR + cols + 1] = one[0:n1][:, None, :]
-
-    s2[BR + 1 : BR + 1 + rows, own : own + cols] = f2[...].astype(F32)
-    s1[1 : 1 + rows, BR : BR + cols] = f1[...].astype(F32)
-
-    @pl.when(lat_odd)
-    def _():
-        put_rows(rb, ra)
-
-    @pl.when(jnp.logical_not(lat_odd))
-    def _():
-        put_rows(ra, rb)
-
-    @pl.when(lon_odd)
-    def _():
-        put_cols(c_in, c_x)
-
-    @pl.when(jnp.logical_not(lon_odd))
-    def _():
-        put_cols(c_x, c_in)
-
-    for b in range(3):
-        x2[b] = s2[:, BR - 1 + b : BR - 1 + b + wide].astype(BF16)
-        x1[b] = s1[:, BR - 1 + b : BR - 1 + b + cols].astype(BF16)
-
-    def conv(x, row, count, width):
+    place = lax.broadcasted_iota(jnp.int32, (1, BC, CH), 1)
+
+    def beside(side, msg):
+        extra = msg[n2 : n2 + slots2].astype(F32).reshape(slots2 * BC, CH)[0:n2][:, None, :]
+        inner = edges[side, 0:n2][:, None, :]
+        ext[:, BR : BR + BC] = msg[0:n2].astype(F32)
+        ext[:, BR - 1 : BR] = inner if side else extra
+        ext[:, BR + BC : BR + BC + 1] = extra if side else inner
+        for b in range(3):
+            xs[b] = ext[:, BR - 1 + b : BR - 1 + b + BC].astype(BF16)
+        at = BC + cols if side else 0
+        e2[:, at : at + BC] = conv(xs, w, 0, tall, BC).astype(BF16).reshape(tall, BC, CH)
+        near = ext[:, BR : BR + 1] if side else ext[:, BR + BC - 1 : BR + BC]
+        near = near[:, 0, :].astype(BF16)
+        one = msg[n2 + slots2 :].reshape(slots1 * BC, CH)
+        one = one.astype(F32)[0:n1].astype(BF16)
+        taps = jnp.concatenate(
+            [w[(3 * a + 2 * side) * CH : (3 * a + 2 * side + 1) * CH] for a in range(3)], axis=0
+        )
         lhs = jnp.concatenate(
             [
-                x[b, pl.ds(row + a, count)].reshape(count * width, CH)
+                jnp.concatenate([near[a : a + tall], one[a : a + rows]], axis=0)
                 for a in range(3)
-                for b in range(3)
             ],
             axis=1,
         )
-        return jnp.dot(lhs, w[...], preferred_element_type=F32)
-
-    half = BR // 2
-    for g in range(rows // BR):
-        enc_one[g * BR : g * BR + BR] = (
-            conv(x1, g * BR, BR, cols).astype(BF16).reshape(BR, cols, CH)
-        )
-    for g in range((rows + 2 * BR) // half):
-        e2[g * half : g * half + half] = (
-            conv(x2, g * half, half, wide).astype(BF16).reshape(half, wide, CH)
-        )
+        more = jnp.dot(lhs, taps, preferred_element_type=F32)
+        hit = place == (BC - 1 if side else 0)
+        lo = cols - BC if side else 0
+        full = ends2[side] + more[0:tall]
+        slab = jnp.where(hit, full[:, None, :], o2[:, lo : lo + BC].astype(F32))
+        e2[:, BC + lo : 2 * BC + lo] = slab.astype(BF16)
+        full = ends1[side] + more[tall : tall + rows]
+        slab = jnp.where(hit, full[:, None, :], o1[:, lo : lo + BC].astype(F32))
+        enc_one[:, lo : lo + BC] = slab.astype(BF16)
+
+    @pl.when(lon_odd)
+    def _():
+        beside(0, c_in)
+        beside(1, c_x)
+
+    @pl.when(jnp.logical_not(lon_odd))
+    def _():
+        beside(0, c_x)
+        beside(1, c_in)
 
     bands = rows // BR
     queries = BR * cols
@@ -165,37 +224,32 @@
     sub = lax.broadcasted_iota(jnp.int32, (BR, queries), 0).astype(F32)
     q_col = lane % cols
     on_left = q_col < BC
-    lefts = jnp.broadcast_to(on_left[None], (2, BR, queries))
     last = lax.axis_size("lat") - 1
     for g in range(bands):
-        query = (enc_one[g * BR : g * BR + BR].reshape(queries, CH).astype(F32) * (1.0 / math.sqrt(CH))).astype(BF16)
-        sums = [jnp.zeros((BR, queries), F32) for _ in range(6)]
-        sum_y = jnp.zeros((BR, queries), F32)
+        query = enc_one[g * BR : g * BR + BR].reshape(queries, CH).astype(F32)
+        query = (query * (1.0 / math.sqrt(CH))).astype(BF16)
+        sums = None
         for kb in range(3):
-            part = [jnp.zeros((BR, queries), F32) for _ in range(6)]
-            part_y = jnp.zeros((BR, queries), F32)
+            keys = e2[(g + kb) * BR : (g + kb + 1) * BR].reshape(BR * wide, CH)
+            score = lax.dot_general(
+                keys, query, (((1,), (1,)), ((), ())), preferred_element_type=F32
+            ).reshape(BR, wide // BR, BR, queries)
+            part = None
+            part_y = None
             for kr in range(BR):
-                keys = e2[(g + kb) * BR + kr]
-                score = lax.dot_general(
-                    keys, query, (((1,), (1,)), ((), ())), preferred_element_type=F32
-                ).reshape(wide // BR, BR, queries)
-                mid = jnp.exp(score[2:6])
-                rim = jnp.exp(jnp.where(lefts, score[0:2], score[6:8]))
-                pieces = [mid[0], mid[1], mid[2], mid[3], rim[0], rim[1]]
+                line = score[kr]
+                pieces = [jnp.exp(line[2 + i]) for i in range(4)]
+                pieces += [jnp.exp(jnp.where(on_left, line[i], line[6 + i])) for i in range(2)]
                 total = (pieces[0] + pieces[1]) + (pieces[2] + pieces[3]) + (pieces[4] + pieces[5])
-                part = [p + e for p, e in zip(part, pieces)]
-                part_y = part_y + total * float((kb - 1) * BR + kr)
+                scaled = total * float((kb - 1) * BR + kr)
+                part = pieces if part is None else [p + e for p, e in zip(part, pieces)]
+                part_y = scaled if part_y is None else part_y + scaled
+            part = part + [part_y]
             if kb == 0 and g == 0:
-                fits = lat > 0
+                part = [jnp.where(lat > 0, p, 0.0) for p in part]
             elif kb == 2 and g == bands - 1:
-                fits = lat < last
-            else:
-                fits = None
-            if fits is not None:
-                part = [jnp.where(fits, p, 0.0) for p in part]
-                part_y = jnp.where(fits, part_y, 0.0)
-            sums = [s + p for s, p in zip(sums, part)]
-            sum_y = sum_y + part_y
+                part = [jnp.where(lat < last, p, 0.0) for p in part]
+            sums = part if sums is None else [s + p for s, p in zip(sums, part)]
         mass = (sums[0] + sums[1]) + (sums[2] + sums[3]) + (sums[4] + sums[5])
         at_four = jnp.where(on_left, -2.0, 4.0)
         at_five = jnp.where(on_left, -1.0, 5.0)
@@ -203,7 +257,7 @@
         sum_x = octs * 8.0 + mass * sub
         mass = jnp.sum(mass, axis=0, keepdims=True)
         sum_x = jnp.sum(sum_x, axis=0, keepdims=True)
-        sum_y = jnp.sum(sum_y, axis=0, keepdims=True)
+        sum_y = jnp.sum(sums[6], axis=0, keepdims=True)
         row = (lane // cols)[0:1].astype(F32)
         column = q_col[0:1].astype(F32)
         flow[0:1, g * queries : (g + 1) * queries] = sum_y / mass - row
@@ -226,7 +280,7 @@
             mix[:, k, :, c0 : c0 + step] = expo / total[None]
 
 
-def up_kernel(rows, cols, mix, own, lat_a, lat_b, lon_in, lon_x, out, pad):
+def up_kernel(rows, cols, mix, own, lat_a, lat_b, lon_x, lon_in, out, pad):
     lat_odd = lax.axis_index("lat") % 2 == 1
     lon_odd = lax.axis_index("lon") % 2 == 1
     cells = rows * cols
@@ -328,29 +382,34 @@
     slots = n2 + -(-n2 // BC) + -(-n1 // BC)
     wide = cols + 2 * BC
     lats, lons = lax.axis_size("lat"), lax.axis_size("lon")
-    lat_odd = lax.axis_index("lat") % 2 == 1
     far_lat = pair_perm(lats, 1, False)
     near_lat = pair_perm(lats, 0, False)
     far_lon = pair_perm(lons, 1, True)
     near_lon = pair_perm(lons, 0, True)
 
-    def edge_rows(bottom):
-        two = lax.dynamic_slice_in_dim(frame_two, jnp.where(bottom, rows - BR - 1, 0), BR + 1, 0)
-        one = lax.dynamic_slice_in_dim(frame_one, jnp.where(bottom, rows - 1, 0), 1, 0)
-        return jnp.concatenate([two, one], axis=0)
-
-    row_a = lax.ppermute(edge_rows(lat_odd), "lat", far_lat)
-    row_b = lax.ppermute(edge_rows(jnp.logical_not(lat_odd)), "lat", near_lat)
+    edge_rows = jax.ShapeDtypeStruct((BR + 2, cols, CH), BF16)
+    m_a, m_b = pl.pallas_call(
+        functools.partial(edge_kernel, rows),
+        out_shape=(edge_rows, edge_rows),
+        in_specs=[pl.BlockSpec(memory_space=pl.ANY)] * 2,
+        out_specs=(VMEM, VMEM),
+        scratch_shapes=[pltpu.SemaphoreType.DMA((4,))],
+        compiler_params=params(8),
+        name="edge_rows",
+    )(frame_one, frame_two)
+    row_a = lax.ppermute(m_a, "lat", far_lat)
+    row_b = lax.ppermute(m_b, "lat", near_lat)
 
     msg = jax.ShapeDtypeStruct((slots, BC, CH), BF16)
-    m_in, m_x = pl.pallas_call(
+    n2_pad = -(-n2 // BC) * BC
+    m_x, m_in, edges = pl.pallas_call(
         functools.partial(pack_kernel, rows, cols),
-        out_shape=(msg, msg),
+        out_shape=(msg, msg, jax.ShapeDtypeStruct((2, n2_pad, CH), F32)),
         in_specs=[VMEM] * 4,
-        out_specs=(VMEM, VMEM),
+        out_specs=(VMEM,) * 3,
         scratch_shapes=[
             pltpu.VMEM((n2 + n1, cols, CH), BF16),
-            pltpu.VMEM((-(-n2 // BC) * BC, CH), F32),
+            pltpu.VMEM((n2_pad, CH), F32),
         ],
         compiler_params=params(16),
         name="pack",
@@ -358,24 +417,47 @@
     col_x = lax.ppermute(m_x, "lon", far_lon)
     col_in = lax.ppermute(m_in, "lon", near_lon)
 
+    tall = rows + 2 * BR
+    weight = enc_weight.reshape(9 * CH, CH)
+    own_two, own_one, ends_two, ends_one = pl.pallas_call(
+        functools.partial(own_kernel, rows, cols),
+        out_shape=(
+            jax.ShapeDtypeStruct((tall, cols, CH), BF16),
+            jax.ShapeDtypeStruct((rows, cols, CH), BF16),
+            jax.ShapeDtypeStruct((2, tall, CH), F32),
+            jax.ShapeDtypeStruct((2, rows, CH), F32),
+        ),
+        in_specs=[VMEM] * 5,
+        out_specs=(VMEM,) * 4,
+        scratch_shapes=[
+            pltpu.VMEM((n2, cols + 2 * BR, CH), F32),
+            pltpu.VMEM((n1, cols + 2 * BR, CH), F32),
+            pltpu.VMEM((3, n2, cols, CH), BF16),
+            pltpu.VMEM((3, n1, cols, CH), BF16),
+        ],
+        compiler_params=params(20),
+        cost_estimate=pl.CostEstimate(
+            flops=2 * 9 * CH * CH * cols * (tall + rows), bytes_accessed=4 << 20, transcendentals=0
+        ),
+        name="encode_own",
+    )(frame_one, frame_two, row_a, row_b, weight)
+
     flow, enc_one = pl.pallas_call(
         functools.partial(flow_kernel, rows, cols),
         out_shape=(
             jax.ShapeDtypeStruct((2, cells), F32),
             jax.ShapeDtypeStruct((rows, cols, CH), BF16),
         ),
-        in_specs=[VMEM] * 7,
+        in_specs=[VMEM] * 8,
         out_specs=(VMEM, VMEM),
         scratch_shapes=[
-            pltpu.VMEM((n2, wide + 2 * BR, CH), F32),
-            pltpu.VMEM((n1, cols + 2 * BR, CH), F32),
-            pltpu.VMEM((3, n2, wide, CH), BF16),
-            pltpu.VMEM((3, n1, cols, CH), BF16),
-            pltpu.VMEM((rows + 2 * BR, wide, CH), BF16),
+            pltpu.VMEM((n2, BC + 2 * BR, CH), F32),
+            pltpu.VMEM((3, n2, BC, CH), BF16),
+            pltpu.VMEM((tall, wide, CH), BF16),
         ],
-        compiler_params=params(32),
+        compiler_params=params(20),
         name="flow",
-    )(frame_one, frame_two, row_a, row_b, col_in, col_x, enc_weight.reshape(9 * CH, CH))
+    )(own_two, own_one, ends_two, ends_one, edges, col_x, col_in, weight)
 
     flow_a = lax.ppermute(flow, "lat", far_lat)
     flow_b = lax.ppermute(flow, "lat", near_lat)
@@ -405,7 +487,7 @@
         scratch_shapes=[pltpu.VMEM((3, 2, lanes), F32)],
         compiler_params=params(16),
         name="upsample",
-    )(mix, flow, flow_a, flow_b, lon_in, lon_x)
+    )(mix, flow, flow_a, flow_b, lon_x, lon_in)
 
 
 def solution(mesh):

time: 69.8 us -> 64.8 us (0.928)
  the two profiles are of different devices: /device:TPU:6 before, /device:TPU:7 now
where the time goes in v1:
time: 64.8 us; the launch traced here: 64.3 us
  starting transfers between devices  43.3 us (67%)
  Pallas kernels  7.93 us (12%)
  waiting for transfers between devices  7.06 us (11%)
  local copies, waits for them, and re-layouts  5.86 us (9%)
    ppermute x1, starting transfers between devices, body(): lon_in = lax.ppermute(trio, 'lon', near_lon)  9.75 us
    ppermute x1, starting transfers between devices, body(): col_in = lax.ppermute(m_in, 'lon', near_lon)  8.2 us
    ppermute x1, starting transfers between devices, body(): row_a = lax.ppermute(m_a, 'lat', far_lat)  7.88 us
    ppermute x1, starting transfers between devices, body(): flow_a = lax.ppermute(flow, 'lat', far_lat)  6.74 us
    unnamed x16, local copies, waits for them, and re-layouts  5.8 us
    ppermute x1, starting transfers between devices, body(): col_x = lax.ppermute(m_x, 'lon', far_lon)  4.95 us
    ppermute x1, waiting for transfers between devices, body(): row_b = lax.ppermute(m_b, 'lat', near_lat)  2.69 us
    pallas_call x1, Pallas kernels, body(): pl.pallas_call(functools.partial(flow_kernel, rows, cols), out_shape=(jax...  2.58 us
  transfers between devices with their start and end apart: 8, of which 3 were waited for; matrix products, arithmetic and copies ran while one was open for 0% of the time, Pallas kernels for 5%

profile of v1, /device:TPU:7, one launch (start us, length us, event | category | flops | bytes accessed | tf_op | source)
XLA Modules:
  0.0 64.3 jit_solution(2672064017272720881)
XLA Ops:
  0.0 0.0 copy-start
  0.0 0.0 copy-start.1
  0.0 1.0 %copy-done.1 = bf16[16,32,256]{2,1,0:T(8,128)(2,1)S(1)} copy-done((bf16[16,32,256]{2,1,0:T(8,128)(2,1)S(1)}, bf16[16,32,256]{2,1,0:T(8,128)(2,1)}, u32[]{:S(2)}) %copy-start.1) | copy-done | bytes 262168
  1.0 0.0 copy-start.4
  1.1 0.9 %copy-done.4 = bf16[16,32,256]{2,1,0:T(8,128)(2,1)S(1)} copy-done((bf16[16,32,256]{2,1,0:T(8,128)(2,1)S(1)}, bf16[16,32,256]{2,1,0:T(8,128)(2,1)}, u32[]{:S(2)}) %copy-start.4) | copy-done | bytes 262168
  2.0 0.4 edge_rows.1
  2.4 7.9 %collective-permute-start = (bf16[10,32,256]{2,1,0:T(8,128)(2,1)S(1)}, bf16[10,32,256]{2,1,0:T(8,128)(2,1)S(1)}, u32[]{:S(2)}, u32[]{:S(2)}) collective-permute-start(bf16[10,32,256]{2,1,0:T(8,128)(2,1)S(1)} %get-tuple-element.16), channel_id=1, source_target_pairs={{32,64},{64,32},{96,128},{128,96},{160,192},{192,160},{224,256},{2... | collective-permute-start | bytes 491528 | tf_op jit(solution)/shard_map/ppermute | solution.py:400
  10.3 1.9 %collective-permute-start.1 = (bf16[10,32,256]{2,1,0:T(8,128)(2,1)S(1)}, bf16[10,32,256]{2,1,0:T(8,128)(2,1)S(1)}, u32[]{:S(2)}, u32[]{:S(2)}) collective-permute-start(bf16[10,32,256]{2,1,0:T(8,128)(2,1)S(1)} %get-tuple-element.17), channel_id=1, source_target_pairs={{0,32},{32,0},{64,96},{96,64},{128,160},{160,128},{192,224},{224,1... | collective-permute-start | bytes 491528 | tf_op jit(solution)/shard_map/ppermute | solution.py:401
  12.3 2.0 %collective-permute-done.ra = bf16[10,32,256]{2,1,0:T(8,128)(2,1)S(1)} collective-permute-done((bf16[10,32,256]{2,1,0:T(8,128)(2,1)S(1)}, bf16[10,32,256]{2,1,0:T(8,128)(2,1)S(1)}, u32[]{:S(2)}, u32[]{:S(2)}) %collective-permute-start) | collective-permute-done | bytes 163872 | tf_op jit(solution)/shard_map/ppermute | solution.py:400
  14.3 2.7 %collective-permute-done.1.rb = bf16[10,32,256]{2,1,0:T(8,128)(2,1)S(1)} collective-permute-done((bf16[10,32,256]{2,1,0:T(8,128)(2,1)S(1)}, bf16[10,32,256]{2,1,0:T(8,128)(2,1)S(1)}, u32[]{:S(2)}, u32[]{:S(2)}) %collective-permute-start.1) | collective-permute-done | bytes 163872 | tf_op jit(solution)/shard_map/ppermute | solution.py:401
  17.0 0.0 copy-start.2
  17.0 0.9 %copy-done.2 = bf16[16,32,256]{2,1,0:T(8,128)(2,1)S(1)} copy-done((bf16[16,32,256]{2,1,0:T(8,128)(2,1)S(1)}, bf16[16,32,256]{2,1,0:T(8,128)(2,1)}, u32[]{:S(2)}) %copy-start.2) | copy-done | bytes 262168
  17.9 0.0 copy-start.5
  17.9 0.9 %copy-done.5 = bf16[16,32,256]{2,1,0:T(8,128)(2,1)S(1)} copy-done((bf16[16,32,256]{2,1,0:T(8,128)(2,1)S(1)}, bf16[16,32,256]{2,1,0:T(8,128)(2,1)}, u32[]{:S(2)}) %copy-start.5) | copy-done | bytes 262168
  18.9 0.2 pack.1
  19.1 5.0 %collective-permute-start.2 = (bf16[39,16,256]{2,1,0:T(8,128)(2,1)S(1)}, bf16[39,16,256]{2,1,0:T(8,128)(2,1)S(1)}, u32[]{:S(2)}, u32[]{:S(2)}) collective-permute-start(bf16[39,16,256]{2,1,0:T(8,128)(2,1)S(1)} %get-tuple-element.23), channel_id=1, source_target_pairs={{1,2},{2,1},{3,4},{4,3},{5,6},{6,5},{7,8},{8,7},{9,10},{10,9},{11,... | collective-permute-start | bytes 958472 | tf_op jit(solution)/shard_map/ppermute | solution.py:417
  24.0 8.2 %collective-permute-start.3 = (bf16[39,16,256]{2,1,0:T(8,128)(2,1)S(1)}, bf16[39,16,256]{2,1,0:T(8,128)(2,1)S(1)}, u32[]{:S(2)}, u32[]{:S(2)}) collective-permute-start(bf16[39,16,256]{2,1,0:T(8,128)(2,1)S(1)} %get-tuple-element.24), channel_id=1, source_target_pairs={{0,1},{1,0},{2,3},{3,2},{4,5},{5,4},{6,7},{7,6},{8,9},{9,8},{10,11... | collective-permute-start | bytes 958472 | tf_op jit(solution)/shard_map/ppermute | solution.py:418
  32.3 0.0 copy-done
  32.3 0.0 copy-start.3
  32.3 0.9 %copy-done.3 = bf16[16,32,256]{2,1,0:T(8,128)(2,1)S(1)} copy-done((bf16[16,32,256]{2,1,0:T(8,128)(2,1)S(1)}, bf16[16,32,256]{2,1,0:T(8,128)(2,1)}, u32[]{:S(2)}) %copy-start.3) | copy-done | bytes 262168
  33.2 0.0 copy-start.6
  33.2 0.9 %copy-done.6 = bf16[16,32,256]{2,1,0:T(8,128)(2,1)S(1)} copy-done((bf16[16,32,256]{2,1,0:T(8,128)(2,1)S(1)}, bf16[16,32,256]{2,1,0:T(8,128)(2,1)}, u32[]{:S(2)}) %copy-start.6) | copy-done | bytes 262168
  34.2 2.2 %encode_own.1 = (bf16[32,32,256]{2,1,0:T(8,128)(2,1)S(1)}, bf16[16,32,256]{2,1,0:T(8,128)(2,1)S(1)}, f32[2,32,256]{2,1,0:T(8,128)S(1)}, f32[2,16,256]{2,1,0:T(8,128)S(1)}) custom-call(bf16[16,32,256]{2,1,0:T(8,128)(2,1)S(1)} %copy-done.3, bf16[16,32,256]{2,1,0:T(8,128)(2,1)S(1)} %copy-done.6, bf16[10,32,256]{2,1,0:T(8,128)(2,1)S(1)} %collective-permute-done.ra, ...), custom_call_target="tpu_custom_call" | custom-call | flops 1811939328 | bytes 4194304 | tf_op jit(solution)/shard_map/encode_own/pallas_call | solution.py:422
  36.3 0.0 collective-permute-done.2.c_x
  36.4 0.0 collective-permute-done.3.c_in
  36.4 0.0 copy-start.7
  36.4 2.6 %flow.1 = (f32[2,512]{1,0:T(2,128)S(1)}, bf16[16,32,256]{2,1,0:T(8,128)(2,1)S(1)}) custom-call(bf16[32,32,256]{2,1,0:T(8,128)(2,1)S(1)} %get-tuple-element.18.o2, bf16[16,32,256]{2,1,0:T(8,128)(2,1)S(1)} %get-tuple-element.19.o1, f32[2,32,256]{2,1,0:T(8,128)S(1)} %get-tuple-element.20.ends2, f32[2,16,256]{2,1,0:T(8,128)S(1)} %get-tuple-element.21.ends1, ...), custom_call_target="tpu_custom_call" | custom-call | tf_op jit(solution)/shard_map/flow/pallas_call | solution.py:445
  39.0 6.7 %collective-permute-start.4 = (f32[2,512]{1,0:T(2,128)S(1)}, f32[2,512]{1,0:T(2,128)S(1)}, u32[]{:S(2)}, u32[]{:S(2)}) collective-permute-start(f32[2,512]{1,0:T(2,128)S(1)} %get-tuple-element.26.own), channel_id=1, source_target_pairs={{32,64},{64,32},{96,128},{128,96},{160,192},{192,160},{224,256},{2... | collective-permute-start | bytes 12296 | tf_op jit(solution)/shard_map/ppermute | solution.py:462
  45.7 1.9 %collective-permute-start.5 = (f32[2,512]{1,0:T(2,128)S(1)}, f32[2,512]{1,0:T(2,128)S(1)}, u32[]{:S(2)}, u32[]{:S(2)}) collective-permute-start(f32[2,512]{1,0:T(2,128)S(1)} %get-tuple-element.26.own), channel_id=1, source_target_pairs={{0,32},{32,0},{64,96},{96,64},{128,160},{160,128},{192,224},{224,1... | collective-permute-start | bytes 12296 | tf_op jit(solution)/shard_map/ppermute | solution.py:463
  47.6 0.0 copy-done.7
  47.7 0.1 copy.5
  47.7 0.0 collective-permute-done.4.lat_a
  47.7 2.3 %collective-permute-done.5.lat_b = f32[2,512]{1,0:T(2,128)S(1)} collective-permute-done((f32[2,512]{1,0:T(2,128)S(1)}, f32[2,512]{1,0:T(2,128)S(1)}, u32[]{:S(2)}, u32[]{:S(2)}) %collective-permute-start.5) | collective-permute-done | bytes 4128 | tf_op jit(solution)/shard_map/ppermute | solution.py:463
  50.1 1.9 %collective-permute-start.6 = (f32[3,2,512]{2,1,0:T(2,128)S(1)}, f32[3,2,512]{2,1,0:T(2,128)S(1)}, u32[]{:S(2)}, u32[]{:S(2)}) collective-permute-start(f32[3,2,512]{2,1,0:T(2,128)S(1)} %pad_maximum_fusion), channel_id=1, source_target_pairs={{1,2},{2,1},{3,4},{4,3},{5,6},{6,5},{7,8},{8,7},{9,10},{10,9},{11,... | collective-permute-start | bytes 36872 | tf_op jit(solution)/shard_map/ppermute | solution.py:479
  52.0 9.7 %collective-permute-start.7 = (f32[3,2,512]{2,1,0:T(2,128)S(1)}, f32[3,2,512]{2,1,0:T(2,128)S(1)}, u32[]{:S(2)}, u32[]{:S(2)}) collective-permute-start(f32[3,2,512]{2,1,0:T(2,128)S(1)} %pad_maximum_fusion), channel_id=1, source_target_pairs={{0,1},{1,0},{2,3},{3,2},{4,5},{5,4},{6,7},{7,6},{8,9},{9,8},{10,11... | collective-permute-start | bytes 36872 | tf_op jit(solution)/shard_map/ppermute | solution.py:480
  61.8 0.8 %mix.1 = f32[9,8,8,512]{3,2,1,0:T(8,128)S(1)} custom-call(bf16[16,32,256]{2,1,0:T(8,128)(2,1)S(1)} %get-tuple-element.25.enc_one, bf16[576,256]{1,0:T(8,128)(2,1)S(1)} %bitcast.8), custom_call_target="tpu_custom_call" | custom-call | flops 150994944 | bytes 1179648 | tf_op jit(solution)/shard_map/mix/pallas_call | solution.py:466
  62.6 0.0 collective-permute-done.6.lon_x
  62.6 0.0 collective-permute-done.7.lon_in
  62.6 1.7 %upsample.1 = f32[2,128,256]{2,1,0:T(8,128)} custom-call(f32[9,8,8,512]{3,2,1,0:T(8,128)S(1)} %mix.1, f32[2,512]{1,0:T(2,128)S(1)} %get-tuple-element.26.own, f32[2,512]{1,0:T(2,128)S(1)} %collective-permute-done.4.lat_a, f32[2,512]{1,0:T(2,128)S(1)} %collective-permute-done.5.lat_b, f32[3,2,512]{2,1,0:T(2,128)S(1)} %collective-permute-done.6.lon_x, ...), custom_call_target="tpu_custom_call" | custom-call | tf_op jit(solution)/shard_map/upsample/pallas_call | solution.py:482
  (1 shorter events, 0.0 us)
Async XLA Ops:
  0.0 32.3 %copy-start = (bf16[3,3,256,256]{3,2,1,0:T(8,128)(2,1)S(1)}, bf16[3,3,256,256]{3,2,1,0:T(8,128)(2,1)}, u32[]{:S(2)}) copy-start(bf16[3,3,256,256]{3,2,1,0:T(8,128)(2,1)} %param.6) | copy-start | bytes 3538948
  0.0 1.0 %copy-start.1 = (bf16[16,32,256]{2,1,0:T(8,128)(2,1)S(1)}, bf16[16,32,256]{2,1,0:T(8,128)(2,1)}, u32[]{:S(2)}) copy-start(bf16[16,32,256]{2,1,0:T(8,128)(2,1)} %f1.5) | copy-start | bytes 786436
  1.0 0.9 %copy-start.4 = (bf16[16,32,256]{2,1,0:T(8,128)(2,1)S(1)}, bf16[16,32,256]{2,1,0:T(8,128)(2,1)}, u32[]{:S(2)}) copy-start(bf16[16,32,256]{2,1,0:T(8,128)(2,1)} %f2.5) | copy-start | bytes 786436
  2.4 11.8 %collective-permute-start = (bf16[10,32,256]{2,1,0:T(8,128)(2,1)S(1)}, bf16[10,32,256]{2,1,0:T(8,128)(2,1)S(1)}, u32[]{:S(2)}, u32[]{:S(2)}) collective-permute-start(bf16[10,32,256]{2,1,0:T(8,128)(2,1)S(1)} %get-tuple-element.16), channel_id=1, source_target_pairs={{32,64},{64,32},{96,128},{128,96},{160,192},{192,160},{224,256},{2... | collective-permute-start | bytes 491528 | tf_op jit(solution)/shard_map/ppermute | solution.py:400
  10.3 6.6 %collective-permute-start.1 = (bf16[10,32,256]{2,1,0:T(8,128)(2,1)S(1)}, bf16[10,32,256]{2,1,0:T(8,128)(2,1)S(1)}, u32[]{:S(2)}, u32[]{:S(2)}) collective-permute-start(bf16[10,32,256]{2,1,0:T(8,128)(2,1)S(1)} %get-tuple-element.17), channel_id=1, source_target_pairs={{0,32},{32,0},{64,96},{96,64},{128,160},{160,128},{192,224},{224,1... | collective-permute-start | bytes 491528 | tf_op jit(solution)/shard_map/ppermute | solution.py:401
  17.0 1.0 %copy-start.2 = (bf16[16,32,256]{2,1,0:T(8,128)(2,1)S(1)}, bf16[16,32,256]{2,1,0:T(8,128)(2,1)}, u32[]{:S(2)}) copy-start(bf16[16,32,256]{2,1,0:T(8,128)(2,1)} %f1.5) | copy-start | bytes 786436
  17.9 0.9 %copy-start.5 = (bf16[16,32,256]{2,1,0:T(8,128)(2,1)S(1)}, bf16[16,32,256]{2,1,0:T(8,128)(2,1)}, u32[]{:S(2)}) copy-start(bf16[16,32,256]{2,1,0:T(8,128)(2,1)} %f2.5) | copy-start | bytes 786436
  19.1 17.3 %collective-permute-start.2 = (bf16[39,16,256]{2,1,0:T(8,128)(2,1)S(1)}, bf16[39,16,256]{2,1,0:T(8,128)(2,1)S(1)}, u32[]{:S(2)}, u32[]{:S(2)}) collective-permute-start(bf16[39,16,256]{2,1,0:T(8,128)(2,1)S(1)} %get-tuple-element.23), channel_id=1, source_target_pairs={{1,2},{2,1},{3,4},{4,3},{5,6},{6,5},{7,8},{8,7},{9,10},{10,9},{11,... | collective-permute-start | bytes 958472 | tf_op jit(solution)/shard_map/ppermute | solution.py:417
  24.0 12.3 %collective-permute-start.3 = (bf16[39,16,256]{2,1,0:T(8,128)(2,1)S(1)}, bf16[39,16,256]{2,1,0:T(8,128)(2,1)S(1)}, u32[]{:S(2)}, u32[]{:S(2)}) collective-permute-start(bf16[39,16,256]{2,1,0:T(8,128)(2,1)S(1)} %get-tuple-element.24), channel_id=1, source_target_pairs={{0,1},{1,0},{2,3},{3,2},{4,5},{5,4},{6,7},{7,6},{8,9},{9,8},{10,11... | collective-permute-start | bytes 958472 | tf_op jit(solution)/shard_map/ppermute | solution.py:418
  32.3 1.0 %copy-start.3 = (bf16[16,32,256]{2,1,0:T(8,128)(2,1)S(1)}, bf16[16,32,256]{2,1,0:T(8,128)(2,1)}, u32[]{:S(2)}) copy-start(bf16[16,32,256]{2,1,0:T(8,128)(2,1)} %f1.5) | copy-start | bytes 786436
  33.2 0.9 %copy-start.6 = (bf16[16,32,256]{2,1,0:T(8,128)(2,1)S(1)}, bf16[16,32,256]{2,1,0:T(8,128)(2,1)}, u32[]{:S(2)}) copy-start(bf16[16,32,256]{2,1,0:T(8,128)(2,1)} %f2.5) | copy-start | bytes 786436
  36.4 11.3 %copy-start.7 = (bf16[256,576]{0,1:T(8,128)(2,1)S(1)}, bf16[256,576]{0,1:T(8,128)(2,1)}, u32[]{:S(2)}) copy-start(bf16[256,576]{0,1:T(8,128)(2,1)} %param.7) | copy-start | bytes 884740
  39.0 8.8 %collective-permute-start.4 = (f32[2,512]{1,0:T(2,128)S(1)}, f32[2,512]{1,0:T(2,128)S(1)}, u32[]{:S(2)}, u32[]{:S(2)}) collective-permute-start(f32[2,512]{1,0:T(2,128)S(1)} %get-tuple-element.26.own), channel_id=1, source_target_pairs={{32,64},{64,32},{96,128},{128,96},{160,192},{192,160},{224,256},{2... | collective-permute-start | bytes 12296 | tf_op jit(solution)/shard_map/ppermute | solution.py:462
  45.7 4.4 %collective-permute-start.5 = (f32[2,512]{1,0:T(2,128)S(1)}, f32[2,512]{1,0:T(2,128)S(1)}, u32[]{:S(2)}, u32[]{:S(2)}) collective-permute-start(f32[2,512]{1,0:T(2,128)S(1)} %get-tuple-element.26.own), channel_id=1, source_target_pairs={{0,32},{32,0},{64,96},{96,64},{128,160},{160,128},{192,224},{224,1... | collective-permute-start | bytes 12296 | tf_op jit(solution)/shard_map/ppermute | solution.py:463
  50.1 12.5 %collective-permute-start.6 = (f32[3,2,512]{2,1,0:T(2,128)S(1)}, f32[3,2,512]{2,1,0:T(2,128)S(1)}, u32[]{:S(2)}, u32[]{:S(2)}) collective-permute-start(f32[3,2,512]{2,1,0:T(2,128)S(1)} %pad_maximum_fusion), channel_id=1, source_target_pairs={{1,2},{2,1},{3,4},{4,3},{5,6},{6,5},{7,8},{8,7},{9,10},{10,9},{11,... | collective-permute-start | bytes 36872 | tf_op jit(solution)/shard_map/ppermute | solution.py:479
  52.0 10.6 %collective-permute-start.7 = (f32[3,2,512]{2,1,0:T(2,128)S(1)}, f32[3,2,512]{2,1,0:T(2,128)S(1)}, u32[]{:S(2)}, u32[]{:S(2)}) collective-permute-start(f32[3,2,512]{2,1,0:T(2,128)S(1)} %pad_maximum_fusion), channel_id=1, source_target_pairs={{0,1},{1,0},{2,3},{3,2},{4,5},{5,4},{6,7},{7,6},{8,9},{9,8},{10,11... | collective-permute-start | bytes 36872 | tf_op jit(solution)/shard_map/ppermute | solution.py:480

commit v2 on v1

--- a/solution.py
+++ b/solution.py
@@ -33,9 +33,13 @@
     return out
 
 
-def edge_kernel(rows, f1, f2, m_a, m_b, sems):
+def edge_kernel(rows, cols, f1, f2, m_a, m_b, m_o, g1, g2, col, sems):
     odd = lax.axis_index("lat") % 2
-    copies = []
+    lon_odd = lax.axis_index("lon") % 2 == 1
+    copies = [
+        pltpu.make_async_copy(f2, g2, sems.at[4]),
+        pltpu.make_async_copy(f1, g1, sems.at[5]),
+    ]
     for k, (msg, low) in enumerate(((m_a, odd), (m_b, 1 - odd))):
         copies.append(
             pltpu.make_async_copy(
@@ -52,22 +56,42 @@
     for copy in copies:
         copy.wait()
 
-
-def pack_kernel(rows, cols, f1, f2, ra, rb, m_x, m_in, ends, ext, col):
+    def column(frame, at):
+        lo = at // BC * BC
+        slab = frame[:, lo : lo + BC].astype(F32)
+        col[0:rows] = slab[:, at - lo, :]
+        return col[...].astype(BF16).reshape(-1, BC, CH)
+
+    def send(main, extra, one):
+        m_o[0:rows] = g2[:, main : main + BC]
+        m_o[rows : rows + col.shape[0] // BC] = column(g2, extra)
+        m_o[rows + col.shape[0] // BC :] = column(g1, one)
+
+    @pl.when(lon_odd)
+    def _():
+        send(cols - BC, cols - BC - 1, cols - 1)
+
+    @pl.when(jnp.logical_not(lon_odd))
+    def _():
+        send(0, BC, 0)
+
+
+def pack_kernel(rows, cols, f1, f2, ra, rb, m_c, m_in, ends, ext, col):
     lat_odd = lax.axis_index("lat") % 2 == 1
     lon_odd = lax.axis_index("lon") % 2 == 1
     n2 = rows + 2 * BR + 2
     n1 = rows + 2
+    nh = BR + 1
     slots2 = -(-n2 // BC)
     slots1 = -(-n1 // BC)
 
     def halo(north, south):
-        ext[0 : BR + 1] = north[0 : BR + 1]
-        ext[BR + 1 : BR + 1 + rows] = f2[...]
-        ext[BR + 1 + rows : n2] = south[0 : BR + 1]
-        ext[n2] = north[BR + 1]
+        ext[0:nh] = north[0:nh]
+        ext[nh : nh + rows] = f2[...]
+        ext[nh + rows : n2] = south[0:nh]
+        ext[n2] = north[nh]
         ext[n2 + 1 : n2 + 1 + rows] = f1[...]
-        ext[n2 + 1 + rows] = south[BR + 1]
+        ext[n2 + 1 + rows] = south[nh]
 
     @pl.when(lat_odd)
     def _():
@@ -82,32 +106,38 @@
     final = ext[0:n2, cols - BC : cols].astype(F32)
     ends[1, 0:n2] = final[:, BC - 1, :]
 
+    def column(lo, hi, at):
+        base = at // BC * BC
+        return ext[lo:hi, base : base + BC].astype(F32)[:, at - base, :]
+
     def edge(msg, main, extra, one):
         msg[0:n2] = ext[0:n2, main : main + BC]
-        lo = extra // BC * BC
-        slab = ext[0:n2, lo : lo + BC].astype(F32)
-        col[0:n2] = slab[:, extra - lo, :]
+        col[0:n2] = column(0, n2, extra)
         msg[n2 : n2 + slots2] = col[0 : slots2 * BC].astype(BF16).reshape(slots2, BC, CH)
-        lo = one // BC * BC
-        slab = ext[n2 : n2 + n1, lo : lo + BC].astype(F32)
-        col[0:n1] = slab[:, one - lo, :]
+        col[0:n1] = column(n2, n2 + n1, one)
         msg[n2 + slots2 :] = col[0 : slots1 * BC].astype(BF16).reshape(slots1, BC, CH)
 
-    def right(msg):
-        edge(msg, cols - BC, cols - BC - 1, cols - 1)
-
-    def left(msg):
-        edge(msg, 0, BC, 0)
+    def corner(msg, main, extra, one):
+        msg[0:nh] = ext[0:nh, main : main + BC]
+        msg[nh : 2 * nh] = ext[n2 - nh : n2, main : main + BC]
+        col[0:nh] = column(0, nh, extra)
+        col[nh : 2 * nh] = column(n2 - nh, n2, extra)
+        col[2 * nh : 2 * nh + 1] = column(n2, n2 + 1, one)
+        col[2 * nh + 1 : 2 * nh + 2] = column(n2 + n1 - 1, n2 + n1, one)
+        msg[2 * nh :] = col[0 : 2 * BC].astype(BF16).reshape(2, BC, CH)
+
+    right = (cols - BC, cols - BC - 1, cols - 1)
+    left = (0, BC, 0)
 
     @pl.when(lon_odd)
     def _():
-        right(m_x)
-        left(m_in)
+        corner(m_c, *right)
+        edge(m_in, *left)
 
     @pl.when(jnp.logical_not(lon_odd))
     def _():
-        left(m_x)
-        right(m_in)
+        corner(m_c, *left)
+        edge(m_in, *right)
 
 
 def conv(x, w, row, count, width):
@@ -163,60 +193,108 @@
     run(x2, e2, ends2, rows + 2 * BR)
 
 
-def flow_kernel(rows, cols, o2, o1, ends2, ends1, edges, c_x, c_in, w, flow, enc_one, ext, xs, e2):
+def finish_side(rows, cols, side, w, o2, o1, ends2, ends1, edges, ext, xs, one, put):
+    n2 = rows + 2 * BR + 2
+    tall = rows + 2 * BR
+    place = lax.broadcasted_iota(jnp.int32, (1, BC, CH), 1)
+    inner = edges[side, 0:n2][:, None, :]
+    at = BR - 1 if side else BR + BC
+    ext[:, at : at + 1] = inner
+    for b in range(3):
+        xs[b] = ext[:, BR - 1 + b : BR - 1 + b + BC].astype(BF16)
+    strip = conv(xs, w, 0, tall, BC).astype(BF16).reshape(tall, BC, CH)
+    near = ext[:, BR : BR + 1] if side else ext[:, BR + BC - 1 : BR + BC]
+    near = near[:, 0, :].astype(BF16)
+    taps = jnp.concatenate(
+        [w[(3 * a + 2 * side) * CH : (3 * a + 2 * side + 1) * CH] for a in range(3)], axis=0
+    )
+    lhs = jnp.concatenate(
+        [jnp.concatenate([near[a : a + tall], one[a : a + rows]], axis=0) for a in range(3)],
+        axis=1,
+    )
+    more = jnp.dot(lhs, taps, preferred_element_type=F32)
+    hit = place == (BC - 1 if side else 0)
+    lo = cols - BC if side else 0
+    full = ends2[side] + more[0:tall]
+    two = jnp.where(hit, full[:, None, :], o2[:, lo : lo + BC].astype(F32)).astype(BF16)
+    full = ends1[side] + more[tall : tall + rows]
+    first = jnp.where(hit, full[:, None, :], o1[:, lo : lo + BC].astype(F32)).astype(BF16)
+    put(side, strip, two, first)
+
+
+def strip_kernel(rows, cols, o2, o1, ends2, ends1, edges, chip, w, strip, two, first, ext, xs):
+    lon_odd = lax.axis_index("lon") % 2 == 1
+    c_in = chip.at[1 - lax.axis_index("lon") % 2]
+    n2 = rows + 2 * BR + 2
+    n1 = rows + 2
+    slots2 = -(-n2 // BC)
+    slots1 = -(-n1 // BC)
+
+    def put(side, *values):
+        for ref, value in zip((strip, two, first), values):
+            ref[...] = value
+
+    def run(side):
+        ext[:, BR : BR + BC] = c_in[0:n2].astype(F32)
+        extra = c_in[n2 : n2 + slots2].astype(F32).reshape(slots2 * BC, CH)
+        at = BR + BC if side else BR - 1
+        ext[:, at : at + 1] = extra[0:n2][:, None, :]
+        one = c_in[n2 + slots2 :].astype(F32).reshape(slots1 * BC, CH)[0:n1].astype(BF16)
+        finish_side(rows, cols, side, w, o2, o1, ends2, ends1, edges, ext, xs, one, put)
+
+    @pl.when(lon_odd)
+    def _():
+        run(0)
+
+    @pl.when(jnp.logical_not(lon_odd))
+    def _():
+        run(1)
+
+
+def flow_kernel(
+    rows, cols, o2, o1, ends2, ends1, edges, strip_in, two_in, first_in, c_o, c_c, w,
+    flow, enc_one, ext, xs, col, e2,
+):
     lat = lax.axis_index("lat")
     lon_odd = lax.axis_index("lon") % 2 == 1
     n2 = rows + 2 * BR + 2
     n1 = rows + 2
+    nh = BR + 1
     wide = cols + 2 * BC
-    tall = rows + 2 * BR
-    slots2 = -(-n2 // BC)
-    slots1 = -(-n1 // BC)
-    place = lax.broadcasted_iota(jnp.int32, (1, BC, CH), 1)
-
-    def beside(side, msg):
-        extra = msg[n2 : n2 + slots2].astype(F32).reshape(slots2 * BC, CH)[0:n2][:, None, :]
-        inner = edges[side, 0:n2][:, None, :]
-        ext[:, BR : BR + BC] = msg[0:n2].astype(F32)
-        ext[:, BR - 1 : BR] = inner if side else extra
-        ext[:, BR + BC : BR + BC + 1] = extra if side else inner
-        for b in range(3):
-            xs[b] = ext[:, BR - 1 + b : BR - 1 + b + BC].astype(BF16)
+    pads = (c_o.shape[0] - rows) // 2
+
+    def put(side, strip, two, first):
         at = BC + cols if side else 0
-        e2[:, at : at + BC] = conv(xs, w, 0, tall, BC).astype(BF16).reshape(tall, BC, CH)
-        near = ext[:, BR : BR + 1] if side else ext[:, BR + BC - 1 : BR + BC]
-        near = near[:, 0, :].astype(BF16)
-        one = msg[n2 + slots2 :].reshape(slots1 * BC, CH)
-        one = one.astype(F32)[0:n1].astype(BF16)
-        taps = jnp.concatenate(
-            [w[(3 * a + 2 * side) * CH : (3 * a + 2 * side + 1) * CH] for a in range(3)], axis=0
-        )
-        lhs = jnp.concatenate(
-            [
-                jnp.concatenate([near[a : a + tall], one[a : a + rows]], axis=0)
-                for a in range(3)
-            ],
-            axis=1,
-        )
-        more = jnp.dot(lhs, taps, preferred_element_type=F32)
-        hit = place == (BC - 1 if side else 0)
+        e2[:, at : at + BC] = strip
         lo = cols - BC if side else 0
-        full = ends2[side] + more[0:tall]
-        slab = jnp.where(hit, full[:, None, :], o2[:, lo : lo + BC].astype(F32))
-        e2[:, BC + lo : 2 * BC + lo] = slab.astype(BF16)
-        full = ends1[side] + more[tall : tall + rows]
-        slab = jnp.where(hit, full[:, None, :], o1[:, lo : lo + BC].astype(F32))
-        enc_one[:, lo : lo + BC] = slab.astype(BF16)
+        e2[:, BC + lo : 2 * BC + lo] = two
+        enc_one[:, lo : lo + BC] = first
+
+    def run(side):
+        put(1 - side, strip_in[...], two_in[...], first_in[...])
+        ext[0:nh, BR : BR + BC] = c_c[0:nh].astype(F32)
+        ext[nh : nh + rows, BR : BR + BC] = c_o[0:rows].astype(F32)
+        ext[nh + rows :, BR : BR + BC] = c_c[nh : 2 * nh].astype(F32)
+        far = c_c[2 * nh :].astype(F32).reshape(2 * BC, CH)
+        mine = c_o[rows : rows + pads].astype(F32).reshape(pads * BC, CH)
+        at = BR + BC if side else BR - 1
+        ext[0:nh, at : at + 1] = far[0:nh][:, None, :]
+        ext[nh : nh + rows, at : at + 1] = mine[0:rows][:, None, :]
+        ext[nh + rows :, at : at + 1] = far[nh : 2 * nh][:, None, :]
+        mine = c_o[rows + pads :].astype(F32).reshape(pads * BC, CH)
+        col[0:1] = far[2 * nh : 2 * nh + 1]
+        col[1 : 1 + rows] = mine[0:rows]
+        col[1 + rows : 2 + rows] = far[2 * nh + 1 : 2 * nh + 2]
+        one = col[0:n1].astype(BF16)
+        finish_side(rows, cols, side, w, o2, o1, ends2, ends1, edges, ext, xs, one, put)
 
     @pl.when(lon_odd)
     def _():
-        beside(0, c_in)
-        beside(1, c_x)
+        run(1)
 
     @pl.when(jnp.logical_not(lon_odd))
     def _():
-        beside(0, c_x)
-        beside(1, c_in)
+        run(0)
 
     bands = rows // BR
     queries = BR * cols
@@ -280,9 +358,10 @@
             mix[:, k, :, c0 : c0 + step] = expo / total[None]
 
 
-def up_kernel(rows, cols, mix, own, lat_a, lat_b, lon_x, lon_in, out, pad):
+def up_kernel(rows, cols, mix, own, lat_a, lat_b, lon_x, chip, out, pad):
     lat_odd = lax.axis_index("lat") % 2 == 1
     lon_odd = lax.axis_index("lon") % 2 == 1
+    lon_in = chip.at[1 - lax.axis_index("lon") % 2]
     cells = rows * cols
     width = cells + 2 * cols
 
@@ -380,31 +459,43 @@
     cells = rows * cols
     n2, n1 = rows + 2 * BR + 2, rows + 2
     slots = n2 + -(-n2 // BC) + -(-n1 // BC)
+    own_slots = rows + 2 * -(-rows // BC)
     wide = cols + 2 * BC
     lats, lons = lax.axis_size("lat"), lax.axis_size("lon")
     far_lat = pair_perm(lats, 1, False)
     near_lat = pair_perm(lats, 0, False)
     far_lon = pair_perm(lons, 1, True)
-    near_lon = pair_perm(lons, 0, True)
+    chips = [[i, i + 1] for i in range(0, lons, 2)]
 
     edge_rows = jax.ShapeDtypeStruct((BR + 2, cols, CH), BF16)
-    m_a, m_b = pl.pallas_call(
-        functools.partial(edge_kernel, rows),
-        out_shape=(edge_rows, edge_rows),
-        in_specs=[pl.BlockSpec(memory_space=pl.ANY)] * 2,
-        out_specs=(VMEM, VMEM),
-        scratch_shapes=[pltpu.SemaphoreType.DMA((4,))],
+    tile = jax.ShapeDtypeStruct((rows, cols, CH), BF16)
+    m_a, m_b, m_o, one, two = pl.pallas_call(
+        functools.partial(edge_kernel, rows, cols),
+        out_shape=(edge_rows, edge_rows, jax.ShapeDtypeStruct((own_slots, BC, CH), BF16), tile, tile),
+        in_specs=[pl.BlockSpec(memory_space=pltpu.MemorySpace.HBM)] * 2,
+        out_specs=(VMEM,) * 5,
+        scratch_shapes=[
+            pltpu.VMEM((-(-rows // BC) * BC, CH), F32),
+            pltpu.SemaphoreType.DMA((6,)),
+        ],
         compiler_params=params(8),
-        name="edge_rows",
-    )(frame_one, frame_two)
+        name="edges",
+    )(
+        pltpu.with_memory_space_constraint(frame_one, pltpu.MemorySpace.HBM),
+        pltpu.with_memory_space_constraint(frame_two, pltpu.MemorySpace.HBM),
+    )
     row_a = lax.ppermute(m_a, "lat", far_lat)
     row_b = lax.ppermute(m_b, "lat", near_lat)
-
-    msg = jax.ShapeDtypeStruct((slots, BC, CH), BF16)
+    col_o = lax.ppermute(m_o, "lon", far_lon)
+
     n2_pad = -(-n2 // BC) * BC
-    m_x, m_in, edges = pl.pallas_call(
+    m_c, m_in, edges = pl.pallas_call(
         functools.partial(pack_kernel, rows, cols),
-        out_shape=(msg, msg, jax.ShapeDtypeStruct((2, n2_pad, CH), F32)),
+        out_shape=(
+            jax.ShapeDtypeStruct((2 * BR + 4, BC, CH), BF16),
+            jax.ShapeDtypeStruct((slots, BC, CH), BF16),
+            jax.ShapeDtypeStruct((2, n2_pad, CH), F32),
+        ),
         in_specs=[VMEM] * 4,
         out_specs=(VMEM,) * 3,
         scratch_shapes=[
@@ -413,9 +504,9 @@
         ],
         compiler_params=params(16),
         name="pack",
-    )(frame_one, frame_two, row_a, row_b)
-    col_x = lax.ppermute(m_x, "lon", far_lon)
-    col_in = lax.ppermute(m_in, "lon", near_lon)
+    )(one, two, row_a, row_b)
+    col_c = lax.ppermute(m_c, "lon", far_lon)
+    col_in = lax.all_gather(m_in, "lon", axis_index_groups=chips)
 
     tall = rows + 2 * BR
     weight = enc_weight.reshape(9 * CH, CH)
@@ -440,7 +531,22 @@
             flops=2 * 9 * CH * CH * cols * (tall + rows), bytes_accessed=4 << 20, transcendentals=0
         ),
         name="encode_own",
-    )(frame_one, frame_two, row_a, row_b, weight)
+    )(one, two, row_a, row_b, weight)
+
+    strip = jax.ShapeDtypeStruct((tall, BC, CH), BF16)
+    side_scratch = [pltpu.VMEM((n2, BC + 2 * BR, CH), F32), pltpu.VMEM((3, n2, BC, CH), BF16)]
+    strip_in, two_in, first_in = pl.pallas_call(
+        functools.partial(strip_kernel, rows, cols),
+        out_shape=(strip, strip, jax.ShapeDtypeStruct((rows, BC, CH), BF16)),
+        in_specs=[VMEM] * 7,
+        out_specs=(VMEM,) * 3,
+        scratch_shapes=side_scratch,
+        compiler_params=params(16),
+        cost_estimate=pl.CostEstimate(
+            flops=2 * 9 * CH * CH * BC * tall, bytes_accessed=4 << 20, transcendentals=0
+        ),
+        name="strip",
+    )(own_two, own_one, ends_two, ends_one, edges, col_in, weight)
 
     flow, enc_one = pl.pallas_call(
         functools.partial(flow_kernel, rows, cols),
@@ -448,16 +554,15 @@
             jax.ShapeDtypeStruct((2, cells), F32),
             jax.ShapeDtypeStruct((rows, cols, CH), BF16),
         ),
-        in_specs=[VMEM] * 8,
+        in_specs=[VMEM] * 11,
         out_specs=(VMEM, VMEM),
-        scratch_shapes=[
-            pltpu.VMEM((n2, BC + 2 * BR, CH), F32),
-            pltpu.VMEM((3, n2, BC, CH), BF16),
-            pltpu.VMEM((tall, wide, CH), BF16),
-        ],
+        scratch_shapes=side_scratch
+        + [pltpu.VMEM((-(-n1 // BR) * BR, CH), F32), pltpu.VMEM((tall, wide, CH), BF16)],
         compiler_params=params(20),
         name="flow",
-    )(own_two, own_one, ends_two, ends_one, edges, col_x, col_in, weight)
+    )(
+        own_two, own_one, ends_two, ends_one, edges, strip_in, two_in, first_in, col_o, col_c, weight
+    )
 
     flow_a = lax.ppermute(flow, "lat", far_lat)
     flow_b = lax.ppermute(flow, "lat", near_lat)
@@ -477,7 +582,7 @@
 
     trio = jnp.stack([flow, flow_a, flow_b])
     lon_x = lax.ppermute(trio, "lon", far_lon)
-    lon_in = lax.ppermute(trio, "lon", near_lon)
+    lon_in = lax.all_gather(trio, "lon", axis_index_groups=chips)
     lanes = -(-(cells + 2 * cols) // 128) * 128
     return pl.pallas_call(
         functools.partial(up_kernel, rows, cols),

time: 64.8 us -> 62.5 us (0.965)
  the two profiles are of different devices: /device:TPU:7 before, /device:TPU:6 now
where the time goes in v2:
time: 62.5 us; the launch traced here: 62.2 us
  starting transfers between devices  41.9 us (67%)
  Pallas kernels  8.83 us (14%)
  waiting for transfers between devices  7.11 us (11%)
  blocking collectives  4.09 us (7%)
    ppermute x1, starting transfers between devices, body(): col_o = lax.ppermute(m_o, 'lon', far_lon)  10.3 us
    ppermute x1, starting transfers between devices, body(): row_a = lax.ppermute(m_a, 'lat', far_lat)  8.16 us
    ppermute x1, starting transfers between devices, body(): flow_a = lax.ppermute(flow, 'lat', far_lat)  7.69 us
    ppermute x1, starting transfers between devices, body(): col_c = lax.ppermute(m_c, 'lon', far_lon)  6.24 us
    ppermute x1, starting transfers between devices, body(): lon_x = lax.ppermute(trio, 'lon', far_lon)  5.72 us
    ppermute x1, waiting for transfers between devices, body(): flow_b = lax.ppermute(flow, 'lat', near_lat)  3.49 us
    ppermute x1, waiting for transfers between devices, body(): lon_x = lax.ppermute(trio, 'lon', far_lon)  2.64 us
    all_gather x1, blocking collectives, body(): col_in = lax.all_gather(m_in, 'lon', axis_index_groups=chips)  2.26 us
  transfers between devices with their start and end apart: 7, of which 3 were waited for; matrix products, arithmetic and copies ran while one was open for 0% of the time, Pallas kernels for 7%

profile of v2, /device:TPU:6, one launch (start us, length us, event | category | flops | bytes accessed | tf_op | source)
XLA Modules:
  0.0 62.2 jit_solution(9333336076905600540)
XLA Ops:
  0.0 0.0 copy-start
  0.0 1.3 %edges.1 = (bf16[10,32,256]{2,1,0:T(8,128)(2,1)S(1)}, bf16[10,32,256]{2,1,0:T(8,128)(2,1)S(1)}, bf16[18,16,256]{2,1,0:T(8,128)(2,1)S(1)}, bf16[16,32,256]{2,1,0:T(8,128)(2,1)S(1)}, bf16[16,32,256]{2,1,0:T(8,128)(2,1)S(1)}) custom-call(bf16[16,32,256]{2,1,0:T(8,128)(2,1)} %f1.1, bf16[16,32,256]{2,1,0:T(8,128)(2,1)} %f2.1), custom_call_target="tpu_custom_call" | custom-call | tf_op jit(solution)/shard_map/edges/pallas_call | solution.py:472
  1.3 8.2 %collective-permute-start = (bf16[10,32,256]{2,1,0:T(8,128)(2,1)S(1)}, bf16[10,32,256]{2,1,0:T(8,128)(2,1)S(1)}, u32[]{:S(2)}, u32[]{:S(2)}) collective-permute-start(bf16[10,32,256]{2,1,0:T(8,128)(2,1)S(1)} %get-tuple-element.24), channel_id=1, source_target_pairs={{32,64},{64,32},{96,128},{128,96},{160,192},{192,160},{224,256},{2... | collective-permute-start | bytes 491528 | tf_op jit(solution)/shard_map/ppermute | solution.py:487
  9.5 1.9 %collective-permute-start.1 = (bf16[10,32,256]{2,1,0:T(8,128)(2,1)S(1)}, bf16[10,32,256]{2,1,0:T(8,128)(2,1)S(1)}, u32[]{:S(2)}, u32[]{:S(2)}) collective-permute-start(bf16[10,32,256]{2,1,0:T(8,128)(2,1)S(1)} %get-tuple-element.25), channel_id=1, source_target_pairs={{0,32},{32,0},{64,96},{96,64},{128,160},{160,128},{192,224},{224,1... | collective-permute-start | bytes 491528 | tf_op jit(solution)/shard_map/ppermute | solution.py:488
  11.4 10.3 %collective-permute-start.2 = (bf16[18,16,256]{2,1,0:T(8,128)(2,1)S(1)}, bf16[18,16,256]{2,1,0:T(8,128)(2,1)S(1)}, u32[]{:S(2)}, u32[]{:S(2)}) collective-permute-start(bf16[18,16,256]{2,1,0:T(8,128)(2,1)S(1)} %get-tuple-element.35), channel_id=1, source_target_pairs={{1,2},{2,1},{3,4},{4,3},{5,6},{6,5},{7,8},{8,7},{9,10},{10,9},{11,... | collective-permute-start | bytes 442376 | tf_op jit(solution)/shard_map/ppermute | solution.py:489
  21.7 0.0 collective-permute-done.ra
  21.7 0.0 collective-permute-done.1.rb
  21.7 0.2 pack.1
  21.9 6.2 %collective-permute-start.3 = (bf16[20,16,256]{2,1,0:T(8,128)(2,1)S(1)}, bf16[20,16,256]{2,1,0:T(8,128)(2,1)S(1)}, u32[]{:S(2)}, u32[]{:S(2)}) collective-permute-start(bf16[20,16,256]{2,1,0:T(8,128)(2,1)S(1)} %get-tuple-element.36), channel_id=1, source_target_pairs={{1,2},{2,1},{3,4},{4,3},{5,6},{6,5},{7,8},{8,7},{9,10},{10,9},{11,... | collective-permute-start | bytes 491528 | tf_op jit(solution)/shard_map/ppermute | solution.py:508
  28.2 0.0 copy-done
  28.2 2.2 %encode_own.1 = (bf16[32,32,256]{2,1,0:T(8,128)(2,1)S(1)}, bf16[16,32,256]{2,1,0:T(8,128)(2,1)S(1)}, f32[2,32,256]{2,1,0:T(8,128)S(1)}, f32[2,16,256]{2,1,0:T(8,128)S(1)}) custom-call(bf16[16,32,256]{2,1,0:T(8,128)(2,1)S(1)} %get-tuple-element.22.f1, bf16[16,32,256]{2,1,0:T(8,128)(2,1)S(1)} %get-tuple-element.23.f2, ...), custom_call_target="tpu_custom_call" | custom-call | flops 1811939328 | bytes 4194304 | tf_op jit(solution)/shard_map/encode_own/pallas_call | solution.py:513
  30.4 2.3 %all-gather = bf16[78,16,256]{2,1,0:T(8,128)(2,1)S(1)} all-gather(bf16[39,16,256]{2,1,0:T(8,128)(2,1)S(1)} %get-tuple-element.31), channel_id=2, replica_groups={{0,1},{2,3},{4,5},{6,7},{8,9},{10,11},{12,13},{14,15},{16,17},{18,19},{..., dimensions={0}, use_global_device_ids=true | all-gather | bytes 958464 | tf_op jit(solution)/shard_map/all_gather | solution.py:509
  32.6 1.0 %strip.1 = (bf16[32,16,256]{2,1,0:T(8,128)(2,1)S(1)}, bf16[32,16,256]{2,1,0:T(8,128)(2,1)S(1)}, bf16[16,16,256]{2,1,0:T(8,128)(2,1)S(1)}) custom-call(bf16[32,32,256]{2,1,0:T(8,128)(2,1)S(1)} %get-tuple-element.26.o2, bf16[16,32,256]{2,1,0:T(8,128)(2,1)S(1)} %get-tuple-element.27.o1, f32[2,32,256]{2,1,0:T(8,128)S(1)} %get-tuple-element.28.ends2, ...), custom_call_target="tpu_custom_call" | custom-call | flops 603979776 | bytes 4194304 | tf_op jit(solution)/shard_map/strip/pallas_call | solution.py:538
  33.6 0.0 collective-permute-done.2.c_o
  33.6 1.0 %collective-permute-done.3.c_c = bf16[20,16,256]{2,1,0:T(8,128)(2,1)S(1)} collective-permute-done((bf16[20,16,256]{2,1,0:T(8,128)(2,1)S(1)}, bf16[20,16,256]{2,1,0:T(8,128)(2,1)S(1)}, u32[]{:S(2)}, u32[]{:S(2)}) %collective-permute-start.3) | collective-permute-done | bytes 163872 | tf_op jit(solution)/shard_map/ppermute | solution.py:508
  34.6 0.0 copy-start.1
  34.6 1.7 %flow.1 = (f32[2,512]{1,0:T(2,128)S(1)}, bf16[16,32,256]{2,1,0:T(8,128)(2,1)S(1)}) custom-call(bf16[32,32,256]{2,1,0:T(8,128)(2,1)S(1)} %get-tuple-element.26.o2, bf16[16,32,256]{2,1,0:T(8,128)(2,1)S(1)} %get-tuple-element.27.o1, f32[2,32,256]{2,1,0:T(8,128)S(1)} %get-tuple-element.28.ends2, f32[2,16,256]{2,1,0:T(8,128)S(1)} %get-tuple-element.29.ends1, ...), custom_call_target="tpu_custom_call" | custom-call | tf_op jit(solution)/shard_map/flow/pallas_call | solution.py:551
  36.3 7.7 %collective-permute-start.4 = (f32[2,512]{1,0:T(2,128)S(1)}, f32[2,512]{1,0:T(2,128)S(1)}, u32[]{:S(2)}, u32[]{:S(2)}) collective-permute-start(f32[2,512]{1,0:T(2,128)S(1)} %get-tuple-element.38.own), channel_id=1, source_target_pairs={{32,64},{64,32},{96,128},{128,96},{160,192},{192,160},{224,256},{2... | collective-permute-start | bytes 12296 | tf_op jit(solution)/shard_map/ppermute | solution.py:567
  44.0 1.9 %collective-permute-start.5 = (f32[2,512]{1,0:T(2,128)S(1)}, f32[2,512]{1,0:T(2,128)S(1)}, u32[]{:S(2)}, u32[]{:S(2)}) collective-permute-start(f32[2,512]{1,0:T(2,128)S(1)} %get-tuple-element.38.own), channel_id=1, source_target_pairs={{0,32},{32,0},{64,96},{96,64},{128,160},{160,128},{192,224},{224,1... | collective-permute-start | bytes 12296 | tf_op jit(solution)/shard_map/ppermute | solution.py:568
  45.9 0.0 copy-done.1
  45.9 0.1 copy.6
  46.0 0.0 collective-permute-done.4.lat_a
  46.0 3.5 %collective-permute-done.5.lat_b = f32[2,512]{1,0:T(2,128)S(1)} collective-permute-done((f32[2,512]{1,0:T(2,128)S(1)}, f32[2,512]{1,0:T(2,128)S(1)}, u32[]{:S(2)}, u32[]{:S(2)}) %collective-permute-start.5) | collective-permute-done | bytes 4128 | tf_op jit(solution)/shard_map/ppermute | solution.py:568
  49.5 5.7 %collective-permute-start.6 = (f32[3,2,512]{2,1,0:T(2,128)S(1)}, f32[3,2,512]{2,1,0:T(2,128)S(1)}, u32[]{:S(2)}, u32[]{:S(2)}) collective-permute-start(f32[3,2,512]{2,1,0:T(2,128)S(1)} %pad_maximum_fusion), channel_id=1, source_target_pairs={{1,2},{2,1},{3,4},{4,3},{5,6},{6,5},{7,8},{8,7},{9,10},{10,9},{11,... | collective-permute-start | bytes 36872 | tf_op jit(solution)/shard_map/ppermute | solution.py:584
  55.2 0.8 %mix.1 = f32[9,8,8,512]{3,2,1,0:T(8,128)S(1)} custom-call(bf16[16,32,256]{2,1,0:T(8,128)(2,1)S(1)} %get-tuple-element.37.enc_one, bf16[576,256]{1,0:T(8,128)(2,1)S(1)} %bitcast.14), custom_call_target="tpu_custom_call" | custom-call | flops 150994944 | bytes 1179648 | tf_op jit(solution)/shard_map/mix/pallas_call | solution.py:571
  56.0 1.8 %all-gather.1 = f32[6,2,512]{2,1,0:T(2,128)S(1)} all-gather(f32[3,2,512]{2,1,0:T(2,128)S(1)} %pad_maximum_fusion), channel_id=3, replica_groups={{0,1},{2,3},{4,5},{6,7},{8,9},{10,11},{12,13},{14,15},{16,17},{18,19},{..., dimensions={0}, use_global_device_ids=true | all-gather | bytes 36864 | tf_op jit(solution)/shard_map/all_gather | solution.py:585
  57.8 2.6 %collective-permute-done.6.lon_x = f32[3,2,512]{2,1,0:T(2,128)S(1)} collective-permute-done((f32[3,2,512]{2,1,0:T(2,128)S(1)}, f32[3,2,512]{2,1,0:T(2,128)S(1)}, u32[]{:S(2)}, u32[]{:S(2)}) %collective-permute-start.6) | collective-permute-done | bytes 12320 | tf_op jit(solution)/shard_map/ppermute | solution.py:584
  60.5 1.7 %upsample.1 = f32[2,128,256]{2,1,0:T(8,128)} custom-call(f32[9,8,8,512]{3,2,1,0:T(8,128)S(1)} %mix.1, f32[2,512]{1,0:T(2,128)S(1)} %get-tuple-element.38.own, f32[2,512]{1,0:T(2,128)S(1)} %collective-permute-done.4.lat_a, f32[2,512]{1,0:T(2,128)S(1)} %collective-permute-done.5.lat_b, f32[3,2,512]{2,1,0:T(2,128)S(1)} %collective-permute-done.6.lon_x, ...), custom_call_target="tpu_custom_call" | custom-call | tf_op jit(solution)/shard_map/upsample/pallas_call | solution.py:587
  (1 shorter events, 0.0 us)
Async XLA Ops:
  0.0 28.2 %copy-start = (bf16[3,3,256,256]{3,2,1,0:T(8,128)(2,1)S(1)}, bf16[3,3,256,256]{3,2,1,0:T(8,128)(2,1)}, u32[]{:S(2)}) copy-start(bf16[3,3,256,256]{3,2,1,0:T(8,128)(2,1)} %param.6) | copy-start | bytes 3538948
  1.3 20.4 %collective-permute-start = (bf16[10,32,256]{2,1,0:T(8,128)(2,1)S(1)}, bf16[10,32,256]{2,1,0:T(8,128)(2,1)S(1)}, u32[]{:S(2)}, u32[]{:S(2)}) collective-permute-start(bf16[10,32,256]{2,1,0:T(8,128)(2,1)S(1)} %get-tuple-element.24), channel_id=1, source_target_pairs={{32,64},{64,32},{96,128},{128,96},{160,192},{192,160},{224,256},{2... | collective-permute-start | bytes 491528 | tf_op jit(solution)/shard_map/ppermute | solution.py:487
  9.5 12.2 %collective-permute-start.1 = (bf16[10,32,256]{2,1,0:T(8,128)(2,1)S(1)}, bf16[10,32,256]{2,1,0:T(8,128)(2,1)S(1)}, u32[]{:S(2)}, u32[]{:S(2)}) collective-permute-start(bf16[10,32,256]{2,1,0:T(8,128)(2,1)S(1)} %get-tuple-element.25), channel_id=1, source_target_pairs={{0,32},{32,0},{64,96},{96,64},{128,160},{160,128},{192,224},{224,1... | collective-permute-start | bytes 491528 | tf_op jit(solution)/shard_map/ppermute | solution.py:488
  11.4 22.2 %collective-permute-start.2 = (bf16[18,16,256]{2,1,0:T(8,128)(2,1)S(1)}, bf16[18,16,256]{2,1,0:T(8,128)(2,1)S(1)}, u32[]{:S(2)}, u32[]{:S(2)}) collective-permute-start(bf16[18,16,256]{2,1,0:T(8,128)(2,1)S(1)} %get-tuple-element.35), channel_id=1, source_target_pairs={{1,2},{2,1},{3,4},{4,3},{5,6},{6,5},{7,8},{8,7},{9,10},{10,9},{11,... | collective-permute-start | bytes 442376 | tf_op jit(solution)/shard_map/ppermute | solution.py:489
  21.9 12.7 %collective-permute-start.3 = (bf16[20,16,256]{2,1,0:T(8,128)(2,1)S(1)}, bf16[20,16,256]{2,1,0:T(8,128)(2,1)S(1)}, u32[]{:S(2)}, u32[]{:S(2)}) collective-permute-start(bf16[20,16,256]{2,1,0:T(8,128)(2,1)S(1)} %get-tuple-element.36), channel_id=1, source_target_pairs={{1,2},{2,1},{3,4},{4,3},{5,6},{6,5},{7,8},{8,7},{9,10},{10,9},{11,... | collective-permute-start | bytes 491528 | tf_op jit(solution)/shard_map/ppermute | solution.py:508
  34.6 11.3 %copy-start.1 = (bf16[256,576]{0,1:T(8,128)(2,1)S(1)}, bf16[256,576]{0,1:T(8,128)(2,1)}, u32[]{:S(2)}) copy-start(bf16[256,576]{0,1:T(8,128)(2,1)} %param.7) | copy-start | bytes 884740
  36.3 9.7 %collective-permute-start.4 = (f32[2,512]{1,0:T(2,128)S(1)}, f32[2,512]{1,0:T(2,128)S(1)}, u32[]{:S(2)}, u32[]{:S(2)}) collective-permute-start(f32[2,512]{1,0:T(2,128)S(1)} %get-tuple-element.38.own), channel_id=1, source_target_pairs={{32,64},{64,32},{96,128},{128,96},{160,192},{192,160},{224,256},{2... | collective-permute-start | bytes 12296 | tf_op jit(solution)/shard_map/ppermute | solution.py:567
  44.0 5.5 %collective-permute-start.5 = (f32[2,512]{1,0:T(2,128)S(1)}, f32[2,512]{1,0:T(2,128)S(1)}, u32[]{:S(2)}, u32[]{:S(2)}) collective-permute-start(f32[2,512]{1,0:T(2,128)S(1)} %get-tuple-element.38.own), channel_id=1, source_target_pairs={{0,32},{32,0},{64,96},{96,64},{128,160},{160,128},{192,224},{224,1... | collective-permute-start | bytes 12296 | tf_op jit(solution)/shard_map/ppermute | solution.py:568
  49.5 11.0 %collective-permute-start.6 = (f32[3,2,512]{2,1,0:T(2,128)S(1)}, f32[3,2,512]{2,1,0:T(2,128)S(1)}, u32[]{:S(2)}, u32[]{:S(2)}) collective-permute-start(f32[3,2,512]{2,1,0:T(2,128)S(1)} %pad_maximum_fusion), channel_id=1, source_target_pairs={{1,2},{2,1},{3,4},{4,3},{5,6},{6,5},{7,8},{8,7},{9,10},{10,9},{11,... | collective-permute-start | bytes 36872 | tf_op jit(solution)/shard_map/ppermute | solution.py:584

commit v3 on v2

v3 whole, which is shorter than its diff:
```python
import functools
import math

import jax
import jax.numpy as jnp
from jax import lax
from jax.experimental import pallas as pl
from jax.experimental.pallas import tpu as pltpu
from jax.sharding import PartitionSpec as P

CH = 256
BR = 8
BC = 16
UP = 8
F32 = jnp.float32
BF16 = jnp.bfloat16
VMEM = pl.BlockSpec(memory_space=pltpu.VMEM)


def params(mib):
    return pltpu.CompilerParams(vmem_limit_bytes=mib * 1024 * 1024)


def pair_perm(size, first, wrap):
    out = []
    for i in range(first, size, 2):
        j = i + 1
        if j >= size:
            if not wrap:
                continue
            j -= size
        out += [(i, j), (j, i)]
    return out


def edge_kernel(rows, cols, f1, f2, m_a, m_b, m_o, g1, g2, col, sems):
    odd = lax.axis_index("lat") % 2
    lon_odd = lax.axis_index("lon") % 2 == 1
    copies = [
        pltpu.make_async_copy(f2, g2, sems.at[4]),
        pltpu.make_async_copy(f1, g1, sems.at[5]),
    ]
    for k, (msg, low) in enumerate(((m_a, odd), (m_b, 1 - odd))):
        copies.append(
            pltpu.make_async_copy(
                f2.at[pl.ds(low * (rows - BR - 1), BR + 1)], msg.at[pl.ds(0, BR + 1)], sems.at[2 * k]
            )
        )
        copies.append(
            pltpu.make_async_copy(
                f1.at[pl.ds(low * (rows - 1), 1)], msg.at[pl.ds(BR + 1, 1)], sems.at[2 * k + 1]
            )
        )
    for copy in copies:
        copy.start()
    for copy in copies:
        copy.wait()

    def column(frame, at):
        lo = at // BC * BC
        slab = frame[:, lo : lo + BC].astype(F32)
        col[0:rows] = slab[:, at - lo, :]
        return col[...].astype(BF16).reshape(-1, BC, CH)

    def send(main, extra, one):
        m_o[0:rows] = g1[:, main : main + BC]
        m_o[rows : rows + col.shape[0] // BC] = column(g1, extra)
        m_o[rows + col.shape[0] // BC :] = column(g2, one)

    @pl.when(lon_odd)
    def _():
        send(cols - BC, cols - BC - 1, cols - 1)

    @pl.when(jnp.logical_not(lon_odd))
    def _():
        send(0, BC, 0)


def pack_kernel(rows, cols, f1, f2, ra, rb, m_c, m_in, ends, ext1, ext2, col):
    lat_odd = lax.axis_index("lat") % 2 == 1
    lon_odd = lax.axis_index("lon") % 2 == 1
    n2 = rows + 2 * BR + 2
    n1 = rows + 2
    nh = BR + 1
    slots2 = -(-n2 // BC)
    slots1 = -(-n1 // BC)

    def halo(north, south):
        ext2[0:nh] = north[0:nh]
        ext2[nh : nh + rows] = f2[...]
        ext2[nh + rows : n2] = south[0:nh]
        ext1[0] = north[nh]
        ext1[1 : 1 + rows] = f1[...]
        ext1[1 + rows] = south[nh]

    @pl.when(lat_odd)
    def _():
        halo(rb, ra)

    @pl.when(jnp.logical_not(lat_odd))
    def _():
        halo(ra, rb)

    def column(frame, lo, hi, at):
        base = at // BC * BC
        return frame[lo:hi, base : base + BC].astype(F32)[:, at - base, :]

    ends[0, 0:n1] = column(ext1, 0, n1, 0)
    ends[1, 0:n1] = column(ext1, 0, n1, cols - 1)

    def edge(msg, main, extra, one):
        msg[0:n1] = ext1[0:n1, main : main + BC]
        col[0:n1] = column(ext1, 0, n1, extra)
        msg[n1 : n1 + slots1] = col[0 : slots1 * BC].astype(BF16).reshape(slots1, BC, CH)
        col[0:n2] = column(ext2, 0, n2, one)
        msg[n1 + slots1 :] = col[0 : slots2 * BC].astype(BF16).reshape(slots2, BC, CH)

    def corner(msg, main, extra, one):
        msg[0] = ext1[0, main : main + BC]
        msg[1] = ext1[n1 - 1, main : main + BC]
        col[0:nh] = column(ext2, 0, nh, one)
        col[nh : 2 * nh] = column(ext2, n2 - nh, n2, one)
        col[2 * nh : 2 * nh + 1] = column(ext1, 0, 1, extra)
        col[2 * nh + 1 : 2 * nh + 2] = column(ext1, n1 - 1, n1, extra)
        msg[2:] = col[0 : 2 * BC].astype(BF16).reshape(2, BC, CH)

    right = (cols - BC, cols - BC - 1, cols - 1)
    left = (0, BC, 0)

    @pl.when(lon_odd)
    def _():
        corner(m_c, *right)
        edge(m_in, *left)

    @pl.when(jnp.logical_not(lon_odd))
    def _():
        corner(m_c, *left)
        edge(m_in, *right)


def conv(x, w, row, count, width):
    lhs = jnp.concatenate(
        [
            x[b, row + a : row + a + count].reshape(count * width, CH)
            for a in range(3)
            for b in range(3)
        ],
        axis=1,
    )
    return jnp.dot(lhs, w[...], preferred_element_type=F32)


def own_kernel(rows, cols, f1, f2, ra, rb, w, e2, e1, ends2, ends1, s2, s1, x2, x1):
    lat_odd = lax.axis_index("lat") % 2 == 1
    n2 = rows + 2 * BR + 2
    n1 = rows + 2

    def put_rows(north, south):
        s2[0 : BR + 1, BR : BR + cols] = north[0 : BR + 1].astype(F32)
        s2[BR + 1 + rows :, BR : BR + cols] = south[0 : BR + 1].astype(F32)
        s1[0, BR : BR + cols] = north[BR + 1].astype(F32)
        s1[n1 - 1, BR : BR + cols] = south[BR + 1].astype(F32)

    s2[BR + 1 : BR + 1 + rows, BR : BR + cols] = f2[...].astype(F32)
    s1[1 : 1 + rows, BR : BR + cols] = f1[...].astype(F32)

    @pl.when(lat_odd)
    def _():
        put_rows(rb, ra)

    @pl.when(jnp.logical_not(lat_odd))
    def _():
        put_rows(ra, rb)

    for s in (s2, s1):
        s[:, 0:BR] = jnp.zeros((s.shape[0], BR, CH), F32)
        s[:, BR + cols :] = jnp.zeros((s.shape[0], BR, CH), F32)
    for b in range(3):
        x2[b] = s2[:, BR - 1 + b : BR - 1 + b + cols].astype(BF16)
        x1[b] = s1[:, BR - 1 + b : BR - 1 + b + cols].astype(BF16)

    def run(x, out, ends, total):
        step = 2 * BR
        for r in range(0, total, step):
            acc = conv(x, w, r, step, cols).reshape(step, cols, CH)
            out[r : r + step] = acc.astype(BF16)
            ends[0, r : r + step] = acc[:, 0, :]
            ends[1, r : r + step] = acc[:, cols - 1, :]

    run(x1, e1, ends1, rows)
    run(x2, e2, ends2, rows + 2 * BR)


def finish_side(rows, cols, side, w, o2, o1, ends2, ends1, edges, ext, xs, rim, put):
    n1 = rows + 2
    tall = rows + 2 * BR
    place = lax.broadcasted_iota(jnp.int32, (1, BC, CH), 1)
    at = BR - 1 if side else BR + BC
    ext[:, at : at + 1] = edges[side, 0:n1][:, None, :]
    for b in range(3):
        xs[b] = ext[:, BR - 1 + b : BR - 1 + b + BC].astype(BF16)
    strip = conv(xs, w, 0, rows, BC).astype(BF16).reshape(rows, BC, CH)
    near = ext[:, BR : BR + 1] if side else ext[:, BR + BC - 1 : BR + BC]
    near = near[:, 0, :].astype(BF16)
    taps = jnp.concatenate(
        [w[(3 * a + 2 * side) * CH : (3 * a + 2 * side + 1) * CH] for a in range(3)], axis=0
    )
    lhs = jnp.concatenate(
        [jnp.concatenate([rim[a : a + tall], near[a : a + rows]], axis=0) for a in range(3)],
        axis=1,
    )
    more = jnp.dot(lhs, taps, preferred_element_type=F32)
    hit = place == (BC - 1 if side else 0)
    lo = cols - BC if side else 0
    full = ends2[side] + more[0:tall]
    two = jnp.where(hit, full[:, None, :], o2[:, lo : lo + BC].astype(F32)).astype(BF16)
    full = ends1[side] + more[tall : tall + rows]
    first = jnp.where(hit, full[:, None, :], o1[:, lo : lo + BC].astype(F32)).astype(BF16)
    put(side, strip, two, first)


def strip_kernel(rows, cols, o2, o1, ends2, ends1, edges, chip, w, strip, two, first, ext, xs):
    lon_odd = lax.axis_index("lon") % 2 == 1
    c_in = chip.at[1 - lax.axis_index("lon") % 2]
    n2 = rows + 2 * BR + 2
    n1 = rows + 2
    slots2 = -(-n2 // BC)
    slots1 = -(-n1 // BC)

    def put(side, *values):
        for ref, value in zip((strip, two, first), values):
            ref[...] = value

    def run(side):
        ext[:, BR : BR + BC] = c_in[0:n1].astype(F32)
        extra = c_in[n1 : n1 + slots1].astype(F32).reshape(slots1 * BC, CH)
        at = BR + BC if side else BR - 1
        ext[:, at : at + 1] = extra[0:n1][:, None, :]
        rim = c_in[n1 + slots1 :].astype(F32).reshape(slots2 * BC, CH)[0:n2].astype(BF16)
        finish_side(rows, cols, side, w, o2, o1, ends2, ends1, edges, ext, xs, rim, put)

    @pl.when(lon_odd)
    def _():
        run(0)

    @pl.when(jnp.logical_not(lon_odd))
    def _():
        run(1)


def score_kernel(
    rows, cols, o2, o1, ends2, ends1, edges, strip_in, two_in, first_in, c_o, c_c, w,
    sums, enc_one, ext, xs, col, e2, beside,
):
    lat = lax.axis_index("lat")
    lon_odd = lax.axis_index("lon") % 2 == 1
    n2 = rows + 2 * BR + 2
    n1 = rows + 2
    nh = BR + 1
    pads = (c_o.shape[0] - rows) // 2

    def put(side, strip, two, first):
        lo = cols - BC if side else 0
        e2[:, lo : lo + BC] = two
        enc_one[:, lo : lo + BC] = first
        lo = 0 if side else cols - BC
        beside[:, lo : lo + BC] = strip

    def run(side):
        put(1 - side, strip_in[...], two_in[...], first_in[...])
        far = c_c[2:].astype(F32).reshape(2 * BC, CH)
        mine = c_o[rows : rows + pads].astype(F32).reshape(pads * BC, CH)
        at = BR + BC if side else BR - 1
        ext[0, BR : BR + BC] = c_c[0].astype(F32)
        ext[1 : 1 + rows, BR : BR + BC] = c_o[0:rows].astype(F32)
        ext[1 + rows, BR : BR + BC] = c_c[1].astype(F32)
        ext[0:1, at : at + 1] = far[2 * nh : 2 * nh + 1][:, None, :]
        ext[1 : 1 + rows, at : at + 1] = mine[0:rows][:, None, :]
        ext[1 + rows : n1, at : at + 1] = far[2 * nh + 1 : 2 * nh + 2][:, None, :]
        mine = c_o[rows + pads :].astype(F32).reshape(pads * BC, CH)
        col[0:nh] = far[0:nh]
        col[nh : nh + rows] = mine[0:rows]
        col[nh + rows : n2] = far[nh : 2 * nh]
        rim = col[0:n2].astype(BF16)
        finish_side(rows, cols, side, w, o2, o1, ends2, ends1, edges, ext, xs, rim, put)

    @pl.when(lon_odd)
    def _():
        run(1)

    @pl.when(jnp.logical_not(lon_odd))
    def _():
        run(0)

    bands = rows // BR
    queries = BR * cols
    shape = (BR, queries)
    sub = lax.broadcasted_iota(jnp.int32, shape, 0).astype(F32)
    of_right = lax.broadcasted_iota(jnp.int32, shape, 1) % cols < BC
    base = jnp.where(of_right, float(BC - cols), float(cols))
    last = lax.axis_size("lat") - 1
    scale = 1.0 / math.sqrt(CH)
    for g in range(bands):
        band = slice(g * BR, g * BR + BR)
        query = [
            (r[band].reshape(queries, CH).astype(F32) * scale).astype(BF16)
            for r in (enc_one, beside)
        ]
        acc = None
        for kb in range(3):
            keys = e2[(g + kb) * BR : (g + kb + 1) * BR].reshape(queries, CH)
            mine, other = (
                lax.dot_general(
                    keys, q, (((1,), (1,)), ((), ())), preferred_element_type=F32
                ).reshape(BR, cols // BR, BR, queries)
                for q in query
            )
            part = None
            for kr in range(BR):
                own = [jnp.exp(mine[kr, i]) for i in range(4)]
                ext_e = [
                    jnp.exp(jnp.where(of_right, other[kr, 2 + i], other[kr, i])) for i in range(2)
                ]
                row = float((kb - 1) * BR + kr)
                now = own + [row * ((own[0] + own[1]) + (own[2] + own[3]))]
                now += ext_e + [row * (ext_e[0] + ext_e[1])]
                part = now if part is None else [p + e for p, e in zip(part, now)]
            if kb == 0 and g == 0:
                part = [jnp.where(lat > 0, p, 0.0) for p in part]
            elif kb == 2 and g == bands - 1:
                part = [jnp.where(lat < last, p, 0.0) for p in part]
            acc = part if acc is None else [s + p for s, p in zip(acc, part)]
        mass = (acc[0] + acc[1]) + (acc[2] + acc[3])
        mass_b = acc[5] + acc[6]
        values = [
            mass,
            acc[4],
            (acc[1] + 2.0 * acc[2] + 3.0 * acc[3]) * 8.0 + mass * sub,
            mass_b,
            acc[7],
            acc[6] * 8.0 + mass_b * (sub + base),
        ]
        values = [jnp.sum(v, axis=0, keepdims=True) for v in values]
        values += [jnp.zeros((2, queries), F32)]
        sums[:, g * queries : (g + 1) * queries] = jnp.concatenate(values, axis=0)


def combine_kernel(rows, cols, mine, far, chip, _, fields):
    lon_odd = lax.axis_index("lon") % 2
    cells = rows * cols
    lane = lax.broadcasted_iota(jnp.int32, (1, cells), 1)
    column = lane % cols
    row = (lane // cols % BR).astype(F32)
    partner = chip[1 - lon_odd]
    is_odd = jnp.broadcast_to(lon_odd == 1, partner.shape)
    left = jnp.where(is_odd, partner, far[...])
    right = jnp.where(is_odd, far[...], partner)
    own = mine[...]

    def flow(total):
        return jnp.concatenate(
            [total[1:2] / total[0:1] - row, total[2:3] / total[0:1] - column.astype(F32)], axis=0
        ) * float(UP)

    mid = flow(own[0:3] + jnp.where(column < BC, left[3:6], right[3:6]))
    west = flow(left[0:3] + own[3:6])
    east = flow(right[0:3] + own[3:6])
    fields[0:2] = jnp.where(
        column == 0, pltpu.roll(west, cells - (cols - 1), 1), pltpu.roll(mid, 1, 1)
    )
    fields[2:4] = mid
    fields[4:6] = jnp.where(
        column == cols - 1, pltpu.roll(east, cols - 1, 1), pltpu.roll(mid, cells - 1, 1)
    )
    fields[6:8] = jnp.zeros((2, cells), F32)


def mix_kernel(cells, enc_one, wt, mix):
    feats = enc_one[...].reshape(cells, CH)
    step = 256
    for c0 in range(0, cells, step):
        for k in range(UP):
            wk = jnp.concatenate(
                [wt[n * 64 + k * UP : n * 64 + k * UP + UP] for n in range(9)], axis=0
            )
            logits = lax.dot_general(
                wk, feats[c0 : c0 + step], (((1,), (1,)), ((), ())), preferred_element_type=F32
            )
            expo = jnp.exp(logits).reshape(9, UP, step)
            total = jnp.sum(expo, axis=0)
            mix[:, k, :, c0 : c0 + step] = expo / total[None]


def lane_order(cols):
    src = lax.broadcasted_iota(jnp.int32, (UP * cols, UP * cols), 0)
    dst = lax.broadcasted_iota(jnp.int32, (UP * cols, UP * cols), 1)
    return jnp.where((dst // UP == src % cols) & (dst % UP == src // cols), 1.0, 0.0).astype(BF16)


def reorder(value, order):
    high = value.astype(BF16)
    low = (value - high.astype(F32)).astype(BF16)
    return jnp.dot(high, order, preferred_element_type=F32) + jnp.dot(
        low, order, preferred_element_type=F32
    )


def up_kernel(rows, cols, mix, fields, out, rim):
    cells = rows * cols
    lane = lax.broadcasted_iota(jnp.int32, (1, cells), 1)
    field = fields[...]
    north = jnp.where(lane < cols, 0.0, pltpu.roll(field, cols, 1))
    south = jnp.where(lane >= cells - cols, 0.0, pltpu.roll(field, cells - cols, 1))
    shifted = [(v, 2 * b) for v in (north, field, south) for b in range(3)]
    order = lane_order(cols)
    tile = 128
    group = tile // cols
    lane = lax.broadcasted_iota(jnp.int32, (UP, tile), 1)
    bits = []
    span = 1
    while span < group:
        bits.append((span, (lane // (span * cols)) % 2 == 1))
        span *= 2
    for d in range(2):
        lanes_of = [[None] * (UP // group) for _ in range(rows)]
        for t in range(cells // tile):
            flows = [
                jnp.broadcast_to(v[k + d : k + d + 1, t * tile : (t + 1) * tile], (UP, tile))
                for v, k in shifted
            ]
            for u in range(UP // group):
                block = []
                for k in range(group):
                    acc = None
                    for n in range(9):
                        term = mix[n, u * group + k, :, t * tile : (t + 1) * tile] * flows[n]
                        acc = term if acc is None else acc + term
                    block.append(acc)
                for span, high in bits:
                    shift = span * cols
                    done = list(block)
                    for k in range(group):
                        if k & span:
                            continue
                        lo_v, hi_v = block[k], block[k | span]
                        done[k] = jnp.where(high, pltpu.roll(hi_v, shift, 1), lo_v)
                        done[k | span] = jnp.where(
                            high, hi_v, pltpu.roll(lo_v, tile - shift, 1)
                        )
                    block = done
                for k in range(group):
                    lanes_of[t * group + k][u] = block[k]
        value = jnp.concatenate([jnp.concatenate(v, axis=1) for v in lanes_of], axis=0)
        value = reorder(value, order)
        out[d] = value
        rim[2 * d] = value[0:UP]
        rim[2 * d + 1] = value[(rows - 1) * UP :]


def rim_kernel(rows, cols, mix, flow_a, flow_b, rim, _, out, done, sems):
    lat_odd = lax.axis_index("lat") % 2 == 1
    cells = rows * cols
    tile = 128
    group = tile // cols
    lane = lax.broadcasted_iota(jnp.int32, (UP, tile), 1) // cols
    a, b = flow_a[...], flow_b[...]
    odd = jnp.broadcast_to(lat_odd, a.shape)
    north = jnp.where(odd, b, a)[:, cells - tile :]
    south = jnp.where(odd, a, b)[:, 0:tile]
    north = pltpu.roll(north, cols, 1)
    south = pltpu.roll(south, tile - cols, 1)
    pieces = []
    for d in range(2):
        for field, first, at, slot in (
            (north, 0, 0, 0),
            (south, 6, cells - tile, group - 1),
        ):
            flows = [
                jnp.broadcast_to(field[2 * k + d : 2 * k + d + 1], (UP, tile)) for k in range(3)
            ]
            halves = []
            for u in range(UP // group):
                whole = None
                for k in range(group):
                    acc = None
                    for n in range(3):
                        term = mix[first + n, u * group + k, :, at : at + tile] * flows[n]
                        acc = term if acc is None else acc + term
                    moved = acc if k == slot else pltpu.roll(acc, (k - slot) * cols % tile, 1)
                    whole = moved if whole is None else jnp.where(lane == k, moved, whole)
                halves.append(whole)
            pieces.append(jnp.concatenate(halves, axis=1))
    value = reorder(jnp.concatenate(pieces, axis=0), lane_order(cols))
    copies = []
    for k in range(4):
        done[k] = rim[k] + value[k * UP : (k + 1) * UP]
        copies.append(
            pltpu.make_async_copy(
                done.at[k],
                out.at[k // 2, pl.ds((k % 2) * (rows - 1) * UP, UP)],
                sems.at[k],
            )
        )
    for copy in copies:
        copy.start()
    for copy in copies:
        copy.wait()


def body(frame_one, frame_two, enc_weight, mask_weight):
    rows, cols = frame_one.shape[0], frame_one.shape[1]
    cells = rows * cols
    n2, n1 = rows + 2 * BR + 2, rows + 2
    slots = n1 + -(-n2 // BC) + -(-n1 // BC)
    own_slots = rows + 2 * -(-rows // BC)
    lats, lons = lax.axis_size("lat"), lax.axis_size("lon")
    far_lat = pair_perm(lats, 1, False)
    near_lat = pair_perm(lats, 0, False)
    far_lon = pair_perm(lons, 1, True)
    chips = [[i, i + 1] for i in range(0, lons, 2)]

    edge_rows = jax.ShapeDtypeStruct((BR + 2, cols, CH), BF16)
    tile = jax.ShapeDtypeStruct((rows, cols, CH), BF16)
    m_a, m_b, m_o, one, two = pl.pallas_call(
        functools.partial(edge_kernel, rows, cols),
        out_shape=(edge_rows, edge_rows, jax.ShapeDtypeStruct((own_slots, BC, CH), BF16), tile, tile),
        in_specs=[pl.BlockSpec(memory_space=pltpu.MemorySpace.HBM)] * 2,
        out_specs=(VMEM,) * 5,
        scratch_shapes=[
            pltpu.VMEM((-(-rows // BC) * BC, CH), F32),
            pltpu.SemaphoreType.DMA((6,)),
        ],
        compiler_params=params(8),
        name="edges",
    )(
        pltpu.with_memory_space_constraint(frame_one, pltpu.MemorySpace.HBM),
        pltpu.with_memory_space_constraint(frame_two, pltpu.MemorySpace.HBM),
    )
    row_a = lax.ppermute(m_a, "lat", far_lat)
    row_b = lax.ppermute(m_b, "lat", near_lat)
    col_o = lax.ppermute(m_o, "lon", far_lon)

    n2_pad = -(-n2 // BC) * BC
    m_c, m_in, edges = pl.pallas_call(
        functools.partial(pack_kernel, rows, cols),
        out_shape=(
            jax.ShapeDtypeStruct((4, BC, CH), BF16),
            jax.ShapeDtypeStruct((slots, BC, CH), BF16),
            jax.ShapeDtypeStruct((2, -(-n1 // BR) * BR, CH), F32),
        ),
        in_specs=[VMEM] * 4,
        out_specs=(VMEM,) * 3,
        scratch_shapes=[
            pltpu.VMEM((n1, cols, CH), BF16),
            pltpu.VMEM((n2, cols, CH), BF16),
            pltpu.VMEM((n2_pad, CH), F32),
        ],
        compiler_params=params(16),
        name="pack",
    )(one, two, row_a, row_b)
    col_c = lax.ppermute(m_c, "lon", far_lon)
    col_in = lax.all_gather(m_in, "lon", axis_index_groups=chips)

    tall = rows + 2 * BR
    weight = enc_weight.reshape(9 * CH, CH)
    own_two, own_one, ends_two, ends_one = pl.pallas_call(
        functools.partial(own_kernel, rows, cols),
        out_shape=(
            jax.ShapeDtypeStruct((tall, cols, CH), BF16),
            jax.ShapeDtypeStruct((rows, cols, CH), BF16),
            jax.ShapeDtypeStruct((2, tall, CH), F32),
            jax.ShapeDtypeStruct((2, rows, CH), F32),
        ),
        in_specs=[VMEM] * 5,
        out_specs=(VMEM,) * 4,
        scratch_shapes=[
            pltpu.VMEM((n2, cols + 2 * BR, CH), F32),
            pltpu.VMEM((n1, cols + 2 * BR, CH), F32),
            pltpu.VMEM((3, n2, cols, CH), BF16),
            pltpu.VMEM((3, n1, cols, CH), BF16),
        ],
        compiler_params=params(20),
        cost_estimate=pl.CostEstimate(
            flops=2 * 9 * CH * CH * cols * (tall + rows), bytes_accessed=4 << 20, transcendentals=0
        ),
        name="encode_own",
    )(one, two, row_a, row_b, weight)

    queries = jax.ShapeDtypeStruct((rows, BC, CH), BF16)
    side_scratch = [
        pltpu.VMEM((n1, BC + 2 * BR, CH), F32),
        pltpu.VMEM((3, n1, BC, CH), BF16),
    ]
    strip_in, two_in, first_in = pl.pallas_call(
        functools.partial(strip_kernel, rows, cols),
        out_shape=(queries, jax.ShapeDtypeStruct((tall, BC, CH), BF16), queries),
        in_specs=[VMEM] * 7,
        out_specs=(VMEM,) * 3,
        scratch_shapes=side_scratch,
        compiler_params=params(16),
        cost_estimate=pl.CostEstimate(
            flops=2 * 9 * CH * CH * BC * tall, bytes_accessed=4 << 20, transcendentals=0
        ),
        name="strip",
    )(own_two, own_one, ends_two, ends_one, edges, col_in, weight)

    lanes = jax.ShapeDtypeStruct((8, cells), F32)
    sums, enc_one = pl.pallas_call(
        functools.partial(score_kernel, rows, cols),
        out_shape=(lanes, tile),
        in_specs=[VMEM] * 11,
        out_specs=(VMEM, VMEM),
        scratch_shapes=side_scratch
        + [
            pltpu.VMEM((n2_pad, CH), F32),
            pltpu.VMEM((tall, cols, CH), BF16),
            pltpu.VMEM((rows, cols, CH), BF16),
        ],
        compiler_params=params(20),
        name="score",
    )(
        own_two, own_one, ends_two, ends_one, edges, strip_in, two_in, first_in, col_o, col_c, weight
    )
    sums_far = lax.ppermute(sums, "lon", far_lon)
    sums_in = lax.all_gather(sums, "lon", axis_index_groups=chips)

    wt = mask_weight.reshape(CH, 9, UP, UP).transpose(1, 3, 2, 0).reshape(9 * UP * UP, CH)
    mix = pl.pallas_call(
        functools.partial(mix_kernel, cells),
        out_shape=jax.ShapeDtypeStruct((9, UP, UP, cells), F32),
        in_specs=[VMEM] * 2,
        out_specs=VMEM,
        compiler_params=params(16),
        cost_estimate=pl.CostEstimate(
            flops=2 * 576 * CH * cells, bytes_accessed=4 * 576 * cells, transcendentals=576 * cells
        ),
        name="mix",
    )(enc_one, wt)

    fields = pl.pallas_call(
        functools.partial(combine_kernel, rows, cols),
        out_shape=lanes,
        in_specs=[VMEM] * 3 + [pl.BlockSpec(memory_space=pl.ANY)],
        out_specs=VMEM,
        compiler_params=params(8),
        name="combine",
    )(sums, sums_far, sums_in, mix)
    flow_a = lax.ppermute(fields, "lat", far_lat)
    flow_b = lax.ppermute(fields, "lat", near_lat)

    fine = jax.ShapeDtypeStruct((2, rows * UP, cols * UP), F32)
    whole, rim = pl.pallas_call(
        functools.partial(up_kernel, rows, cols),
        out_shape=(fine, jax.ShapeDtypeStruct((4, UP, cols * UP), F32)),
        in_specs=[VMEM] * 2,
        out_specs=(VMEM, VMEM),
        compiler_params=params(16),
        cost_estimate=pl.CostEstimate(
            flops=2 * 576 * CH * cells, bytes_accessed=4 * 576 * cells, transcendentals=0
        ),
        name="upsample",
    )(mix, fields)
    return pl.pallas_call(
        functools.partial(rim_kernel, rows, cols),
        out_shape=fine,
        in_specs=[VMEM] * 4 + [pl.BlockSpec(memory_space=pl.ANY)],
        out_specs=pl.BlockSpec(memory_space=pl.ANY),
        scratch_shapes=[
            pltpu.VMEM((4, UP, cols * UP), F32),
            pltpu.SemaphoreType.DMA((4,)),
        ],
        input_output_aliases={4: 0},
        compiler_params=params(8),
        name="rim",
    )(mix, flow_a, flow_b, rim, whole)


def solution(mesh):
    in_specs = (P("lat", "lon", None), P("lat", "lon", None), P(), P())
    return jax.shard_map(
        body, mesh=mesh, in_specs=in_specs, out_specs=P(None, "lat", "lon"), check_vma=False
    )
```

time: 62.5 us -> 61.1 us (0.978)
  starting transfers between devices: 41.9 us -> 40.5 us
  local copies, waits for them, and re-layouts: 0.07 us -> 1.03 us
    ppermute x1, starting transfers between devices: 6.24 us -> 5.22 us  [body(): col_c = lax.ppermute(m_c, 'lon', far_lon)]
    reshape x1, local copies, waits for them, and re-layouts: 0.06 us -> 1.02 us  [body(): mask_weight.reshape(CH, 9, UP, UP).transpose(1, 3, 2, 0)]
    ppermute x3, waiting for transfers between devices: 6.13 us -> 5.4 us  [the longest x1 2.95 us: body(): sums_far = lax.ppermute(sums, 'lon', far_lon)]
    pallas_call x3 -> x5, Pallas kernels: 4.32 us -> 4.23 us  [the longest x1 1.3 us: body(): pl.pallas_call(functools.partial(score_kernel, rows, cols), out_shape=(la...]
  transfers between devices with their start and end apart: 7 -> 7, of which waited for: 3 -> 3; matrix products, arithmetic and copies ran while one was open for 0% -> 2% of each run, Pallas kernels for 7% -> 8%
where the time goes in v3:
time: 61.1 us; the launch traced here: 60.8 us
  starting transfers between devices  40.5 us (66%)
  Pallas kernels  8.67 us (14%)
  waiting for transfers between devices  6.56 us (11%)
  blocking collectives  3.91 us (6%)
  local copies, waits for them, and re-layouts  1.03 us (2%)
    ppermute x1, starting transfers between devices, body(): col_o = lax.ppermute(m_o, 'lon', far_lon)  10.3 us
    ppermute x1, starting transfers between devices, body(): row_a = lax.ppermute(m_a, 'lat', far_lat)  8.16 us
    ppermute x1, starting transfers between devices, body(): flow_a = lax.ppermute(fields, 'lat', far_lat)  7.5 us
    ppermute x1, starting transfers between devices, body(): sums_far = lax.ppermute(sums, 'lon', far_lon)  5.46 us
    ppermute x1, starting transfers between devices, body(): col_c = lax.ppermute(m_c, 'lon', far_lon)  5.22 us
    ppermute x1, waiting for transfers between devices, body(): sums_far = lax.ppermute(sums, 'lon', far_lon)  2.95 us
    ppermute x1, waiting for transfers between devices, body(): flow_b = lax.ppermute(fields, 'lat', near_lat)  2.44 us
    pallas_call x1, Pallas kernels, body(): pl.pallas_call(functools.partial(own_kernel, rows, cols), out_shape=(jax....  2.15 us
  transfers between devices with their start and end apart: 7, of which 3 were waited for; matrix products, arithmetic and copies ran while one was open for 2% of the time, Pallas kernels for 8%

profile of v3, /device:TPU:6, one launch (start us, length us, event | category | flops | bytes accessed | tf_op | source)
XLA Modules:
  0.0 60.8 jit_solution(10017075763671876937)
XLA Ops:
  0.0 0.0 copy-start
  0.0 1.3 %edges.1 = (bf16[10,32,256]{2,1,0:T(8,128)(2,1)S(1)}, bf16[10,32,256]{2,1,0:T(8,128)(2,1)S(1)}, bf16[18,16,256]{2,1,0:T(8,128)(2,1)S(1)}, bf16[16,32,256]{2,1,0:T(8,128)(2,1)S(1)}, bf16[16,32,256]{2,1,0:T(8,128)(2,1)S(1)}) custom-call(bf16[16,32,256]{2,1,0:T(8,128)(2,1)} %f1.1, bf16[16,32,256]{2,1,0:T(8,128)(2,1)} %f2.1), custom_call_target="tpu_custom_call" | custom-call | tf_op jit(solution)/shard_map/edges/pallas_call | solution.py:524
  1.3 8.2 %collective-permute-start = (bf16[10,32,256]{2,1,0:T(8,128)(2,1)S(1)}, bf16[10,32,256]{2,1,0:T(8,128)(2,1)S(1)}, u32[]{:S(2)}, u32[]{:S(2)}) collective-permute-start(bf16[10,32,256]{2,1,0:T(8,128)(2,1)S(1)} %get-tuple-element.26), channel_id=1, source_target_pairs={{32,64},{64,32},{96,128},{128,96},{160,192},{192,160},{224,256},{2... | collective-permute-start | bytes 491528 | tf_op jit(solution)/shard_map/ppermute | solution.py:539
  9.5 1.9 %collective-permute-start.1 = (bf16[10,32,256]{2,1,0:T(8,128)(2,1)S(1)}, bf16[10,32,256]{2,1,0:T(8,128)(2,1)S(1)}, u32[]{:S(2)}, u32[]{:S(2)}) collective-permute-start(bf16[10,32,256]{2,1,0:T(8,128)(2,1)S(1)} %get-tuple-element.27), channel_id=1, source_target_pairs={{0,32},{32,0},{64,96},{96,64},{128,160},{160,128},{192,224},{224,1... | collective-permute-start | bytes 491528 | tf_op jit(solution)/shard_map/ppermute | solution.py:540
  11.4 10.3 %collective-permute-start.2 = (bf16[18,16,256]{2,1,0:T(8,128)(2,1)S(1)}, bf16[18,16,256]{2,1,0:T(8,128)(2,1)S(1)}, u32[]{:S(2)}, u32[]{:S(2)}) collective-permute-start(bf16[18,16,256]{2,1,0:T(8,128)(2,1)S(1)} %get-tuple-element.37), channel_id=1, source_target_pairs={{1,2},{2,1},{3,4},{4,3},{5,6},{6,5},{7,8},{8,7},{9,10},{10,9},{11,... | collective-permute-start | bytes 442376 | tf_op jit(solution)/shard_map/ppermute | solution.py:541
  21.7 1.0 %copy.7 = bf16[256,9,8,8]{0,2,3,1:T(8,128)(2,1)S(1)} copy(bf16[256,9,8,8]{0,3,2,1:T(8,128)(2,1)} %bitcast.13) | data formatting | bytes 589824 | tf_op jit(solution)/shard_map/reshape | solution.py:627
  22.7 0.0 collective-permute-done.ra
  22.8 0.0 collective-permute-done.1.rb
  22.8 0.2 pack.1
  22.9 5.2 %collective-permute-start.3 = (bf16[4,16,256]{2,1,0:T(8,128)(2,1)S(1)}, bf16[4,16,256]{2,1,0:T(8,128)(2,1)S(1)}, u32[]{:S(2)}, u32[]{:S(2)}) collective-permute-start(bf16[4,16,256]{2,1,0:T(8,128)(2,1)S(1)} %get-tuple-element.38), channel_id=1, source_target_pairs={{1,2},{2,1},{3,4},{4,3},{5,6},{6,5},{7,8},{8,7},{9,10},{10,9},{11,... | collective-permute-start | bytes 98312 | tf_op jit(solution)/shard_map/ppermute | solution.py:561
  28.1 0.0 copy-done
  28.2 2.1 %encode_own.1 = (bf16[32,32,256]{2,1,0:T(8,128)(2,1)S(1)}, bf16[16,32,256]{2,1,0:T(8,128)(2,1)S(1)}, f32[2,32,256]{2,1,0:T(8,128)S(1)}, f32[2,16,256]{2,1,0:T(8,128)S(1)}) custom-call(bf16[16,32,256]{2,1,0:T(8,128)(2,1)S(1)} %get-tuple-element.24.f1, bf16[16,32,256]{2,1,0:T(8,128)(2,1)S(1)} %get-tuple-element.25.f2, ...), custom_call_target="tpu_custom_call" | custom-call | flops 1811939328 | bytes 4194304 | tf_op jit(solution)/shard_map/encode_own/pallas_call | solution.py:566
  30.3 2.1 %all-gather = bf16[46,16,256]{2,1,0:T(8,128)(2,1)S(1)} all-gather(bf16[23,16,256]{2,1,0:T(8,128)(2,1)S(1)} %get-tuple-element.33), channel_id=2, replica_groups={{0,1},{2,3},{4,5},{6,7},{8,9},{10,11},{12,13},{14,15},{16,17},{18,19},{..., dimensions={0}, use_global_device_ids=true | all-gather | bytes 565248 | tf_op jit(solution)/shard_map/all_gather | solution.py:562
  32.4 0.6 %strip.1 = (bf16[16,16,256]{2,1,0:T(8,128)(2,1)S(1)}, bf16[32,16,256]{2,1,0:T(8,128)(2,1)S(1)}, bf16[16,16,256]{2,1,0:T(8,128)(2,1)S(1)}) custom-call(bf16[32,32,256]{2,1,0:T(8,128)(2,1)S(1)} %get-tuple-element.28.o2, bf16[16,32,256]{2,1,0:T(8,128)(2,1)S(1)} %get-tuple-element.29.o1, f32[2,32,256]{2,1,0:T(8,128)S(1)} %get-tuple-element.30.ends2, ...), custom_call_target="tpu_custom_call" | custom-call | flops 603979776 | bytes 4194304 | tf_op jit(solution)/shard_map/strip/pallas_call | solution.py:594
  33.0 0.0 collective-permute-done.2.c_o
  33.0 1.2 %collective-permute-done.3.c_c = bf16[4,16,256]{2,1,0:T(8,128)(2,1)S(1)} collective-permute-done((bf16[4,16,256]{2,1,0:T(8,128)(2,1)S(1)}, bf16[4,16,256]{2,1,0:T(8,128)(2,1)S(1)}, u32[]{:S(2)}, u32[]{:S(2)}) %collective-permute-start.3) | collective-permute-done | bytes 32800 | tf_op jit(solution)/shard_map/ppermute | solution.py:561
  34.2 1.3 %score.1 = (f32[8,512]{1,0:T(8,128)S(1)}, bf16[16,32,256]{2,1,0:T(8,128)(2,1)S(1)}) custom-call(bf16[32,32,256]{2,1,0:T(8,128)(2,1)S(1)} %get-tuple-element.28.o2, bf16[16,32,256]{2,1,0:T(8,128)(2,1)S(1)} %get-tuple-element.29.o1, f32[2,32,256]{2,1,0:T(8,128)S(1)} %get-tuple-element.30.ends2, f32[2,16,256]{2,1,0:T(8,128)S(1)} %get-tuple-element.31.ends1, ...), custom_call_target="tpu_custom_call" | custom-call | tf_op jit(solution)/shard_map/score/pallas_call | solution.py:608
  35.5 5.5 %collective-permute-start.4 = (f32[8,512]{1,0:T(8,128)S(1)}, f32[8,512]{1,0:T(8,128)S(1)}, u32[]{:S(2)}, u32[]{:S(2)}) collective-permute-start(f32[8,512]{1,0:T(8,128)S(1)} %get-tuple-element.40.mine), channel_id=1, source_target_pairs={{1,2},{2,1},{3,4},{4,3},{5,6},{6,5},{7,8},{8,7},{9,10},{10,9},{11,... | collective-permute-start | bytes 49160 | tf_op jit(solution)/shard_map/ppermute | solution.py:624
  40.9 1.8 %all-gather.1 = f32[16,512]{1,0:T(8,128)S(1)} all-gather(f32[8,512]{1,0:T(8,128)S(1)} %get-tuple-element.40.mine), channel_id=3, replica_groups={{0,1},{2,3},{4,5},{6,7},{8,9},{10,11},{12,13},{14,15},{16,17},{18,19},{..., dimensions={0}, use_global_device_ids=true | all-gather | bytes 49152 | tf_op jit(solution)/shard_map/all_gather | solution.py:625
  42.8 0.8 %mix.1._ = f32[9,8,8,512]{3,2,1,0:T(8,128)S(1)} custom-call(bf16[16,32,256]{2,1,0:T(8,128)(2,1)S(1)} %get-tuple-element.39.enc_one, bf16[576,256]{1,0:T(8,128)(2,1)S(1)} %bitcast.11), custom_call_target="tpu_custom_call" | custom-call | flops 150994944 | bytes 1179648 | tf_op jit(solution)/shard_map/mix/pallas_call | solution.py:628
  43.6 3.0 %collective-permute-done.4.far = f32[8,512]{1,0:T(8,128)S(1)} collective-permute-done((f32[8,512]{1,0:T(8,128)S(1)}, f32[8,512]{1,0:T(8,128)S(1)}, u32[]{:S(2)}, u32[]{:S(2)}) %collective-permute-start.4) | collective-permute-done | bytes 16416 | tf_op jit(solution)/shard_map/ppermute | solution.py:624
  46.6 0.1 combine.1.fields
  46.7 7.5 %collective-permute-start.5 = (f32[8,512]{1,0:T(8,128)S(1)}, f32[8,512]{1,0:T(8,128)S(1)}, u32[]{:S(2)}, u32[]{:S(2)}) collective-permute-start(f32[8,512]{1,0:T(8,128)S(1)} %combine.1.fields), channel_id=1, source_target_pairs={{32,64},{64,32},{96,128},{128,96},{160,192},{192,160},{224,256},{2... | collective-permute-start | bytes 49160 | tf_op jit(solution)/shard_map/ppermute | solution.py:648
  54.2 1.9 %collective-permute-start.6 = (f32[8,512]{1,0:T(8,128)S(1)}, f32[8,512]{1,0:T(8,128)S(1)}, u32[]{:S(2)}, u32[]{:S(2)}) collective-permute-start(f32[8,512]{1,0:T(8,128)S(1)} %combine.1.fields), channel_id=1, source_target_pairs={{0,32},{32,0},{64,96},{96,64},{128,160},{160,128},{192,224},{224,1... | collective-permute-start | bytes 49160 | tf_op jit(solution)/shard_map/ppermute | solution.py:649
  56.1 1.3 %upsample.1 = (f32[2,128,256]{2,1,0:T(8,128)}, f32[4,8,256]{2,1,0:T(8,128)S(1)}) custom-call(f32[9,8,8,512]{3,2,1,0:T(8,128)S(1)} %mix.1._, f32[8,512]{1,0:T(8,128)S(1)} %combine.1.fields), custom_call_target="tpu_custom_call" | custom-call | flops 150994944 | bytes 1179648 | tf_op jit(solution)/shard_map/upsample/pallas_call | solution.py:652
  57.4 0.0 collective-permute-done.5.flow_a
  57.4 2.4 %collective-permute-done.6.flow_b = f32[8,512]{1,0:T(8,128)S(1)} collective-permute-done((f32[8,512]{1,0:T(8,128)S(1)}, f32[8,512]{1,0:T(8,128)S(1)}, u32[]{:S(2)}, u32[]{:S(2)}) %collective-permute-start.6) | collective-permute-done | bytes 16416 | tf_op jit(solution)/shard_map/ppermute | solution.py:649
  59.8 0.9 %rim.1 = f32[2,128,256]{2,1,0:T(8,128)} custom-call(f32[9,8,8,512]{3,2,1,0:T(8,128)S(1)} %mix.1._, f32[8,512]{1,0:T(8,128)S(1)} %collective-permute-done.5.flow_a, f32[8,512]{1,0:T(8,128)S(1)} %collective-permute-done.6.flow_b, f32[4,8,256]{2,1,0:T(8,128)S(1)} %get-tuple-element.41.rim, ...), custom_call_target="tpu_custom_call", output_to_operand_aliasing={{}: (4, {})} | custom-call | tf_op jit(solution)/shard_map/rim/pallas_call | solution.py:663
Async XLA Ops:
  0.0 28.2 %copy-start = (bf16[3,3,256,256]{3,2,1,0:T(8,128)(2,1)S(1)}, bf16[3,3,256,256]{3,2,1,0:T(8,128)(2,1)}, u32[]{:S(2)}) copy-start(bf16[3,3,256,256]{3,2,1,0:T(8,128)(2,1)} %param.6) | copy-start | bytes 3538948
  1.3 21.4 %collective-permute-start = (bf16[10,32,256]{2,1,0:T(8,128)(2,1)S(1)}, bf16[10,32,256]{2,1,0:T(8,128)(2,1)S(1)}, u32[]{:S(2)}, u32[]{:S(2)}) collective-permute-start(bf16[10,32,256]{2,1,0:T(8,128)(2,1)S(1)} %get-tuple-element.26), channel_id=1, source_target_pairs={{32,64},{64,32},{96,128},{128,96},{160,192},{192,160},{224,256},{2... | collective-permute-start | bytes 491528 | tf_op jit(solution)/shard_map/ppermute | solution.py:539
  9.5 13.3 %collective-permute-start.1 = (bf16[10,32,256]{2,1,0:T(8,128)(2,1)S(1)}, bf16[10,32,256]{2,1,0:T(8,128)(2,1)S(1)}, u32[]{:S(2)}, u32[]{:S(2)}) collective-permute-start(bf16[10,32,256]{2,1,0:T(8,128)(2,1)S(1)} %get-tuple-element.27), channel_id=1, source_target_pairs={{0,32},{32,0},{64,96},{96,64},{128,160},{160,128},{192,224},{224,1... | collective-permute-start | bytes 491528 | tf_op jit(solution)/shard_map/ppermute | solution.py:540
  11.4 21.6 %collective-permute-start.2 = (bf16[18,16,256]{2,1,0:T(8,128)(2,1)S(1)}, bf16[18,16,256]{2,1,0:T(8,128)(2,1)S(1)}, u32[]{:S(2)}, u32[]{:S(2)}) collective-permute-start(bf16[18,16,256]{2,1,0:T(8,128)(2,1)S(1)} %get-tuple-element.37), channel_id=1, source_target_pairs={{1,2},{2,1},{3,4},{4,3},{5,6},{6,5},{7,8},{8,7},{9,10},{10,9},{11,... | collective-permute-start | bytes 442376 | tf_op jit(solution)/shard_map/ppermute | solution.py:541
  22.9 11.3 %collective-permute-start.3 = (bf16[4,16,256]{2,1,0:T(8,128)(2,1)S(1)}, bf16[4,16,256]{2,1,0:T(8,128)(2,1)S(1)}, u32[]{:S(2)}, u32[]{:S(2)}) collective-permute-start(bf16[4,16,256]{2,1,0:T(8,128)(2,1)S(1)} %get-tuple-element.38), channel_id=1, source_target_pairs={{1,2},{2,1},{3,4},{4,3},{5,6},{6,5},{7,8},{8,7},{9,10},{10,9},{11,... | collective-permute-start | bytes 98312 | tf_op jit(solution)/shard_map/ppermute | solution.py:561
  35.5 11.1 %collective-permute-start.4 = (f32[8,512]{1,0:T(8,128)S(1)}, f32[8,512]{1,0:T(8,128)S(1)}, u32[]{:S(2)}, u32[]{:S(2)}) collective-permute-start(f32[8,512]{1,0:T(8,128)S(1)} %get-tuple-element.40.mine), channel_id=1, source_target_pairs={{1,2},{2,1},{3,4},{4,3},{5,6},{6,5},{7,8},{8,7},{9,10},{10,9},{11,... | collective-permute-start | bytes 49160 | tf_op jit(solution)/shard_map/ppermute | solution.py:624
  46.7 10.7 %collective-permute-start.5 = (f32[8,512]{1,0:T(8,128)S(1)}, f32[8,512]{1,0:T(8,128)S(1)}, u32[]{:S(2)}, u32[]{:S(2)}) collective-permute-start(f32[8,512]{1,0:T(8,128)S(1)} %combine.1.fields), channel_id=1, source_target_pairs={{32,64},{64,32},{96,128},{128,96},{160,192},{192,160},{224,256},{2... | collective-permute-start | bytes 49160 | tf_op jit(solution)/shard_map/ppermute | solution.py:648
  54.2 5.6 %collective-permute-start.6 = (f32[8,512]{1,0:T(8,128)S(1)}, f32[8,512]{1,0:T(8,128)S(1)}, u32[]{:S(2)}, u32[]{:S(2)}) collective-permute-start(f32[8,512]{1,0:T(8,128)S(1)} %combine.1.fields), channel_id=1, source_target_pairs={{0,32},{32,0},{64,96},{96,64},{128,160},{160,128},{192,224},{224,1... | collective-permute-start | bytes 49160 | tf_op jit(solution)/shard_map/ppermute | solution.py:649

commit v4 on v1

v4 whole, which is shorter than its diff:
```python
import functools
import math

import jax
import jax.numpy as jnp
from jax import lax
from jax.experimental import pallas as pl
from jax.experimental.pallas import tpu as pltpu
from jax.sharding import PartitionSpec as P

CH = 256
BR = 8
BC = 16
UP = 8
F32 = jnp.float32
BF16 = jnp.bfloat16
VMEM = pl.BlockSpec(memory_space=pltpu.VMEM)


def params(mib):
    return pltpu.CompilerParams(vmem_limit_bytes=mib * 1024 * 1024)


def pair_perm(size, first, wrap, apart=1):
    out = []
    for i in range(size):
        if (i - first) % (2 * apart) >= apart:
            continue
        j = i + apart
        if j >= size:
            if not wrap:
                continue
            j -= size
        out += [(i, j), (j, i)]
    return out


def edge_kernel(rows, cols, f1, f2, m_a, m_b, m_c, m_d, g1, g2, sems):
    band = lax.axis_index("lat")
    odd = band % 2
    upper = band % 4 // 2
    copies = [
        pltpu.make_async_copy(f2, g2, sems.at[0]),
        pltpu.make_async_copy(f1, g1, sems.at[1]),
    ]
    for k, (msg, low) in enumerate(((m_a, odd), (m_b, 1 - odd))):
        copies.append(
            pltpu.make_async_copy(f2, msg.at[pl.ds(0, rows)], sems.at[2 + 2 * k])
        )
        copies.append(
            pltpu.make_async_copy(
                f1.at[pl.ds(low * (rows - 2), 2)], msg.at[pl.ds(rows, 2)], sems.at[3 + 2 * k]
            )
        )
    for k, (msg, low) in enumerate(((m_c, upper), (m_d, 1 - upper))):
        copies.append(
            pltpu.make_async_copy(f2.at[pl.ds(low * (rows - 1), 1)], msg, sems.at[6 + k])
        )
    for copy in copies:
        copy.start()
    for copy in copies:
        copy.wait()


def by_parity(lat_run, ra, rb, rc, rd):
    band = lax.axis_index("lat")
    for odd in (0, 1):
        for upper in (0, 1):

            @pl.when((band % 2 == odd) & (band % 4 // 2 == upper))
            def _():
                pair = (rb, ra) if odd else (ra, rb)
                lat_run(*pair, *((rd, rc) if upper else (rc, rd)))


def edge(msg, main_cols, extra, rim, col):
    n1, n2 = main_cols.shape[0], rim.shape[0]
    slots1, slots2 = -(-n1 // BC), -(-n2 // BC)
    msg[0:n1] = main_cols
    col[0:n1] = extra
    msg[n1 : n1 + slots1] = col[0 : slots1 * BC].astype(BF16).reshape(slots1, BC, CH)
    col[0:n2] = rim
    msg[n1 + slots1 :] = col[0 : slots2 * BC].astype(BF16).reshape(slots2, BC, CH)


def edge_places(cols, right):
    return (cols - BC, cols - BC - 1, cols - 1) if right else (0, BC, 0)


def pack_kernel(rows, cols, f1, f2, ra, rb, rc, rd, m_x, ext1, ext2, col):
    lon_odd = lax.axis_index("lon") % 2
    n2 = 3 * rows + 2
    n1 = rows + 4

    def halo(north, south, north_far, south_far):
        ext2[0:1] = north_far[...]
        ext2[1 : 1 + rows] = north[0:rows]
        ext2[1 + 2 * rows : 1 + 3 * rows] = south[0:rows]
        ext2[n2 - 1 : n2] = south_far[...]
        ext1[0:2] = north[rows : rows + 2]
        ext1[n1 - 2 : n1] = south[rows : rows + 2]

    ext2[1 + rows : 1 + 2 * rows] = f2[...]
    ext1[2 : 2 + rows] = f1[...]
    by_parity(halo, ra, rb, rc, rd)

    def column(frame, at):
        base = at // BC * BC
        return frame[:, base : base + BC].astype(F32)[:, at - base, :]

    for odd in (0, 1):

        @pl.when(lon_odd == odd)
        def _():
            main, extra, one = edge_places(cols, odd == 1)
            edge(m_x, ext1[:, main : main + BC], column(ext1, extra), column(ext2, one), col)


def conv(x, w, row, count, width):
    lhs = jnp.concatenate(
        [
            x[b, row + a : row + a + count].reshape(count * width, CH)
            for a in range(3)
            for b in range(3)
        ],
        axis=1,
    )
    return jnp.dot(lhs, w[...], preferred_element_type=F32)


def own_kernel(
    rows, cols, f1, f2, ra, rb, rc, rd, w, e2, e1, ends2, ends1, m_in, edges, s2, s1, x2, x1, col
):
    lon_odd = lax.axis_index("lon") % 2
    n2 = 3 * rows + 2
    n1 = rows + 4
    own = slice(BR, BR + cols)

    def halo(north, south, north_far, south_far):
        s2[0:1, own] = north_far[...].astype(F32)
        s2[1 : 1 + rows, own] = north[0:rows].astype(F32)
        s2[1 + 2 * rows : 1 + 3 * rows, own] = south[0:rows].astype(F32)
        s2[n2 - 1 : n2, own] = south_far[...].astype(F32)
        s1[0:2, own] = north[rows : rows + 2].astype(F32)
        s1[n1 - 2 : n1, own] = south[rows : rows + 2].astype(F32)

    s2[1 + rows : 1 + 2 * rows, own] = f2[...].astype(F32)
    s1[2 : 2 + rows, own] = f1[...].astype(F32)
    by_parity(halo, ra, rb, rc, rd)
    for s in (s2, s1):
        s[:, 0:BR] = jnp.zeros((s.shape[0], BR, CH), F32)
        s[:, BR + cols :] = jnp.zeros((s.shape[0], BR, CH), F32)
    for b in range(3):
        x2[b] = s2[:, BR - 1 + b : BR - 1 + b + cols].astype(BF16)
        x1[b] = s1[:, BR - 1 + b : BR - 1 + b + cols].astype(BF16)

    def run(x, out, ends, total):
        for r in range(0, total, 2 * BR):
            step = min(2 * BR, total - r)
            acc = conv(x, w, r, step, cols).reshape(step, cols, CH)
            out[r : r + step] = acc.astype(BF16)
            ends[0, r : r + step] = acc[:, 0, :]
            ends[1, r : r + step] = acc[:, cols - 1, :]

    run(x1, e1, ends1, rows + 2)
    run(x2, e2, ends2, 3 * rows)
    edges[0, 0:n1] = s1[:, BR, :]
    edges[1, 0:n1] = s1[:, BR + cols - 1, :]
    for odd in (0, 1):

        @pl.when(lon_odd == odd)
        def _():
            main, extra, one = edge_places(cols, odd == 0)
            edge(m_in, x1[1, :, main : main + BC], s1[:, BR + extra, :], s2[:, BR + one, :], col)


def finish_side(rows, cols, side, msg, w, o2, o1, ends2, ends1, edges, ext, xs, put):
    n2 = 3 * rows + 2
    n1 = rows + 4
    slots2 = -(-n2 // BC)
    slots1 = -(-n1 // BC)
    few, tall = rows + 2, 3 * rows
    extra = msg[n1 : n1 + slots1].astype(F32).reshape(slots1 * BC, CH)[0:n1]
    rim = msg[n1 + slots1 :].astype(F32).reshape(slots2 * BC, CH)[0:n2].astype(BF16)
    inner = edges[side, 0:n1]
    ext[:, BR : BR + BC] = msg[0:n1].astype(F32)
    ext[:, BR - 1 : BR] = (inner if side else extra)[:, None, :]
    ext[:, BR + BC : BR + BC + 1] = (extra if side else inner)[:, None, :]
    for b in range(3):
        xs[b] = ext[:, BR - 1 + b : BR - 1 + b + BC].astype(BF16)
    strip = conv(xs, w, 0, few, BC).astype(BF16).reshape(few, BC, CH)
    near = ext[:, BR : BR + 1] if side else ext[:, BR + BC - 1 : BR + BC]
    near = near[:, 0, :].astype(BF16)
    taps = jnp.concatenate(
        [w[(3 * a + 2 * side) * CH : (3 * a + 2 * side + 1) * CH] for a in range(3)], axis=0
    )
    lhs = jnp.concatenate(
        [jnp.concatenate([rim[a : a + tall], near[a : a + few]], axis=0) for a in range(3)],
        axis=1,
    )
    more = jnp.dot(lhs, taps, preferred_element_type=F32)
    hit = lax.broadcasted_iota(jnp.int32, (1, BC, CH), 1) == (BC - 1 if side else 0)
    lo = cols - BC if side else 0
    full = ends2[side, 0:tall] + more[0:tall]
    two = jnp.where(hit, full[:, None, :], o2[:, lo : lo + BC].astype(F32)).astype(BF16)
    full = ends1[side, 0:few] + more[tall : tall + few]
    first = jnp.where(hit, full[:, None, :], o1[:, lo : lo + BC].astype(F32)).astype(BF16)
    put(side, strip, two, first)


def strip_kernel(rows, cols, o2, o1, ends2, ends1, edges, chip, w, strip, two, first, ext, xs):
    lon_odd = lax.axis_index("lon") % 2
    msg = chip.at[1 - lon_odd]

    def put(side, *values):
        for ref, value in zip((strip, two, first), values):
            ref[...] = value

    for odd in (0, 1):

        @pl.when(lon_odd == odd)
        def _():
            finish_side(rows, cols, 1 - odd, msg, w, o2, o1, ends2, ends1, edges, ext, xs, put)


def score_kernel(
    rows, cols, o2, o1, ends2, ends1, edges, strip_in, two_in, first_in, c_x, w,
    sums, enc_one, ext, xs, e2, beside,
):
    lat = lax.axis_index("lat")
    lon_odd = lax.axis_index("lon") % 2

    def put(side, strip, two, first):
        lo = cols - BC if side else 0
        e2[:, lo : lo + BC] = two
        enc_one[:, lo : lo + BC] = first
        lo = 0 if side else cols - BC
        beside[:, lo : lo + BC] = strip

    for odd in (0, 1):

        @pl.when(lon_odd == odd)
        def _():
            put(1 - odd, strip_in[...], two_in[...], first_in[...])
            finish_side(rows, cols, odd, c_x, w, o2, o1, ends2, ends1, edges, ext, xs, put)

    bands = rows // BR
    last = lax.axis_size("lat") - 1
    scale = 1.0 / math.sqrt(CH)
    groups = cols // BR

    def features(ref, row, count):
        flat = ref[row : row + count].reshape(count * cols, CH).astype(F32)
        return (flat * scale).astype(BF16)

    def scores(block, query):
        keys = e2[block * BR : (block + 1) * BR].reshape(BR * cols, CH)
        return lax.dot_general(
            keys, query, (((1,), (1,)), ((), ())), preferred_element_type=F32
        ).reshape(BR, groups, BR, query.shape[0])

    def add(total, now):
        return now if total is None else [p + e for p, e in zip(total, now)]

    def triple(pieces, by_row, sub, base):
        mass = pieces[0]
        octs = None
        for i, piece in enumerate(pieces[1:], 1):
            mass = mass + piece
            octs = piece * float(i) if octs is None else octs + piece * float(i)
        across = octs * 8.0 + mass * (sub if base is None else sub + base)
        return [jnp.sum(v, axis=0, keepdims=True) for v in (mass, by_row, across)]

    queries = BR * cols
    sub = lax.broadcasted_iota(jnp.int32, (BR, queries), 0).astype(F32)
    of_right = lax.broadcasted_iota(jnp.int32, (BR, queries), 1) % cols < BC
    base = jnp.where(of_right, float(BC - cols), float(cols))
    for g in range(bands):
        query_own = features(enc_one, 1 + g * BR, BR)
        query_side = features(beside, 1 + g * BR, BR)
        acc = None
        for kb in range(3):
            mine = scores(g + kb + 1, query_own)
            other = scores(g + kb + 1, query_side)
            part = None
            for kr in range(BR):
                row = float((kb - 1) * BR + kr)
                own = [jnp.exp(mine[kr, i]) for i in range(4)]
                side = [
                    jnp.exp(jnp.where(of_right, other[kr, 2 + i], other[kr, i])) for i in range(2)
                ]
                now = own + [row * ((own[0] + own[1]) + (own[2] + own[3]))]
                now += side + [row * (side[0] + side[1])]
                part = add(part, now)
            if kb == 0 and g == 0:
                part = [jnp.where(lat > 0, p, 0.0) for p in part]
            elif kb == 2 and g == bands - 1:
                part = [jnp.where(lat < last, p, 0.0) for p in part]
            acc = add(acc, part)
        values = triple(acc[0:4], acc[4], sub, None) + triple(acc[5:7], acc[7], sub, base)
        values += [jnp.zeros((2, queries), F32)]
        sums[:, cols + g * queries : cols + (g + 1) * queries] = jnp.concatenate(values, axis=0)

    lanes = 2 * cols
    sub = lax.broadcasted_iota(jnp.int32, (BR, lanes), 0).astype(F32)
    lane = lax.broadcasted_iota(jnp.int32, (BR, lanes), 1)
    is_own = lane < cols
    of_right = (lane >= cols) & (lane < cols + BC)
    base = jnp.where(is_own, 0.0, jnp.where(of_right, float(BC - cols), float(cols)))
    for row_at, first, at in ((0, 0, 0), (rows + 1, bands + 1, cols + rows * cols)):
        query = jnp.concatenate([features(enc_one, row_at, 1), features(beside, row_at, 1)], axis=0)
        acc = None
        for kb in range(3):
            both = scores(first + kb, query)
            for kr in range(BR):
                row = float((kb - 1) * BR + kr)
                now = [
                    jnp.exp(jnp.where(of_right, both[kr, 2 + i], both[kr, i])) for i in range(2)
                ]
                now += [jnp.where(is_own, jnp.exp(both[kr, i]), 0.0) for i in range(2, 4)]
                now += [row * ((now[0] + now[1]) + (now[2] + now[3]))]
                acc = add(acc, now)
        values = triple(acc[0:4], acc[4], sub, base)
        sums[0:3, at : at + cols] = jnp.concatenate([v[:, 0:cols] for v in values], axis=0)
        sums[3:6, at : at + cols] = jnp.concatenate([v[:, cols:] for v in values], axis=0)
        sums[6:8, at : at + cols] = jnp.zeros((2, cols), F32)


def mix_kernel(rows, cells, enc_one, wt, mix):
    feats = enc_one[1 : 1 + rows].reshape(cells, CH)
    step = 256
    for c0 in range(0, cells, step):
        for k in range(UP):
            wk = jnp.concatenate(
                [wt[n * 64 + k * UP : n * 64 + k * UP + UP] for n in range(9)], axis=0
            )
            logits = lax.dot_general(
                wk, feats[c0 : c0 + step], (((1,), (1,)), ((), ())), preferred_element_type=F32
            )
            expo = jnp.exp(logits).reshape(9, UP, step)
            total = jnp.sum(expo, axis=0)
            mix[:, k, :, c0 : c0 + step] = expo / total[None]


def up_kernel(rows, cols, mine, far, chip, mix, out):
    lat = lax.axis_index("lat")
    last = lax.axis_size("lat") - 1
    lon_odd = lax.axis_index("lon") % 2
    cells = rows * cols
    width = mine.shape[1]
    lane = lax.broadcasted_iota(jnp.int32, (1, width), 1)
    column = lane % cols
    row = ((lane // cols + BR - 1) % BR).astype(F32)
    outside = ((lane < cols) & (lat == 0)) | ((lane >= cols + cells) & (lat == last))
    partner = chip[1 - lon_odd]
    is_odd = jnp.broadcast_to(lon_odd == 1, partner.shape)
    left = jnp.where(is_odd, partner, far[...])
    right = jnp.where(is_odd, far[...], partner)
    own = mine[...]

    def flow(total):
        both = jnp.concatenate(
            [total[1:2] / total[0:1] - row, total[2:3] / total[0:1] - column.astype(F32)], axis=0
        )
        return jnp.where(outside, 0.0, both * float(UP))

    mid = flow(own[0:3] + jnp.where(column < BC, left[3:6], right[3:6]))
    west = flow(left[0:3] + own[3:6])
    east = flow(right[0:3] + own[3:6])
    west = jnp.where(
        column == 0, pltpu.roll(west, width - (cols - 1), 1), pltpu.roll(mid, 1, 1)
    )
    east = jnp.where(
        column == cols - 1, pltpu.roll(east, cols - 1, 1), pltpu.roll(mid, width - 1, 1)
    )
    shifted = []
    for a in range(3):
        for field in (west, mid, east):
            moved = field if a == 0 else pltpu.roll(field, width - a * cols, 1)
            shifted.append(moved[:, 0:cells])
    src = lax.broadcasted_iota(jnp.int32, (UP * cols, UP * cols), 0)
    dst = lax.broadcasted_iota(jnp.int32, (UP * cols, UP * cols), 1)
    order = jnp.where((dst // UP == src % cols) & (dst % UP == src // cols), 1.0, 0.0).astype(BF16)
    tile = 128
    group = tile // cols
    lane = lax.broadcasted_iota(jnp.int32, (UP, tile), 1)
    bits = []
    span = 1
    while span < group:
        bits.append((span, (lane // (span * cols)) % 2 == 1))
        span *= 2
    for d in range(2):
        lanes_of = [[None] * (UP // group) for _ in range(rows)]
        for t in range(cells // tile):
            flows = [
                jnp.broadcast_to(v[d : d + 1, t * tile : (t + 1) * tile], (UP, tile))
                for v in shifted
            ]
            for u in range(UP // group):
                block = []
                for k in range(group):
                    acc = None
                    for n in range(9):
                        term = mix[n, u * group + k, :, t * tile : (t + 1) * tile] * flows[n]
                        acc = term if acc is None else acc + term
                    block.append(acc)
                for span, high in bits:
                    shift = span * cols
                    done = list(block)
                    for k in range(group):
                        if k & span:
                            continue
                        lo_v, hi_v = block[k], block[k | span]
                        done[k] = jnp.where(high, pltpu.roll(hi_v, shift, 1), lo_v)
                        done[k | span] = jnp.where(
                            high, hi_v, pltpu.roll(lo_v, tile - shift, 1)
                        )
                    block = done
                for k in range(group):
                    lanes_of[t * group + k][u] = block[k]
        value = jnp.concatenate([jnp.concatenate(v, axis=1) for v in lanes_of], axis=0)
        high_part = value.astype(BF16)
        low_part = (value - high_part.astype(F32)).astype(BF16)
        out[d] = jnp.dot(high_part, order, preferred_element_type=F32) + jnp.dot(
            low_part, order, preferred_element_type=F32
        )


def body(frame_one, frame_two, enc_weight, mask_weight):
    rows, cols = frame_one.shape[0], frame_one.shape[1]
    cells = rows * cols
    n2, n1, few, tall = 3 * rows + 2, rows + 4, rows + 2, 3 * rows
    n2_pad = -(-n2 // BC) * BC
    slots = n1 + n2_pad // BC + -(-n1 // BC)
    lats, lons = lax.axis_size("lat"), lax.axis_size("lon")
    far_lat = pair_perm(lats, 1, False)
    near_lat = pair_perm(lats, 0, False)
    low_lat = pair_perm(lats, 0, False, 2)
    high_lat = pair_perm(lats, 2, False, 2)
    far_lon = pair_perm(lons, 1, True)
    chips = [[i, i + 1] for i in range(0, lons, 2)]

    def array(*shape, dtype=BF16):
        return jax.ShapeDtypeStruct(shape, dtype)

    tile = array(rows, cols, CH)
    m_a, m_b, m_c, m_d, one, two = pl.pallas_call(
        functools.partial(edge_kernel, rows, cols),
        out_shape=(array(few, cols, CH),) * 2 + (array(1, cols, CH),) * 2 + (tile, tile),
        in_specs=[pl.BlockSpec(memory_space=pltpu.MemorySpace.HBM)] * 2,
        out_specs=(VMEM,) * 6,
        scratch_shapes=[pltpu.SemaphoreType.DMA((8,))],
        compiler_params=params(8),
        name="edges",
    )(
        pltpu.with_memory_space_constraint(frame_one, pltpu.MemorySpace.HBM),
        pltpu.with_memory_space_constraint(frame_two, pltpu.MemorySpace.HBM),
    )
    row_a = lax.ppermute(m_a, "lat", far_lat)
    row_b = lax.ppermute(m_b, "lat", near_lat)
    row_c = lax.ppermute(m_c, "lat", high_lat)
    row_d = lax.ppermute(m_d, "lat", low_lat)

    m_x = pl.pallas_call(
        functools.partial(pack_kernel, rows, cols),
        out_shape=array(slots, BC, CH),
        in_specs=[VMEM] * 6,
        out_specs=VMEM,
        scratch_shapes=[
            pltpu.VMEM((n1, cols, CH), BF16),
            pltpu.VMEM((n2, cols, CH), BF16),
            pltpu.VMEM((n2_pad, CH), F32),
        ],
        compiler_params=params(16),
        name="pack",
    )(one, two, row_a, row_b, row_c, row_d)
    col_x = lax.ppermute(m_x, "lon", far_lon)

    weight = enc_weight.reshape(9 * CH, CH)
    few_pad = -(-few // BR) * BR
    own_two, own_one, ends_two, ends_one, m_in, edges = pl.pallas_call(
        functools.partial(own_kernel, rows, cols),
        out_shape=(
            array(tall, cols, CH),
            array(few, cols, CH),
            array(2, tall, CH, dtype=F32),
            array(2, few_pad, CH, dtype=F32),
            array(slots, BC, CH),
            array(2, -(-n1 // BR) * BR, CH, dtype=F32),
        ),
        in_specs=[VMEM] * 7,
        out_specs=(VMEM,) * 6,
        scratch_shapes=[
            pltpu.VMEM((n2, cols + 2 * BR, CH), F32),
            pltpu.VMEM((n1, cols + 2 * BR, CH), F32),
            pltpu.VMEM((3, n2, cols, CH), BF16),
            pltpu.VMEM((3, n1, cols, CH), BF16),
            pltpu.VMEM((n2_pad, CH), F32),
        ],
        compiler_params=params(24),
        cost_estimate=pl.CostEstimate(
            flops=2 * 9 * CH * CH * cols * (tall + few), bytes_accessed=4 << 20, transcendentals=0
        ),
        name="encode_own",
    )(one, two, row_a, row_b, row_c, row_d, weight)

    col_in = lax.all_gather(m_in, "lon", axis_index_groups=chips)
    side_scratch = [
        pltpu.VMEM((n1, BC + 2 * BR, CH), F32),
        pltpu.VMEM((3, n1, BC, CH), BF16),
    ]
    strip_in, two_in, first_in = pl.pallas_call(
        functools.partial(strip_kernel, rows, cols),
        out_shape=(array(few, BC, CH), array(tall, BC, CH), array(few, BC, CH)),
        in_specs=[VMEM] * 7,
        out_specs=(VMEM,) * 3,
        scratch_shapes=side_scratch,
        compiler_params=params(16),
        cost_estimate=pl.CostEstimate(
            flops=2 * 9 * CH * CH * BC * few, bytes_accessed=4 << 20, transcendentals=0
        ),
        name="strip",
    )(own_two, own_one, ends_two, ends_one, edges, col_in, weight)

    width = -(-few * cols // 128) * 128
    sums, enc_one = pl.pallas_call(
        functools.partial(score_kernel, rows, cols),
        out_shape=(array(8, width, dtype=F32), array(few, cols, CH)),
        in_specs=[VMEM] * 10,
        out_specs=(VMEM, VMEM),
        scratch_shapes=side_scratch
        + [pltpu.VMEM((tall, cols, CH), BF16), pltpu.VMEM((few, cols, CH), BF16)],
        compiler_params=params(20),
        name="score",
    )(own_two, own_one, ends_two, ends_one, edges, strip_in, two_in, first_in, col_x, weight)
    sums_far = lax.ppermute(sums, "lon", far_lon)
    sums_in = lax.all_gather(sums, "lon", axis_index_groups=chips)

    wt = mask_weight.reshape(CH, 9, UP, UP).transpose(1, 3, 2, 0).reshape(9 * UP * UP, CH)
    mix = pl.pallas_call(
        functools.partial(mix_kernel, rows, cells),
        out_shape=array(9, UP, UP, cells, dtype=F32),
        in_specs=[VMEM] * 2,
        out_specs=VMEM,
        compiler_params=params(16),
        cost_estimate=pl.CostEstimate(
            flops=2 * 576 * CH * cells, bytes_accessed=4 * 576 * cells, transcendentals=576 * cells
        ),
        name="mix",
    )(enc_one, wt)
    return pl.pallas_call(
        functools.partial(up_kernel, rows, cols),
        out_shape=array(2, rows * UP, cols * UP, dtype=F32),
        in_specs=[VMEM] * 4,
        out_specs=VMEM,
        compiler_params=params(16),
        name="upsample",
    )(sums, sums_far, sums_in, mix)


def solution(mesh):
    in_specs = (P("lat", "lon", None), P("lat", "lon", None), P(), P())
    return jax.shard_map(
        body, mesh=mesh, in_specs=in_specs, out_specs=P(None, "lat", "lon"), check_vma=False
    )
```

time: 64.8 us -> 56.5 us (0.87)
  the two profiles are of different devices: /device:TPU:7 before, /device:TPU:1 now
where the time goes in v4:
time: 56.5 us; the launch traced here: 56.2 us
  starting transfers between devices  22.9 us (41%)
  blocking collectives  18.5 us (33%)
  Pallas kernels  9.09 us (16%)
  waiting for transfers between devices  4.52 us (8%)
  local copies, waits for them, and re-layouts  1.03 us (2%)
    all_gather x1, blocking collectives, body(): col_in = lax.all_gather(m_in, 'lon', axis_index_groups=chips)  10.5 us
    ppermute x1, starting transfers between devices, body(): row_b = lax.ppermute(m_b, 'lat', near_lat)  8.15 us
    ppermute x1, starting transfers between devices, body(): row_d = lax.ppermute(m_d, 'lat', low_lat)  7.96 us
    all_gather x1, blocking collectives, body(): sums_in = lax.all_gather(sums, 'lon', axis_index_groups=chips)  7.93 us
    ppermute x1, starting transfers between devices, body(): col_x = lax.ppermute(m_x, 'lon', far_lon)  3.58 us
    pallas_call x1, Pallas kernels, body(): pl.pallas_call(functools.partial(own_kernel, rows, cols), out_shape=(arra...  3.09 us
    ppermute x1, waiting for transfers between devices, body(): row_b = lax.ppermute(m_b, 'lat', near_lat)  2.94 us
    ppermute x1, starting transfers between devices, body(): sums_far = lax.ppermute(sums, 'lon', far_lon)  1.91 us
  transfers between devices with their start and end apart: 6, of which 2 were waited for; matrix products, arithmetic and copies ran while one was open for 2% of the time, Pallas kernels for 8%

profile of v4, /device:TPU:1, one launch (start us, length us, event | category | flops | bytes accessed | tf_op | source)
XLA Modules:
  0.0 56.2 jit_solution(15793065122584102682)
XLA Ops:
  0.0 0.0 copy-start
  0.0 1.4 %edges.1 = (bf16[18,32,256]{2,1,0:T(8,128)(2,1)S(1)}, bf16[18,32,256]{2,1,0:T(8,128)(2,1)S(1)}, bf16[1,32,256]{2,1,0:T(8,128)(2,1)S(1)}, bf16[1,32,256]{2,1,0:T(...) custom-call(bf16[16,32,256]{2,1,0:T(8,128)(2,1)} %f1.1, bf16[16,32,256]{2,1,0:T(8,128)(2,1)} %f2.1), custom_call_target="tpu_custom_call" | custom-call | tf_op jit(solution)/shard_map/edges/pallas_call | solution.py:447
  1.4 0.7 %collective-permute-start = (bf16[18,32,256]{2,1,0:T(8,128)(2,1)S(1)}, bf16[18,32,256]{2,1,0:T(8,128)(2,1)S(1)}, u32[]{:S(2)}, u32[]{:S(2)}) collective-permute-start(bf16[18,32,256]{2,1,0:T(8,128)(2,1)S(1)} %get-tuple-element.24), channel_id=1, source_target_pairs={{32,64},{64,32},{96,128},{128,96},{160,192},{192,160},{224,256},{2... | collective-permute-start | bytes 884744 | tf_op jit(solution)/shard_map/ppermute | solution.py:459
  2.1 8.2 %collective-permute-start.1 = (bf16[18,32,256]{2,1,0:T(8,128)(2,1)S(1)}, bf16[18,32,256]{2,1,0:T(8,128)(2,1)S(1)}, u32[]{:S(2)}, u32[]{:S(2)}) collective-permute-start(bf16[18,32,256]{2,1,0:T(8,128)(2,1)S(1)} %get-tuple-element.25), channel_id=1, source_target_pairs={{0,32},{32,0},{64,96},{96,64},{128,160},{160,128},{192,224},{224,1... | collective-permute-start | bytes 884744 | tf_op jit(solution)/shard_map/ppermute | solution.py:460
  10.2 0.7 %collective-permute-start.2 = (bf16[1,32,256]{2,1,0:T(8,128)(2,1)S(1)}, bf16[1,32,256]{2,1,0:T(8,128)(2,1)S(1)}, u32[]{:S(2)}, u32[]{:S(2)}) collective-permute-start(bf16[1,32,256]{2,1,0:T(8,128)(2,1)S(1)} %get-tuple-element.26), channel_id=1, source_target_pairs={{64,128},{128,64},{96,160},{160,96},{192,256},{256,192},{224,288},... | collective-permute-start | bytes 49160 | tf_op jit(solution)/shard_map/ppermute | solution.py:461
  10.9 8.0 %collective-permute-start.3 = (bf16[1,32,256]{2,1,0:T(8,128)(2,1)S(1)}, bf16[1,32,256]{2,1,0:T(8,128)(2,1)S(1)}, u32[]{:S(2)}, u32[]{:S(2)}) collective-permute-start(bf16[1,32,256]{2,1,0:T(8,128)(2,1)S(1)} %get-tuple-element.27), channel_id=1, source_target_pairs={{0,64},{64,0},{32,96},{96,32},{128,192},{192,128},{160,224},{224,1... | collective-permute-start | bytes 49160 | tf_op jit(solution)/shard_map/ppermute | solution.py:462
  18.9 1.0 %copy.6 = bf16[256,9,8,8]{0,2,3,1:T(8,128)(2,1)S(1)} copy(bf16[256,9,8,8]{0,3,2,1:T(8,128)(2,1)} %bitcast.13) | data formatting | bytes 589824 | tf_op jit(solution)/shard_map/reshape | solution.py:539
  19.9 0.0 collective-permute-done.2.rc
  19.9 1.6 %collective-permute-done.3.rd = bf16[1,32,256]{2,1,0:T(8,128)(2,1)S(1)} collective-permute-done((bf16[1,32,256]{2,1,0:T(8,128)(2,1)S(1)}, bf16[1,32,256]{2,1,0:T(8,128)(2,1)S(1)}, u32[]{:S(2)}, u32[]{:S(2)}) %collective-permute-start.3) | collective-permute-done | bytes 16416 | tf_op jit(solution)/shard_map/ppermute | solution.py:462
  21.5 0.0 collective-permute-done.ra
  21.5 2.9 %collective-permute-done.1.rb = bf16[18,32,256]{2,1,0:T(8,128)(2,1)S(1)} collective-permute-done((bf16[18,32,256]{2,1,0:T(8,128)(2,1)S(1)}, bf16[18,32,256]{2,1,0:T(8,128)(2,1)S(1)}, u32[]{:S(2)}, u32[]{:S(2)}) %collective-permute-start.1) | collective-permute-done | bytes 294944 | tf_op jit(solution)/shard_map/ppermute | solution.py:460
  24.4 0.1 pack.1
  24.6 3.6 %collective-permute-start.4 = (bf16[26,16,256]{2,1,0:T(8,128)(2,1)S(1)}, bf16[26,16,256]{2,1,0:T(8,128)(2,1)S(1)}, u32[]{:S(2)}, u32[]{:S(2)}) collective-permute-start(bf16[26,16,256]{2,1,0:T(8,128)(2,1)S(1)} %pack.1), channel_id=1, source_target_pairs={{1,2},{2,1},{3,4},{4,3},{5,6},{6,5},{7,8},{8,7},{9,10},{10,9},{11,... | collective-permute-start | bytes 638984 | tf_op jit(solution)/shard_map/ppermute | solution.py:477
  28.2 0.0 copy-done
  28.2 3.1 %encode_own.1 = (bf16[48,32,256]{2,1,0:T(8,128)(2,1)S(1)}, bf16[18,32,256]{2,1,0:T(8,128)(2,1)S(1)}, f32[2,48,256]{2,1,0:T(8,128)S(1)}, f32[2,24,256]{2,1,0:T(8,...) custom-call(bf16[16,32,256]{2,1,0:T(8,128)(2,1)S(1)} %get-tuple-element.22.f1, ...), custom_call_target="tpu_custom_call" | custom-call | flops 2491416576 | bytes 4194304 | tf_op jit(solution)/shard_map/encode_own/pallas_call | solution.py:481
  31.3 10.5 %all-gather = bf16[52,16,256]{2,1,0:T(8,128)(2,1)S(1)} all-gather(bf16[26,16,256]{2,1,0:T(8,128)(2,1)S(1)} %get-tuple-element.33), channel_id=2, replica_groups={{0,1},{2,3},{4,5},{6,7},{8,9},{10,11},{12,13},{14,15},{16,17},{18,19},{..., dimensions={0}, use_global_device_ids=true | all-gather | bytes 638976 | tf_op jit(solution)/shard_map/all_gather | solution.py:507
  41.8 0.7 %strip.1 = (bf16[18,16,256]{2,1,0:T(8,128)(2,1)S(1)}, bf16[48,16,256]{2,1,0:T(8,128)(2,1)S(1)}, bf16[18,16,256]{2,1,0:T(8,128)(2,1)S(1)}) custom-call(bf16[48,32,256]{2,1,0:T(8,128)(2,1)S(1)} %get-tuple-element.28.o2, bf16[18,32,256]{2,1,0:T(8,128)(2,1)S(1)} %get-tuple-element.29.o1, f32[2,48,256]{2,1,0:T(8,128)S(1)} %get-tuple-element.30.ends2, ...), custom_call_target="tpu_custom_call" | custom-call | flops 339738624 | bytes 4194304 | tf_op jit(solution)/shard_map/strip/pallas_call | solution.py:512
  42.5 0.0 collective-permute-done.4.c_x
  42.5 1.7 %score.1 = (f32[8,640]{1,0:T(8,128)S(1)}, bf16[18,32,256]{2,1,0:T(8,128)(2,1)S(1)}) custom-call(bf16[48,32,256]{2,1,0:T(8,128)(2,1)S(1)} %get-tuple-element.28.o2, bf16[18,32,256]{2,1,0:T(8,128)(2,1)S(1)} %get-tuple-element.29.o1, f32[2,48,256]{2,1,0:T(8,128)S(1)} %get-tuple-element.30.ends2, f32[2,24,256]{2,1,0:T(8,128)S(1)} %get-tuple-element.31.ends1, ...), custom_call_target="tpu_custom_call" | custom-call | tf_op jit(solution)/shard_map/score/pallas_call | solution.py:526
  44.2 1.9 %collective-permute-start.5 = (f32[8,640]{1,0:T(8,128)S(1)}, f32[8,640]{1,0:T(8,128)S(1)}, u32[]{:S(2)}, u32[]{:S(2)}) collective-permute-start(f32[8,640]{1,0:T(8,128)S(1)} %get-tuple-element.37.mine), channel_id=1, source_target_pairs={{1,2},{2,1},{3,4},{4,3},{5,6},{6,5},{7,8},{8,7},{9,10},{10,9},{11,... | collective-permute-start | bytes 61448 | tf_op jit(solution)/shard_map/ppermute | solution.py:536
  46.1 7.9 %all-gather.1 = f32[16,640]{1,0:T(8,128)S(1)} all-gather(f32[8,640]{1,0:T(8,128)S(1)} %get-tuple-element.37.mine), channel_id=3, replica_groups={{0,1},{2,3},{4,5},{6,7},{8,9},{10,11},{12,13},{14,15},{16,17},{18,19},{..., dimensions={0}, use_global_device_ids=true | all-gather | bytes 61440 | tf_op jit(solution)/shard_map/all_gather | solution.py:537
  54.0 0.8 %mix.1 = f32[9,8,8,512]{3,2,1,0:T(8,128)S(1)} custom-call(bf16[18,32,256]{2,1,0:T(8,128)(2,1)S(1)} %get-tuple-element.38.enc_one, bf16[576,256]{1,0:T(8,128)(2,1)S(1)} %bitcast.11), custom_call_target="tpu_custom_call" | custom-call | flops 150994944 | bytes 1179648 | tf_op jit(solution)/shard_map/mix/pallas_call | solution.py:540
  54.9 0.0 collective-permute-done.5.far
  54.9 1.3 %upsample.1 = f32[2,128,256]{2,1,0:T(8,128)} custom-call(f32[8,640]{1,0:T(8,128)S(1)} %get-tuple-element.37.mine, f32[8,640]{1,0:T(8,128)S(1)} %collective-permute-done.5.far, f32[2,8,640]{2,1,0:T(8,128)S(1)} %bitcast.12, f32[9,8,8,512]{3,2,1,0:T(8,128)S(1)} %mix.1), custom_call_target="tpu_custom_call" | custom-call | tf_op jit(solution)/shard_map/upsample/pallas_call | solution.py:551
Async XLA Ops:
  0.0 28.2 %copy-start = (bf16[3,3,256,256]{3,2,1,0:T(8,128)(2,1)S(1)}, bf16[3,3,256,256]{3,2,1,0:T(8,128)(2,1)}, u32[]{:S(2)}) copy-start(bf16[3,3,256,256]{3,2,1,0:T(8,128)(2,1)} %param.6) | copy-start | bytes 3538948
  1.4 20.1 %collective-permute-start = (bf16[18,32,256]{2,1,0:T(8,128)(2,1)S(1)}, bf16[18,32,256]{2,1,0:T(8,128)(2,1)S(1)}, u32[]{:S(2)}, u32[]{:S(2)}) collective-permute-start(bf16[18,32,256]{2,1,0:T(8,128)(2,1)S(1)} %get-tuple-element.24), channel_id=1, source_target_pairs={{32,64},{64,32},{96,128},{128,96},{160,192},{192,160},{224,256},{2... | collective-permute-start | bytes 884744 | tf_op jit(solution)/shard_map/ppermute | solution.py:459
  2.1 22.3 %collective-permute-start.1 = (bf16[18,32,256]{2,1,0:T(8,128)(2,1)S(1)}, bf16[18,32,256]{2,1,0:T(8,128)(2,1)S(1)}, u32[]{:S(2)}, u32[]{:S(2)}) collective-permute-start(bf16[18,32,256]{2,1,0:T(8,128)(2,1)S(1)} %get-tuple-element.25), channel_id=1, source_target_pairs={{0,32},{32,0},{64,96},{96,64},{128,160},{160,128},{192,224},{224,1... | collective-permute-start | bytes 884744 | tf_op jit(solution)/shard_map/ppermute | solution.py:460
  10.2 9.7 %collective-permute-start.2 = (bf16[1,32,256]{2,1,0:T(8,128)(2,1)S(1)}, bf16[1,32,256]{2,1,0:T(8,128)(2,1)S(1)}, u32[]{:S(2)}, u32[]{:S(2)}) collective-permute-start(bf16[1,32,256]{2,1,0:T(8,128)(2,1)S(1)} %get-tuple-element.26), channel_id=1, source_target_pairs={{64,128},{128,64},{96,160},{160,96},{192,256},{256,192},{224,288},... | collective-permute-start | bytes 49160 | tf_op jit(solution)/shard_map/ppermute | solution.py:461
  10.9 10.6 %collective-permute-start.3 = (bf16[1,32,256]{2,1,0:T(8,128)(2,1)S(1)}, bf16[1,32,256]{2,1,0:T(8,128)(2,1)S(1)}, u32[]{:S(2)}, u32[]{:S(2)}) collective-permute-start(bf16[1,32,256]{2,1,0:T(8,128)(2,1)S(1)} %get-tuple-element.27), channel_id=1, source_target_pairs={{0,64},{64,0},{32,96},{96,32},{128,192},{192,128},{160,224},{224,1... | collective-permute-start | bytes 49160 | tf_op jit(solution)/shard_map/ppermute | solution.py:462
  24.6 17.9 %collective-permute-start.4 = (bf16[26,16,256]{2,1,0:T(8,128)(2,1)S(1)}, bf16[26,16,256]{2,1,0:T(8,128)(2,1)S(1)}, u32[]{:S(2)}, u32[]{:S(2)}) collective-permute-start(bf16[26,16,256]{2,1,0:T(8,128)(2,1)S(1)} %pack.1), channel_id=1, source_target_pairs={{1,2},{2,1},{3,4},{4,3},{5,6},{6,5},{7,8},{8,7},{9,10},{10,9},{11,... | collective-permute-start | bytes 638984 | tf_op jit(solution)/shard_map/ppermute | solution.py:477
  44.2 10.7 %collective-permute-start.5 = (f32[8,640]{1,0:T(8,128)S(1)}, f32[8,640]{1,0:T(8,128)S(1)}, u32[]{:S(2)}, u32[]{:S(2)}) collective-permute-start(f32[8,640]{1,0:T(8,128)S(1)} %get-tuple-element.37.mine), channel_id=1, source_target_pairs={{1,2},{2,1},{3,4},{4,3},{5,6},{6,5},{7,8},{8,7},{9,10},{10,9},{11,... | collective-permute-start | bytes 61448 | tf_op jit(solution)/shard_map/ppermute | solution.py:536

commit v5 on v4

--- a/solution.py
+++ b/solution.py
@@ -35,27 +35,25 @@
     return out
 
 
-def edge_kernel(rows, cols, f1, f2, m_a, m_b, m_c, m_d, g1, g2, sems):
+def edge_kernel(rows, cols, f1, f2, m_a, m_b, m_c, m_d, g1, sems):
     band = lax.axis_index("lat")
     odd = band % 2
     upper = band % 4 // 2
-    copies = [
-        pltpu.make_async_copy(f2, g2, sems.at[0]),
-        pltpu.make_async_copy(f1, g1, sems.at[1]),
-    ]
+    copies = []
     for k, (msg, low) in enumerate(((m_a, odd), (m_b, 1 - odd))):
         copies.append(
-            pltpu.make_async_copy(f2, msg.at[pl.ds(0, rows)], sems.at[2 + 2 * k])
+            pltpu.make_async_copy(f2, msg.at[pl.ds(0, rows)], sems.at[2 * k])
         )
         copies.append(
             pltpu.make_async_copy(
-                f1.at[pl.ds(low * (rows - 2), 2)], msg.at[pl.ds(rows, 2)], sems.at[3 + 2 * k]
+                f1.at[pl.ds(low * (rows - 2), 2)], msg.at[pl.ds(rows, 2)], sems.at[1 + 2 * k]
             )
         )
     for k, (msg, low) in enumerate(((m_c, upper), (m_d, 1 - upper))):
         copies.append(
-            pltpu.make_async_copy(f2.at[pl.ds(low * (rows - 1), 1)], msg, sems.at[6 + k])
+            pltpu.make_async_copy(f2.at[pl.ds(low * (rows - 1), 1)], msg, sems.at[4 + k])
         )
+    copies.append(pltpu.make_async_copy(f1, g1, sems.at[6]))
     for copy in copies:
         copy.start()
     for copy in copies:
@@ -100,7 +98,7 @@
         ext1[0:2] = north[rows : rows + 2]
         ext1[n1 - 2 : n1] = south[rows : rows + 2]
 
-    ext2[1 + rows : 1 + 2 * rows] = f2[...]
+    ext2[1 + rows : 1 + 2 * rows] = f2[0:rows]
     ext1[2 : 2 + rows] = f1[...]
     by_parity(halo, ra, rb, rc, rd)
 
@@ -144,7 +142,7 @@
         s1[0:2, own] = north[rows : rows + 2].astype(F32)
         s1[n1 - 2 : n1, own] = south[rows : rows + 2].astype(F32)
 
-    s2[1 + rows : 1 + 2 * rows, own] = f2[...].astype(F32)
+    s2[1 + rows : 1 + 2 * rows, own] = f2[0:rows].astype(F32)
     s1[2 : 2 + rows, own] = f1[...].astype(F32)
     by_parity(halo, ra, rb, rc, rd)
     for s in (s2, s1):
@@ -301,48 +299,60 @@
         values += [jnp.zeros((2, queries), F32)]
         sums[:, cols + g * queries : cols + (g + 1) * queries] = jnp.concatenate(values, axis=0)
 
-    lanes = 2 * cols
+    quarter = cols
+    lanes = 4 * quarter
     sub = lax.broadcasted_iota(jnp.int32, (BR, lanes), 0).astype(F32)
     lane = lax.broadcasted_iota(jnp.int32, (BR, lanes), 1)
-    is_own = lane < cols
-    of_right = (lane >= cols) & (lane < cols + BC)
+    below = lane >= 2 * quarter
+    spot = lane % (2 * quarter)
+    is_own = spot < quarter
+    of_right = (spot >= quarter) & (spot < quarter + BC)
     base = jnp.where(is_own, 0.0, jnp.where(of_right, float(BC - cols), float(cols)))
-    for row_at, first, at in ((0, 0, 0), (rows + 1, bands + 1, cols + rows * cols)):
-        query = jnp.concatenate([features(enc_one, row_at, 1), features(beside, row_at, 1)], axis=0)
-        acc = None
-        for kb in range(3):
-            both = scores(first + kb, query)
-            for kr in range(BR):
-                row = float((kb - 1) * BR + kr)
-                now = [
-                    jnp.exp(jnp.where(of_right, both[kr, 2 + i], both[kr, i])) for i in range(2)
-                ]
-                now += [jnp.where(is_own, jnp.exp(both[kr, i]), 0.0) for i in range(2, 4)]
-                now += [row * ((now[0] + now[1]) + (now[2] + now[3]))]
-                acc = add(acc, now)
-        values = triple(acc[0:4], acc[4], sub, base)
-        sums[0:3, at : at + cols] = jnp.concatenate([v[:, 0:cols] for v in values], axis=0)
-        sums[3:6, at : at + cols] = jnp.concatenate([v[:, cols:] for v in values], axis=0)
+    query = jnp.concatenate(
+        [features(r, at, 1) for at in (0, rows + 1) for r in (enc_one, beside)], axis=0
+    )
+    acc = None
+    for kb in range(3):
+        over = scores(kb, query)
+        under = scores(bands + 1 + kb, query)
+        for kr in range(BR):
+            row = float((kb - 1) * BR + kr)
+            both = [jnp.where(below, under[kr, i], over[kr, i]) for i in range(4)]
+            now = [jnp.exp(jnp.where(of_right, both[2 + i], both[i])) for i in range(2)]
+            now += [jnp.where(is_own, jnp.exp(both[i]), 0.0) for i in range(2, 4)]
+            now += [row * ((now[0] + now[1]) + (now[2] + now[3]))]
+            acc = add(acc, now)
+    values = triple(acc[0:4], acc[4], sub, base)
+    for k, at in enumerate((0, cols + rows * cols)):
+        for m in range(2):
+            lo = (2 * k + m) * quarter
+            sums[3 * m : 3 * m + 3, at : at + cols] = jnp.concatenate(
+                [v[:, lo : lo + quarter] for v in values], axis=0
+            )
         sums[6:8, at : at + cols] = jnp.zeros((2, cols), F32)
 
 
-def mix_kernel(rows, cells, enc_one, wt, mix):
+def mix_kernel(rows, cells, enc_one, wt, sums, mix, total, passed):
+    passed[...] = sums[...]
     feats = enc_one[1 : 1 + rows].reshape(cells, CH)
     step = 256
+    count = UP * UP
     for c0 in range(0, cells, step):
-        for k in range(UP):
-            wk = jnp.concatenate(
-                [wt[n * 64 + k * UP : n * 64 + k * UP + UP] for n in range(9)], axis=0
+        mass = None
+        for n in range(9):
+            logits = lax.dot_general(
+                wt[n * count : (n + 1) * count],
+                feats[c0 : c0 + step],
+                (((1,), (1,)), ((), ())),
+                preferred_element_type=F32,
             )
-            logits = lax.dot_general(
-                wk, feats[c0 : c0 + step], (((1,), (1,)), ((), ())), preferred_element_type=F32
-            )
-            expo = jnp.exp(logits).reshape(9, UP, step)
-            total = jnp.sum(expo, axis=0)
-            mix[:, k, :, c0 : c0 + step] = expo / total[None]
-
-
-def up_kernel(rows, cols, mine, far, chip, mix, out):
+            expo = jnp.exp(logits).reshape(UP, UP, step)
+            mix[n, :, :, c0 : c0 + step] = expo
+            mass = expo if mass is None else mass + expo
+        total[:, :, c0 : c0 + step] = 1.0 / mass
+
+
+def up_kernel(rows, cols, mine, far, chip, mix, total_r, out):
     lat = lax.axis_index("lat")
     last = lax.axis_size("lat") - 1
     lon_odd = lax.axis_index("lon") % 2
@@ -403,7 +413,8 @@
                     for n in range(9):
                         term = mix[n, u * group + k, :, t * tile : (t + 1) * tile] * flows[n]
                         acc = term if acc is None else acc + term
-                    block.append(acc)
+                    part = total_r[u * group + k, :, t * tile : (t + 1) * tile]
+                    block.append(acc * part)
                 for span, high in bits:
                     shift = span * cols
                     done = list(block)
@@ -444,12 +455,12 @@
         return jax.ShapeDtypeStruct(shape, dtype)
 
     tile = array(rows, cols, CH)
-    m_a, m_b, m_c, m_d, one, two = pl.pallas_call(
+    m_a, m_b, m_c, m_d, one = pl.pallas_call(
         functools.partial(edge_kernel, rows, cols),
-        out_shape=(array(few, cols, CH),) * 2 + (array(1, cols, CH),) * 2 + (tile, tile),
+        out_shape=(array(few, cols, CH),) * 2 + (array(1, cols, CH),) * 2 + (tile,),
         in_specs=[pl.BlockSpec(memory_space=pltpu.MemorySpace.HBM)] * 2,
-        out_specs=(VMEM,) * 6,
-        scratch_shapes=[pltpu.SemaphoreType.DMA((8,))],
+        out_specs=(VMEM,) * 5,
+        scratch_shapes=[pltpu.SemaphoreType.DMA((7,))],
         compiler_params=params(8),
         name="edges",
     )(
@@ -473,7 +484,7 @@
         ],
         compiler_params=params(16),
         name="pack",
-    )(one, two, row_a, row_b, row_c, row_d)
+    )(one, m_a, row_a, row_b, row_c, row_d)
     col_x = lax.ppermute(m_x, "lon", far_lon)
 
     weight = enc_weight.reshape(9 * CH, CH)
@@ -502,7 +513,7 @@
             flops=2 * 9 * CH * CH * cols * (tall + few), bytes_accessed=4 << 20, transcendentals=0
         ),
         name="encode_own",
-    )(one, two, row_a, row_b, row_c, row_d, weight)
+    )(one, m_a, row_a, row_b, row_c, row_d, weight)
 
     col_in = lax.all_gather(m_in, "lon", axis_index_groups=chips)
     side_scratch = [
@@ -534,28 +545,32 @@
         name="score",
     )(own_two, own_one, ends_two, ends_one, edges, strip_in, two_in, first_in, col_x, weight)
     sums_far = lax.ppermute(sums, "lon", far_lon)
-    sums_in = lax.all_gather(sums, "lon", axis_index_groups=chips)
 
     wt = mask_weight.reshape(CH, 9, UP, UP).transpose(1, 3, 2, 0).reshape(9 * UP * UP, CH)
-    mix = pl.pallas_call(
+    mix, inverse, sums_too = pl.pallas_call(
         functools.partial(mix_kernel, rows, cells),
-        out_shape=array(9, UP, UP, cells, dtype=F32),
-        in_specs=[VMEM] * 2,
-        out_specs=VMEM,
+        out_shape=(
+            array(9, UP, UP, cells, dtype=F32),
+            array(UP, UP, cells, dtype=F32),
+            array(8, width, dtype=F32),
+        ),
+        in_specs=[VMEM] * 3,
+        out_specs=(VMEM,) * 3,
         compiler_params=params(16),
         cost_estimate=pl.CostEstimate(
             flops=2 * 576 * CH * cells, bytes_accessed=4 * 576 * cells, transcendentals=576 * cells
         ),
         name="mix",
-    )(enc_one, wt)
+    )(enc_one, wt, sums)
+    sums_in = lax.all_gather(sums_too, "lon", axis_index_groups=chips)
     return pl.pallas_call(
         functools.partial(up_kernel, rows, cols),
         out_shape=array(2, rows * UP, cols * UP, dtype=F32),
-        in_specs=[VMEM] * 4,
+        in_specs=[VMEM] * 5,
         out_specs=VMEM,
         compiler_params=params(16),
         name="upsample",
-    )(sums, sums_far, sums_in, mix)
+    )(sums, sums_far, sums_in, mix, inverse)
 
 
 def solution(mesh):

time: 56.5 us -> 56.2 us (level)
  blocking collectives: 18.5 us -> 15.2 us
  starting transfers between devices: 22.9 us -> 25.3 us
    ppermute x1, waiting for transfers between devices: 1.58 us -> 4.95 us  [body(): row_d = lax.ppermute(m_d, 'lat', low_lat)]
    ppermute x1, starting transfers between devices: 8.15 us -> 4.83 us  [body(): row_b = lax.ppermute(m_b, 'lat', near_lat)]
    ppermute x1, starting transfers between devices: 7.96 us -> 11.3 us  [body(): row_d = lax.ppermute(m_d, 'lat', low_lat)]
    ppermute x1, waiting for transfers between devices: 2.94 us -> 0.01 us  [body(): row_b = lax.ppermute(m_b, 'lat', near_lat)]
    all_gather x1, blocking collectives: 10.5 us -> 8.05 us  [body(): col_in = lax.all_gather(m_in, 'lon', axis_index_groups=chips)]
    ppermute x1, starting transfers between devices: 3.58 us -> 5.95 us  [body(): col_x = lax.ppermute(m_x, 'lon', far_lon)]
    all_gather x1, blocking collectives: 7.93 us -> 7.17 us  [body(): sums_in = lax.all_gather(sums_too, 'lon', axis_index_groups=chips)]
  transfers between devices with their start and end apart: 6 -> 6, of which waited for: 2 -> 1; matrix products, arithmetic and copies ran while one was open for 2% -> 2% of each run, Pallas kernels for 8% -> 8%
where the time goes in v5:
time: 56.2 us; the launch traced here: 55.8 us
  starting transfers between devices  25.3 us (45%)
  blocking collectives  15.2 us (27%)
  Pallas kernels  9.15 us (16%)
  waiting for transfers between devices  4.97 us (9%)
  local copies, waits for them, and re-layouts  1.03 us (2%)
    ppermute x1, starting transfers between devices, body(): row_d = lax.ppermute(m_d, 'lat', low_lat)  11.3 us
    all_gather x1, blocking collectives, body(): col_in = lax.all_gather(m_in, 'lon', axis_index_groups=chips)  8.05 us
    all_gather x1, blocking collectives, body(): sums_in = lax.all_gather(sums_too, 'lon', axis_index_groups=chips)  7.17 us
    ppermute x1, starting transfers between devices, body(): col_x = lax.ppermute(m_x, 'lon', far_lon)  5.95 us
    ppermute x1, waiting for transfers between devices, body(): row_d = lax.ppermute(m_d, 'lat', low_lat)  4.95 us
    ppermute x1, starting transfers between devices, body(): row_b = lax.ppermute(m_b, 'lat', near_lat)  4.83 us
    pallas_call x1, Pallas kernels, body(): pl.pallas_call(functools.partial(own_kernel, rows, cols), out_shape=(arra...  3.09 us
    ppermute x1, starting transfers between devices, body(): sums_far = lax.ppermute(sums, 'lon', far_lon)  1.92 us
  transfers between devices with their start and end apart: 6, of which 1 were waited for; matrix products, arithmetic and copies ran while one was open for 2% of the time, Pallas kernels for 8%

profile of v5, /device:TPU:1, one launch (start us, length us, event | category | flops | bytes accessed | tf_op | source)
XLA Modules:
  0.0 55.8 jit_solution(8223429305175571518)
XLA Ops:
  0.0 0.0 copy-start
  0.0 1.3 %edges.1 = (bf16[18,32,256]{2,1,0:T(8,128)(2,1)S(1)}, bf16[18,32,256]{2,1,0:T(8,128)(2,1)S(1)}, bf16[1,32,256]{2,1,0:T(8,128)(2,1)S(1)}, bf16[1,32,256]{2,1,0:T(8,128)(2,1)S(1)}, bf16[16,32,256]{2,1,0:T(8,128)(2,1)S(1)}) custom-call(bf16[16,32,256]{2,1,0:T(8,128)(2,1)} %f1.1, bf16[16,32,256]{2,1,0:T(8,128)(2,1)} %f2.1), custom_call_target="tpu_custom_call" | custom-call | tf_op jit(solution)/shard_map/edges/pallas_call | solution.py:458
  1.3 4.8 %collective-permute-start.1 = (bf16[18,32,256]{2,1,0:T(8,128)(2,1)S(1)}, bf16[18,32,256]{2,1,0:T(8,128)(2,1)S(1)}, u32[]{:S(2)}, u32[]{:S(2)}) collective-permute-start(bf16[18,32,256]{2,1,0:T(8,128)(2,1)S(1)} %get-tuple-element.26), channel_id=1, source_target_pairs={{0,32},{32,0},{64,96},{96,64},{128,160},{160,128},{192,224},{224,1... | collective-permute-start | bytes 884744 | tf_op jit(solution)/shard_map/ppermute | solution.py:471
  6.2 0.7 %collective-permute-start = (bf16[18,32,256]{2,1,0:T(8,128)(2,1)S(1)}, bf16[18,32,256]{2,1,0:T(8,128)(2,1)S(1)}, u32[]{:S(2)}, u32[]{:S(2)}) collective-permute-start(bf16[18,32,256]{2,1,0:T(8,128)(2,1)S(1)} %get-tuple-element.25.f2), channel_id=1, source_target_pairs={{32,64},{64,32},{96,128},{128,96},{160,192},{192,160},{224,256},{2... | collective-permute-start | bytes 884744 | tf_op jit(solution)/shard_map/ppermute | solution.py:470
  6.9 0.7 %collective-permute-start.2 = (bf16[1,32,256]{2,1,0:T(8,128)(2,1)S(1)}, bf16[1,32,256]{2,1,0:T(8,128)(2,1)S(1)}, u32[]{:S(2)}, u32[]{:S(2)}) collective-permute-start(bf16[1,32,256]{2,1,0:T(8,128)(2,1)S(1)} %get-tuple-element.27), channel_id=1, source_target_pairs={{64,128},{128,64},{96,160},{160,96},{192,256},{256,192},{224,288},... | collective-permute-start | bytes 49160 | tf_op jit(solution)/shard_map/ppermute | solution.py:472
  7.5 11.3 %collective-permute-start.3 = (bf16[1,32,256]{2,1,0:T(8,128)(2,1)S(1)}, bf16[1,32,256]{2,1,0:T(8,128)(2,1)S(1)}, u32[]{:S(2)}, u32[]{:S(2)}) collective-permute-start(bf16[1,32,256]{2,1,0:T(8,128)(2,1)S(1)} %get-tuple-element.28), channel_id=1, source_target_pairs={{0,64},{64,0},{32,96},{96,32},{128,192},{192,128},{160,224},{224,1... | collective-permute-start | bytes 49160 | tf_op jit(solution)/shard_map/ppermute | solution.py:473
  18.8 1.0 %copy.6 = bf16[256,9,8,8]{0,2,3,1:T(8,128)(2,1)S(1)} copy(bf16[256,9,8,8]{0,3,2,1:T(8,128)(2,1)} %bitcast.13) | data formatting | bytes 589824 | tf_op jit(solution)/shard_map/reshape | solution.py:549
  19.8 0.0 collective-permute-done.2.rc
  19.9 5.0 %collective-permute-done.3.rd = bf16[1,32,256]{2,1,0:T(8,128)(2,1)S(1)} collective-permute-done((bf16[1,32,256]{2,1,0:T(8,128)(2,1)S(1)}, bf16[1,32,256]{2,1,0:T(8,128)(2,1)S(1)}, u32[]{:S(2)}, u32[]{:S(2)}) %collective-permute-start.3) | collective-permute-done | bytes 16416 | tf_op jit(solution)/shard_map/ppermute | solution.py:473
  24.8 0.0 collective-permute-done.1.rb
  24.8 0.0 collective-permute-done.ra
  24.8 0.2 pack.1
  25.0 5.9 %collective-permute-start.4 = (bf16[26,16,256]{2,1,0:T(8,128)(2,1)S(1)}, bf16[26,16,256]{2,1,0:T(8,128)(2,1)S(1)}, u32[]{:S(2)}, u32[]{:S(2)}) collective-permute-start(bf16[26,16,256]{2,1,0:T(8,128)(2,1)S(1)} %pack.1), channel_id=1, source_target_pairs={{1,2},{2,1},{3,4},{4,3},{5,6},{6,5},{7,8},{8,7},{9,10},{10,9},{11,... | collective-permute-start | bytes 638984 | tf_op jit(solution)/shard_map/ppermute | solution.py:488
  30.9 0.0 copy-done
  30.9 3.1 %encode_own.1 = (bf16[48,32,256]{2,1,0:T(8,128)(2,1)S(1)}, bf16[18,32,256]{2,1,0:T(8,128)(2,1)S(1)}, f32[2,48,256]{2,1,0:T(8,128)S(1)}, f32[2,24,256]{2,1,0:T(8,...) custom-call(bf16[16,32,256]{2,1,0:T(8,128)(2,1)S(1)} %get-tuple-element.24.f1, ...), custom_call_target="tpu_custom_call" | custom-call | flops 2491416576 | bytes 4194304 | tf_op jit(solution)/shard_map/encode_own/pallas_call | solution.py:492
  34.0 8.0 %all-gather = bf16[52,16,256]{2,1,0:T(8,128)(2,1)S(1)} all-gather(bf16[26,16,256]{2,1,0:T(8,128)(2,1)S(1)} %get-tuple-element.34), channel_id=2, replica_groups={{0,1},{2,3},{4,5},{6,7},{8,9},{10,11},{12,13},{14,15},{16,17},{18,19},{..., dimensions={0}, use_global_device_ids=true | all-gather | bytes 638976 | tf_op jit(solution)/shard_map/all_gather | solution.py:518
  42.1 0.7 %strip.1 = (bf16[18,16,256]{2,1,0:T(8,128)(2,1)S(1)}, bf16[48,16,256]{2,1,0:T(8,128)(2,1)S(1)}, bf16[18,16,256]{2,1,0:T(8,128)(2,1)S(1)}) custom-call(bf16[48,32,256]{2,1,0:T(8,128)(2,1)S(1)} %get-tuple-element.29.o2, bf16[18,32,256]{2,1,0:T(8,128)(2,1)S(1)} %get-tuple-element.30.o1, f32[2,48,256]{2,1,0:T(8,128)S(1)} %get-tuple-element.31.ends2, ...), custom_call_target="tpu_custom_call" | custom-call | flops 339738624 | bytes 4194304 | tf_op jit(solution)/shard_map/strip/pallas_call | solution.py:523
  42.8 0.0 collective-permute-done.4.c_x
  42.8 1.7 %score.1 = (f32[8,640]{1,0:T(8,128)S(1)}, bf16[18,32,256]{2,1,0:T(8,128)(2,1)S(1)}) custom-call(bf16[48,32,256]{2,1,0:T(8,128)(2,1)S(1)} %get-tuple-element.29.o2, bf16[18,32,256]{2,1,0:T(8,128)(2,1)S(1)} %get-tuple-element.30.o1, f32[2,48,256]{2,1,0:T(8,128)S(1)} %get-tuple-element.31.ends2, f32[2,24,256]{2,1,0:T(8,128)S(1)} %get-tuple-element.32.ends1, ...), custom_call_target="tpu_custom_call" | custom-call | tf_op jit(solution)/shard_map/score/pallas_call | solution.py:537
  44.5 1.9 %collective-permute-start.5 = (f32[8,640]{1,0:T(8,128)S(1)}, f32[8,640]{1,0:T(8,128)S(1)}, u32[]{:S(2)}, u32[]{:S(2)}) collective-permute-start(f32[8,640]{1,0:T(8,128)S(1)} %get-tuple-element.38.sums.mine), channel_id=1, source_target_pairs={{1,2},{2,1},{3,4},{4,3},{5,6},{6,5},{7,8},{8,7},{9,10},{10,9},{11,... | collective-permute-start | bytes 61448 | tf_op jit(solution)/shard_map/ppermute | solution.py:547
  46.4 0.8 %mix.1 = (f32[9,8,8,512]{3,2,1,0:T(8,128)S(1)}, f32[8,8,512]{2,1,0:T(8,128)S(1)}, f32[8,640]{1,0:T(8,128)S(1)}) custom-call(bf16[18,32,256]{2,1,0:T(8,128)(2,1)S(1)} %get-tuple-element.39.enc_one, bf16[576,256]{1,0:T(8,128)(2,1)S(1)} %bitcast.11, f32[8,640]{1,0:T(8,128)S(1)} %get-tuple-element.38.sums.mine), custom_call_target="tpu_custom_call" | custom-call | flops 150994944 | bytes 1179648 | tf_op jit(solution)/shard_map/mix/pallas_call | solution.py:550
  47.3 7.2 %all-gather.1 = f32[16,640]{1,0:T(8,128)S(1)} all-gather(f32[8,640]{1,0:T(8,128)S(1)} %get-tuple-element.40), channel_id=3, replica_groups={{0,1},{2,3},{4,5},{6,7},{8,9},{10,11},{12,13},{14,15},{16,17},{18,19},{..., dimensions={0}, use_global_device_ids=true | all-gather | bytes 61440 | tf_op jit(solution)/shard_map/all_gather | solution.py:565
  54.4 0.0 collective-permute-done.5.far
  54.4 1.3 %upsample.1 = f32[2,128,256]{2,1,0:T(8,128)} custom-call(f32[8,640]{1,0:T(8,128)S(1)} %get-tuple-element.38.sums.mine, f32[8,640]{1,0:T(8,128)S(1)} %collective-permute-done.5.far, f32[2,8,640]{2,1,0:T(8,128)S(1)} %bitcast.12, f32[9,8,8,512]{3,2,1,0:T(8,128)S(1)} %get-tuple-element.41.mix, f32[8,8,512]{2,1,0:T(8,128)S(1)} %get-tuple-element.42.total_r), custom_call_target="tpu_custom_call" | custom-call | tf_op jit(solution)/shard_map/upsample/pallas_call | solution.py:566
Async XLA Ops:
  0.0 30.9 %copy-start = (bf16[3,3,256,256]{3,2,1,0:T(8,128)(2,1)S(1)}, bf16[3,3,256,256]{3,2,1,0:T(8,128)(2,1)}, u32[]{:S(2)}) copy-start(bf16[3,3,256,256]{3,2,1,0:T(8,128)(2,1)} %param.6) | copy-start | bytes 3538948
  1.3 23.5 %collective-permute-start.1 = (bf16[18,32,256]{2,1,0:T(8,128)(2,1)S(1)}, bf16[18,32,256]{2,1,0:T(8,128)(2,1)S(1)}, u32[]{:S(2)}, u32[]{:S(2)}) collective-permute-start(bf16[18,32,256]{2,1,0:T(8,128)(2,1)S(1)} %get-tuple-element.26), channel_id=1, source_target_pairs={{0,32},{32,0},{64,96},{96,64},{128,160},{160,128},{192,224},{224,1... | collective-permute-start | bytes 884744 | tf_op jit(solution)/shard_map/ppermute | solution.py:471
  6.2 18.6 %collective-permute-start = (bf16[18,32,256]{2,1,0:T(8,128)(2,1)S(1)}, bf16[18,32,256]{2,1,0:T(8,128)(2,1)S(1)}, u32[]{:S(2)}, u32[]{:S(2)}) collective-permute-start(bf16[18,32,256]{2,1,0:T(8,128)(2,1)S(1)} %get-tuple-element.25.f2), channel_id=1, source_target_pairs={{32,64},{64,32},{96,128},{128,96},{160,192},{192,160},{224,256},{2... | collective-permute-start | bytes 884744 | tf_op jit(solution)/shard_map/ppermute | solution.py:470
  6.9 13.0 %collective-permute-start.2 = (bf16[1,32,256]{2,1,0:T(8,128)(2,1)S(1)}, bf16[1,32,256]{2,1,0:T(8,128)(2,1)S(1)}, u32[]{:S(2)}, u32[]{:S(2)}) collective-permute-start(bf16[1,32,256]{2,1,0:T(8,128)(2,1)S(1)} %get-tuple-element.27), channel_id=1, source_target_pairs={{64,128},{128,64},{96,160},{160,96},{192,256},{256,192},{224,288},... | collective-permute-start | bytes 49160 | tf_op jit(solution)/shard_map/ppermute | solution.py:472
  7.5 17.3 %collective-permute-start.3 = (bf16[1,32,256]{2,1,0:T(8,128)(2,1)S(1)}, bf16[1,32,256]{2,1,0:T(8,128)(2,1)S(1)}, u32[]{:S(2)}, u32[]{:S(2)}) collective-permute-start(bf16[1,32,256]{2,1,0:T(8,128)(2,1)S(1)} %get-tuple-element.28), channel_id=1, source_target_pairs={{0,64},{64,0},{32,96},{96,32},{128,192},{192,128},{160,224},{224,1... | collective-permute-start | bytes 49160 | tf_op jit(solution)/shard_map/ppermute | solution.py:473
  25.0 17.8 %collective-permute-start.4 = (bf16[26,16,256]{2,1,0:T(8,128)(2,1)S(1)}, bf16[26,16,256]{2,1,0:T(8,128)(2,1)S(1)}, u32[]{:S(2)}, u32[]{:S(2)}) collective-permute-start(bf16[26,16,256]{2,1,0:T(8,128)(2,1)S(1)} %pack.1), channel_id=1, source_target_pairs={{1,2},{2,1},{3,4},{4,3},{5,6},{6,5},{7,8},{8,7},{9,10},{10,9},{11,... | collective-permute-start | bytes 638984 | tf_op jit(solution)/shard_map/ppermute | solution.py:488
  44.5 10.0 %collective-permute-start.5 = (f32[8,640]{1,0:T(8,128)S(1)}, f32[8,640]{1,0:T(8,128)S(1)}, u32[]{:S(2)}, u32[]{:S(2)}) collective-permute-start(f32[8,640]{1,0:T(8,128)S(1)} %get-tuple-element.38.sums.mine), channel_id=1, source_target_pairs={{1,2},{2,1},{3,4},{4,3},{5,6},{6,5},{7,8},{8,7},{9,10},{10,9},{11,... | collective-permute-start | bytes 61448 | tf_op jit(solution)/shard_map/ppermute | solution.py:547

commit v6 on v5

--- a/solution.py
+++ b/solution.py
@@ -206,7 +206,13 @@
     put(side, strip, two, first)
 
 
-def strip_kernel(rows, cols, o2, o1, ends2, ends1, edges, chip, w, strip, two, first, ext, xs):
+def strip_kernel(
+    rows, cols, o2, o1, ends2, ends1, edges, chip, w, strip, two, first, order, ext, xs
+):
+    src = lax.broadcasted_iota(jnp.int32, order.shape, 0)
+    dst = lax.broadcasted_iota(jnp.int32, order.shape, 1)
+    to = (src % cols) * UP + src // cols
+    order[...] = jnp.where(dst == to, 1.0, 0.0).astype(BF16)
     lon_odd = lax.axis_index("lon") % 2
     msg = chip.at[1 - lon_odd]
 
@@ -252,10 +258,10 @@
         return (flat * scale).astype(BF16)
 
     def scores(block, query):
-        keys = e2[block * BR : (block + 1) * BR].reshape(BR * cols, CH)
+        keys = e2[block * BR : (block + 3) * BR].reshape(3 * BR * cols, CH)
         return lax.dot_general(
             keys, query, (((1,), (1,)), ((), ())), preferred_element_type=F32
-        ).reshape(BR, groups, BR, query.shape[0])
+        ).reshape(3, BR, groups, BR, query.shape[0])
 
     def add(total, now):
         return now if total is None else [p + e for p, e in zip(total, now)]
@@ -277,9 +283,10 @@
         query_own = features(enc_one, 1 + g * BR, BR)
         query_side = features(beside, 1 + g * BR, BR)
         acc = None
+        of_own = scores(g + 1, query_own)
+        of_side = scores(g + 1, query_side)
         for kb in range(3):
-            mine = scores(g + kb + 1, query_own)
-            other = scores(g + kb + 1, query_side)
+            mine, other = of_own[kb], of_side[kb]
             part = None
             for kr in range(BR):
                 row = float((kb - 1) * BR + kr)
@@ -312,9 +319,10 @@
         [features(r, at, 1) for at in (0, rows + 1) for r in (enc_one, beside)], axis=0
     )
     acc = None
+    all_over = scores(0, query)
+    all_under = scores(bands + 1, query)
     for kb in range(3):
-        over = scores(kb, query)
-        under = scores(bands + 1 + kb, query)
+        over, under = all_over[kb], all_under[kb]
         for kr in range(BR):
             row = float((kb - 1) * BR + kr)
             both = [jnp.where(below, under[kr, i], over[kr, i]) for i in range(4)]
@@ -338,21 +346,18 @@
     step = 256
     count = UP * UP
     for c0 in range(0, cells, step):
+        logits = lax.dot_general(
+            wt[...], feats[c0 : c0 + step], (((1,), (1,)), ((), ())), preferred_element_type=F32
+        )
         mass = None
         for n in range(9):
-            logits = lax.dot_general(
-                wt[n * count : (n + 1) * count],
-                feats[c0 : c0 + step],
-                (((1,), (1,)), ((), ())),
-                preferred_element_type=F32,
-            )
-            expo = jnp.exp(logits).reshape(UP, UP, step)
+            expo = jnp.exp(logits[n * count : (n + 1) * count]).reshape(UP, UP, step)
             mix[n, :, :, c0 : c0 + step] = expo
             mass = expo if mass is None else mass + expo
         total[:, :, c0 : c0 + step] = 1.0 / mass
 
 
-def up_kernel(rows, cols, mine, far, chip, mix, total_r, out):
+def up_kernel(rows, cols, mine, far, chip, mix, inverse, order_ref, out, fine, sems):
     lat = lax.axis_index("lat")
     last = lax.axis_size("lat") - 1
     lon_odd = lax.axis_index("lon") % 2
@@ -388,9 +393,7 @@
         for field in (west, mid, east):
             moved = field if a == 0 else pltpu.roll(field, width - a * cols, 1)
             shifted.append(moved[:, 0:cells])
-    src = lax.broadcasted_iota(jnp.int32, (UP * cols, UP * cols), 0)
-    dst = lax.broadcasted_iota(jnp.int32, (UP * cols, UP * cols), 1)
-    order = jnp.where((dst // UP == src % cols) & (dst % UP == src // cols), 1.0, 0.0).astype(BF16)
+    order = order_ref[...]
     tile = 128
     group = tile // cols
     lane = lax.broadcasted_iota(jnp.int32, (UP, tile), 1)
@@ -399,22 +402,27 @@
     while span < group:
         bits.append((span, (lane // (span * cols)) % 2 == 1))
         span *= 2
-    for d in range(2):
-        lanes_of = [[None] * (UP // group) for _ in range(rows)]
-        for t in range(cells // tile):
-            flows = [
-                jnp.broadcast_to(v[d : d + 1, t * tile : (t + 1) * tile], (UP, tile))
-                for v in shifted
-            ]
-            for u in range(UP // group):
-                block = []
-                for k in range(group):
-                    acc = None
-                    for n in range(9):
-                        term = mix[n, u * group + k, :, t * tile : (t + 1) * tile] * flows[n]
-                        acc = term if acc is None else acc + term
-                    part = total_r[u * group + k, :, t * tile : (t + 1) * tile]
-                    block.append(acc * part)
+    count = group * UP
+    copies = []
+    for t in range(cells // tile):
+        here = slice(t * tile, (t + 1) * tile)
+        flows = [
+            [jnp.broadcast_to(v[d : d + 1, here], (UP, tile)) for v in shifted] for d in range(2)
+        ]
+        lanes_of = [[[None] * (UP // group) for _ in range(group)] for _ in range(2)]
+        for u in range(UP // group):
+            blocks = [[], []]
+            for k in range(group):
+                at = u * group + k
+                scale = inverse[at, :, here]
+                weights = [mix[n, at, :, here] for n in range(9)]
+                for d in range(2):
+                    acc = weights[0] * flows[d][0]
+                    for n in range(1, 9):
+                        acc = acc + weights[n] * flows[d][n]
+                    blocks[d].append(acc * scale)
+            for d in range(2):
+                block = blocks[d]
                 for span, high in bits:
                     shift = span * cols
                     done = list(block)
@@ -428,13 +436,26 @@
                         )
                     block = done
                 for k in range(group):
-                    lanes_of[t * group + k][u] = block[k]
-        value = jnp.concatenate([jnp.concatenate(v, axis=1) for v in lanes_of], axis=0)
+                    lanes_of[d][k][u] = block[k]
+        value = jnp.concatenate(
+            [jnp.concatenate(v, axis=1) for d in range(2) for v in lanes_of[d]], axis=0
+        )
         high_part = value.astype(BF16)
         low_part = (value - high_part.astype(F32)).astype(BF16)
-        out[d] = jnp.dot(high_part, order, preferred_element_type=F32) + jnp.dot(
-            low_part, order, preferred_element_type=F32
+        both = jnp.dot(
+            jnp.concatenate([high_part, low_part], axis=0), order, preferred_element_type=F32
         )
+        both = both[0 : 2 * count] + both[2 * count :]
+        for d in range(2):
+            fine[d, t * count : (t + 1) * count] = both[d * count : (d + 1) * count]
+            part = pl.ds(t * count, count)
+            copy = pltpu.make_async_copy(
+                fine.at[d, part], out.at[d, part], sems.at[2 * t + d]
+            )
+            copy.start()
+            copies.append(copy)
+    for copy in copies:
+        copy.wait()
 
 
 def body(frame_one, frame_two, enc_weight, mask_weight):
@@ -484,7 +505,7 @@
         ],
         compiler_params=params(16),
         name="pack",
-    )(one, m_a, row_a, row_b, row_c, row_d)
+    )(one, m_b, row_a, row_b, row_c, row_d)
     col_x = lax.ppermute(m_x, "lon", far_lon)
 
     weight = enc_weight.reshape(9 * CH, CH)
@@ -513,18 +534,23 @@
             flops=2 * 9 * CH * CH * cols * (tall + few), bytes_accessed=4 << 20, transcendentals=0
         ),
         name="encode_own",
-    )(one, m_a, row_a, row_b, row_c, row_d, weight)
+    )(one, m_b, row_a, row_b, row_c, row_d, weight)
 
     col_in = lax.all_gather(m_in, "lon", axis_index_groups=chips)
     side_scratch = [
         pltpu.VMEM((n1, BC + 2 * BR, CH), F32),
         pltpu.VMEM((3, n1, BC, CH), BF16),
     ]
-    strip_in, two_in, first_in = pl.pallas_call(
+    strip_in, two_in, first_in, order = pl.pallas_call(
         functools.partial(strip_kernel, rows, cols),
-        out_shape=(array(few, BC, CH), array(tall, BC, CH), array(few, BC, CH)),
+        out_shape=(
+            array(few, BC, CH),
+            array(tall, BC, CH),
+            array(few, BC, CH),
+            array(UP * cols, UP * cols),
+        ),
         in_specs=[VMEM] * 7,
-        out_specs=(VMEM,) * 3,
+        out_specs=(VMEM,) * 4,
         scratch_shapes=side_scratch,
         compiler_params=params(16),
         cost_estimate=pl.CostEstimate(
@@ -566,11 +592,15 @@
     return pl.pallas_call(
         functools.partial(up_kernel, rows, cols),
         out_shape=array(2, rows * UP, cols * UP, dtype=F32),
-        in_specs=[VMEM] * 5,
-        out_specs=VMEM,
+        in_specs=[VMEM] * 6,
+        out_specs=pl.BlockSpec(memory_space=pl.ANY),
+        scratch_shapes=[
+            pltpu.VMEM((2, rows * UP, cols * UP), F32),
+            pltpu.SemaphoreType.DMA((2 * cells // 128,)),
+        ],
         compiler_params=params(16),
         name="upsample",
-    )(sums, sums_far, sums_in, mix, inverse)
+    )(sums, sums_far, sums_in, mix, inverse, order)
 
 
 def solution(mesh):

time: 56.2 us -> 56 us (level)
  blocking collectives: 15.2 us -> 18.4 us
  starting transfers between devices: 25.3 us -> 22.9 us
    ppermute x1, waiting for transfers between devices: 4.95 us -> 1.58 us  [body(): row_d = lax.ppermute(m_d, 'lat', low_lat)]
    ppermute x1, starting transfers between devices: 11.3 us -> 7.96 us  [body(): row_d = lax.ppermute(m_d, 'lat', low_lat)]
    ppermute x1, starting transfers between devices: 4.83 us -> 8.15 us  [body(): row_b = lax.ppermute(m_b, 'lat', near_lat)]
    ppermute x1, waiting for transfers between devices: 0.01 us -> 2.94 us  [body(): row_b = lax.ppermute(m_b, 'lat', near_lat)]
    all_gather x1, blocking collectives: 8.05 us -> 10.6 us  [body(): col_in = lax.all_gather(m_in, 'lon', axis_index_groups=chips)]
    ppermute x1, starting transfers between devices: 5.95 us -> 3.58 us  [body(): col_x = lax.ppermute(m_x, 'lon', far_lon)]
    all_gather x1, blocking collectives: 7.17 us -> 7.87 us  [body(): sums_in = lax.all_gather(sums_too, 'lon', axis_index_groups=chips)]
  transfers between devices with their start and end apart: 6 -> 6, of which waited for: 1 -> 2; matrix products, arithmetic and copies ran while one was open for 2% -> 2% of each run, Pallas kernels for 8% -> 8%
where the time goes in v6:
time: 56 us; the launch traced here: 55.7 us
  starting transfers between devices  22.9 us (41%)
  blocking collectives  18.4 us (33%)
  Pallas kernels  8.66 us (15%)
  waiting for transfers between devices  4.52 us (8%)
  local copies, waits for them, and re-layouts  1.03 us (2%)
    all_gather x1, blocking collectives, body(): col_in = lax.all_gather(m_in, 'lon', axis_index_groups=chips)  10.6 us
    ppermute x1, starting transfers between devices, body(): row_b = lax.ppermute(m_b, 'lat', near_lat)  8.15 us
    ppermute x1, starting transfers between devices, body(): row_d = lax.ppermute(m_d, 'lat', low_lat)  7.96 us
    all_gather x1, blocking collectives, body(): sums_in = lax.all_gather(sums_too, 'lon', axis_index_groups=chips)  7.87 us
    ppermute x1, starting transfers between devices, body(): col_x = lax.ppermute(m_x, 'lon', far_lon)  3.58 us
    pallas_call x1, Pallas kernels, body(): pl.pallas_call(functools.partial(own_kernel, rows, cols), out_shape=(arra...  3.08 us
    ppermute x1, waiting for transfers between devices, body(): row_b = lax.ppermute(m_b, 'lat', near_lat)  2.94 us
    ppermute x1, starting transfers between devices, body(): sums_far = lax.ppermute(sums, 'lon', far_lon)  1.92 us
  transfers between devices with their start and end apart: 6, of which 2 were waited for; matrix products, arithmetic and copies ran while one was open for 2% of the time, Pallas kernels for 8%

profile of v6, /device:TPU:1, one launch (start us, length us, event | category | flops | bytes accessed | tf_op | source)
XLA Modules:
  0.0 55.7 jit_solution(2086626357872627274)
XLA Ops:
  0.0 0.0 copy-start
  0.0 1.3 %edges.1 = (bf16[18,32,256]{2,1,0:T(8,128)(2,1)S(1)}, bf16[18,32,256]{2,1,0:T(8,128)(2,1)S(1)}, bf16[1,32,256]{2,1,0:T(8,128)(2,1)S(1)}, bf16[1,32,256]{2,1,0:T(8,128)(2,1)S(1)}, bf16[16,32,256]{2,1,0:T(8,128)(2,1)S(1)}) custom-call(bf16[16,32,256]{2,1,0:T(8,128)(2,1)} %f1.1, bf16[16,32,256]{2,1,0:T(8,128)(2,1)} %f2.1), custom_call_target="tpu_custom_call" | custom-call | tf_op jit(solution)/shard_map/edges/pallas_call | solution.py:479
  1.3 0.7 %collective-permute-start = (bf16[18,32,256]{2,1,0:T(8,128)(2,1)S(1)}, bf16[18,32,256]{2,1,0:T(8,128)(2,1)S(1)}, u32[]{:S(2)}, u32[]{:S(2)}) collective-permute-start(bf16[18,32,256]{2,1,0:T(8,128)(2,1)S(1)} %get-tuple-element.27), channel_id=1, source_target_pairs={{32,64},{64,32},{96,128},{128,96},{160,192},{192,160},{224,256},{2... | collective-permute-start | bytes 884744 | tf_op jit(solution)/shard_map/ppermute | solution.py:491
  2.0 8.2 %collective-permute-start.1 = (bf16[18,32,256]{2,1,0:T(8,128)(2,1)S(1)}, bf16[18,32,256]{2,1,0:T(8,128)(2,1)S(1)}, u32[]{:S(2)}, u32[]{:S(2)}) collective-permute-start(bf16[18,32,256]{2,1,0:T(8,128)(2,1)S(1)} %get-tuple-element.26.f2), channel_id=1, source_target_pairs={{0,32},{32,0},{64,96},{96,64},{128,160},{160,128},{192,224},{224,1... | collective-permute-start | bytes 884744 | tf_op jit(solution)/shard_map/ppermute | solution.py:492
  10.2 0.7 %collective-permute-start.2 = (bf16[1,32,256]{2,1,0:T(8,128)(2,1)S(1)}, bf16[1,32,256]{2,1,0:T(8,128)(2,1)S(1)}, u32[]{:S(2)}, u32[]{:S(2)}) collective-permute-start(bf16[1,32,256]{2,1,0:T(8,128)(2,1)S(1)} %get-tuple-element.28), channel_id=1, source_target_pairs={{64,128},{128,64},{96,160},{160,96},{192,256},{256,192},{224,288},... | collective-permute-start | bytes 49160 | tf_op jit(solution)/shard_map/ppermute | solution.py:493
  10.9 8.0 %collective-permute-start.3 = (bf16[1,32,256]{2,1,0:T(8,128)(2,1)S(1)}, bf16[1,32,256]{2,1,0:T(8,128)(2,1)S(1)}, u32[]{:S(2)}, u32[]{:S(2)}) collective-permute-start(bf16[1,32,256]{2,1,0:T(8,128)(2,1)S(1)} %get-tuple-element.29), channel_id=1, source_target_pairs={{0,64},{64,0},{32,96},{96,32},{128,192},{192,128},{160,224},{224,1... | collective-permute-start | bytes 49160 | tf_op jit(solution)/shard_map/ppermute | solution.py:494
  18.8 1.0 %copy.6 = bf16[256,9,8,8]{0,2,3,1:T(8,128)(2,1)S(1)} copy(bf16[256,9,8,8]{0,3,2,1:T(8,128)(2,1)} %bitcast.13) | data formatting | bytes 589824 | tf_op jit(solution)/shard_map/reshape | solution.py:575
  19.8 0.0 collective-permute-done.2.rc
  19.9 1.6 %collective-permute-done.3.rd = bf16[1,32,256]{2,1,0:T(8,128)(2,1)S(1)} collective-permute-done((bf16[1,32,256]{2,1,0:T(8,128)(2,1)S(1)}, bf16[1,32,256]{2,1,0:T(8,128)(2,1)S(1)}, u32[]{:S(2)}, u32[]{:S(2)}) %collective-permute-start.3) | collective-permute-done | bytes 16416 | tf_op jit(solution)/shard_map/ppermute | solution.py:494
  21.4 0.0 collective-permute-done.ra
  21.4 2.9 %collective-permute-done.1.rb = bf16[18,32,256]{2,1,0:T(8,128)(2,1)S(1)} collective-permute-done((bf16[18,32,256]{2,1,0:T(8,128)(2,1)S(1)}, bf16[18,32,256]{2,1,0:T(8,128)(2,1)S(1)}, u32[]{:S(2)}, u32[]{:S(2)}) %collective-permute-start.1) | collective-permute-done | bytes 294944 | tf_op jit(solution)/shard_map/ppermute | solution.py:492
  24.4 0.1 pack.1
  24.5 3.6 %collective-permute-start.4 = (bf16[26,16,256]{2,1,0:T(8,128)(2,1)S(1)}, bf16[26,16,256]{2,1,0:T(8,128)(2,1)S(1)}, u32[]{:S(2)}, u32[]{:S(2)}) collective-permute-start(bf16[26,16,256]{2,1,0:T(8,128)(2,1)S(1)} %pack.1), channel_id=1, source_target_pairs={{1,2},{2,1},{3,4},{4,3},{5,6},{6,5},{7,8},{8,7},{9,10},{10,9},{11,... | collective-permute-start | bytes 638984 | tf_op jit(solution)/shard_map/ppermute | solution.py:509
  28.1 0.0 copy-done
  28.1 3.1 %encode_own.1 = (bf16[48,32,256]{2,1,0:T(8,128)(2,1)S(1)}, bf16[18,32,256]{2,1,0:T(8,128)(2,1)S(1)}, f32[2,48,256]{2,1,0:T(8,128)S(1)}, f32[2,24,256]{2,1,0:T(8,...) custom-call(bf16[16,32,256]{2,1,0:T(8,128)(2,1)S(1)} %get-tuple-element.25.f1, ...), custom_call_target="tpu_custom_call" | custom-call | flops 2491416576 | bytes 4194304 | tf_op jit(solution)/shard_map/encode_own/pallas_call | solution.py:513
  31.2 10.6 %all-gather = bf16[52,16,256]{2,1,0:T(8,128)(2,1)S(1)} all-gather(bf16[26,16,256]{2,1,0:T(8,128)(2,1)S(1)} %get-tuple-element.35), channel_id=2, replica_groups={{0,1},{2,3},{4,5},{6,7},{8,9},{10,11},{12,13},{14,15},{16,17},{18,19},{..., dimensions={0}, use_global_device_ids=true | all-gather | bytes 638976 | tf_op jit(solution)/shard_map/all_gather | solution.py:539
  41.8 0.7 %strip.1 = (bf16[18,16,256]{2,1,0:T(8,128)(2,1)S(1)}, bf16[48,16,256]{2,1,0:T(8,128)(2,1)S(1)}, bf16[18,16,256]{2,1,0:T(8,128)(2,1)S(1)}, bf16[256,256]{1,0:T(8,128)(2,1)S(1)}) custom-call(bf16[48,32,256]{2,1,0:T(8,128)(2,1)S(1)} %get-tuple-element.30.o2, bf16[18,32,256]{2,1,0:T(8,128)(2,1)S(1)} %get-tuple-element.31.o1, ...), custom_call_target="tpu_custom_call" | custom-call | flops 339738624 | bytes 4194304 | tf_op jit(solution)/shard_map/strip/pallas_call | solution.py:544
  42.5 0.0 collective-permute-done.4.c_x
  42.5 1.7 %score.1 = (f32[8,640]{1,0:T(8,128)S(1)}, bf16[18,32,256]{2,1,0:T(8,128)(2,1)S(1)}) custom-call(bf16[48,32,256]{2,1,0:T(8,128)(2,1)S(1)} %get-tuple-element.30.o2, bf16[18,32,256]{2,1,0:T(8,128)(2,1)S(1)} %get-tuple-element.31.o1, f32[2,48,256]{2,1,0:T(8,128)S(1)} %get-tuple-element.32.ends2, f32[2,24,256]{2,1,0:T(8,128)S(1)} %get-tuple-element.33.ends1, ...), custom_call_target="tpu_custom_call" | custom-call | tf_op jit(solution)/shard_map/score/pallas_call | solution.py:563
  44.2 1.9 %collective-permute-start.5 = (f32[8,640]{1,0:T(8,128)S(1)}, f32[8,640]{1,0:T(8,128)S(1)}, u32[]{:S(2)}, u32[]{:S(2)}) collective-permute-start(f32[8,640]{1,0:T(8,128)S(1)} %get-tuple-element.39.sums.mine), channel_id=1, source_target_pairs={{1,2},{2,1},{3,4},{4,3},{5,6},{6,5},{7,8},{8,7},{9,10},{10,9},{11,... | collective-permute-start | bytes 61448 | tf_op jit(solution)/shard_map/ppermute | solution.py:573
  46.1 0.4 mix.1
  46.5 7.9 %all-gather.1 = f32[16,640]{1,0:T(8,128)S(1)} all-gather(f32[8,640]{1,0:T(8,128)S(1)} %get-tuple-element.41), channel_id=3, replica_groups={{0,1},{2,3},{4,5},{6,7},{8,9},{10,11},{12,13},{14,15},{16,17},{18,19},{..., dimensions={0}, use_global_device_ids=true | all-gather | bytes 61440 | tf_op jit(solution)/shard_map/all_gather | solution.py:591
  54.4 0.0 collective-permute-done.5.far
  54.4 1.3 %upsample.1 = f32[2,128,256]{2,1,0:T(8,128)} custom-call(f32[8,640]{1,0:T(8,128)S(1)} %get-tuple-element.39.sums.mine, f32[8,640]{1,0:T(8,128)S(1)} %collective-permute-done.5.far, f32[2,8,640]{2,1,0:T(8,128)S(1)} %bitcast.12, f32[9,8,8,512]{3,2,1,0:T(8,128)S(1)} %get-tuple-element.42.mix, f32[8,8,512]{2,1,0:T(8,128)S(1)} %get-tuple-element.43.inverse, ...), custom_call_target="tpu_custom_call" | custom-call | tf_op jit(solution)/shard_map/upsample/pallas_call | solution.py:592
Async XLA Ops:
  0.0 28.1 %copy-start = (bf16[3,3,256,256]{3,2,1,0:T(8,128)(2,1)S(1)}, bf16[3,3,256,256]{3,2,1,0:T(8,128)(2,1)}, u32[]{:S(2)}) copy-start(bf16[3,3,256,256]{3,2,1,0:T(8,128)(2,1)} %param.6) | copy-start | bytes 3538948
  1.3 20.1 %collective-permute-start = (bf16[18,32,256]{2,1,0:T(8,128)(2,1)S(1)}, bf16[18,32,256]{2,1,0:T(8,128)(2,1)S(1)}, u32[]{:S(2)}, u32[]{:S(2)}) collective-permute-start(bf16[18,32,256]{2,1,0:T(8,128)(2,1)S(1)} %get-tuple-element.27), channel_id=1, source_target_pairs={{32,64},{64,32},{96,128},{128,96},{160,192},{192,160},{224,256},{2... | collective-permute-start | bytes 884744 | tf_op jit(solution)/shard_map/ppermute | solution.py:491
  2.0 22.3 %collective-permute-start.1 = (bf16[18,32,256]{2,1,0:T(8,128)(2,1)S(1)}, bf16[18,32,256]{2,1,0:T(8,128)(2,1)S(1)}, u32[]{:S(2)}, u32[]{:S(2)}) collective-permute-start(bf16[18,32,256]{2,1,0:T(8,128)(2,1)S(1)} %get-tuple-element.26.f2), channel_id=1, source_target_pairs={{0,32},{32,0},{64,96},{96,64},{128,160},{160,128},{192,224},{224,1... | collective-permute-start | bytes 884744 | tf_op jit(solution)/shard_map/ppermute | solution.py:492
  10.2 9.7 %collective-permute-start.2 = (bf16[1,32,256]{2,1,0:T(8,128)(2,1)S(1)}, bf16[1,32,256]{2,1,0:T(8,128)(2,1)S(1)}, u32[]{:S(2)}, u32[]{:S(2)}) collective-permute-start(bf16[1,32,256]{2,1,0:T(8,128)(2,1)S(1)} %get-tuple-element.28), channel_id=1, source_target_pairs={{64,128},{128,64},{96,160},{160,96},{192,256},{256,192},{224,288},... | collective-permute-start | bytes 49160 | tf_op jit(solution)/shard_map/ppermute | solution.py:493
  10.9 10.6 %collective-permute-start.3 = (bf16[1,32,256]{2,1,0:T(8,128)(2,1)S(1)}, bf16[1,32,256]{2,1,0:T(8,128)(2,1)S(1)}, u32[]{:S(2)}, u32[]{:S(2)}) collective-permute-start(bf16[1,32,256]{2,1,0:T(8,128)(2,1)S(1)} %get-tuple-element.29), channel_id=1, source_target_pairs={{0,64},{64,0},{32,96},{96,32},{128,192},{192,128},{160,224},{224,1... | collective-permute-start | bytes 49160 | tf_op jit(solution)/shard_map/ppermute | solution.py:494
  24.5 18.0 %collective-permute-start.4 = (bf16[26,16,256]{2,1,0:T(8,128)(2,1)S(1)}, bf16[26,16,256]{2,1,0:T(8,128)(2,1)S(1)}, u32[]{:S(2)}, u32[]{:S(2)}) collective-permute-start(bf16[26,16,256]{2,1,0:T(8,128)(2,1)S(1)} %pack.1), channel_id=1, source_target_pairs={{1,2},{2,1},{3,4},{4,3},{5,6},{6,5},{7,8},{8,7},{9,10},{10,9},{11,... | collective-permute-start | bytes 638984 | tf_op jit(solution)/shard_map/ppermute | solution.py:509
  44.2 10.2 %collective-permute-start.5 = (f32[8,640]{1,0:T(8,128)S(1)}, f32[8,640]{1,0:T(8,128)S(1)}, u32[]{:S(2)}, u32[]{:S(2)}) collective-permute-start(f32[8,640]{1,0:T(8,128)S(1)} %get-tuple-element.39.sums.mine), channel_id=1, source_target_pairs={{1,2},{2,1},{3,4},{4,3},{5,6},{6,5},{7,8},{8,7},{9,10},{10,9},{11,... | collective-permute-start | bytes 61448 | tf_op jit(solution)/shard_map/ppermute | solution.py:573

commit v7 on v6

--- a/solution.py
+++ b/solution.py
@@ -39,25 +39,17 @@
     band = lax.axis_index("lat")
     odd = band % 2
     upper = band % 4 // 2
-    copies = []
-    for k, (msg, low) in enumerate(((m_a, odd), (m_b, 1 - odd))):
-        copies.append(
-            pltpu.make_async_copy(f2, msg.at[pl.ds(0, rows)], sems.at[2 * k])
-        )
-        copies.append(
-            pltpu.make_async_copy(
-                f1.at[pl.ds(low * (rows - 2), 2)], msg.at[pl.ds(rows, 2)], sems.at[1 + 2 * k]
-            )
-        )
-    for k, (msg, low) in enumerate(((m_c, upper), (m_d, 1 - upper))):
-        copies.append(
-            pltpu.make_async_copy(f2.at[pl.ds(low * (rows - 1), 1)], msg, sems.at[4 + k])
-        )
-    copies.append(pltpu.make_async_copy(f1, g1, sems.at[6]))
-    for copy in copies:
-        copy.start()
-    for copy in copies:
-        copy.wait()
+    second = pltpu.make_async_copy(f2, m_a.at[pl.ds(0, rows)], sems.at[0])
+    first = pltpu.make_async_copy(f1, g1, sems.at[1])
+    second.start()
+    first.start()
+    second.wait()
+    m_b[0:rows] = m_a[0:rows]
+    for msg, low in ((m_c, upper), (m_d, 1 - upper)):
+        msg[...] = m_a[pl.ds(low * (rows - 1), 1)]
+    first.wait()
+    for msg, low in ((m_a, odd), (m_b, 1 - odd)):
+        msg[rows : rows + 2] = g1[pl.ds(low * (rows - 2), 2)]
 
 
 def by_parity(lat_run, ra, rb, rc, rd):
@@ -448,12 +440,10 @@
         both = both[0 : 2 * count] + both[2 * count :]
         for d in range(2):
             fine[d, t * count : (t + 1) * count] = both[d * count : (d + 1) * count]
-            part = pl.ds(t * count, count)
-            copy = pltpu.make_async_copy(
-                fine.at[d, part], out.at[d, part], sems.at[2 * t + d]
-            )
-            copy.start()
-            copies.append(copy)
+        part = pl.ds(t * count, count)
+        copy = pltpu.make_async_copy(fine.at[:, part], out.at[:, part], sems.at[t])
+        copy.start()
+        copies.append(copy)
     for copy in copies:
         copy.wait()
 
@@ -481,7 +471,7 @@
         out_shape=(array(few, cols, CH),) * 2 + (array(1, cols, CH),) * 2 + (tile,),
         in_specs=[pl.BlockSpec(memory_space=pltpu.MemorySpace.HBM)] * 2,
         out_specs=(VMEM,) * 5,
-        scratch_shapes=[pltpu.SemaphoreType.DMA((7,))],
+        scratch_shapes=[pltpu.SemaphoreType.DMA((2,))],
         compiler_params=params(8),
         name="edges",
     )(
@@ -596,7 +586,7 @@
         out_specs=pl.BlockSpec(memory_space=pl.ANY),
         scratch_shapes=[
             pltpu.VMEM((2, rows * UP, cols * UP), F32),
-            pltpu.SemaphoreType.DMA((2 * cells // 128,)),
+            pltpu.SemaphoreType.DMA((cells // 128,)),
         ],
         compiler_params=params(16),
         name="upsample",

time: 56 us -> 55.8 us (level)
  no operation moved by 1% of the time
where the time goes in v7:
time: 55.8 us; the launch traced here: 55.5 us
  starting transfers between devices  22.9 us (41%)
  blocking collectives  18.4 us (33%)
  Pallas kernels  8.48 us (15%)
  waiting for transfers between devices  4.52 us (8%)
  local copies, waits for them, and re-layouts  1.03 us (2%)
    all_gather x1, blocking collectives, body(): col_in = lax.all_gather(m_in, 'lon', axis_index_groups=chips)  10.5 us
    ppermute x1, starting transfers between devices, body(): row_b = lax.ppermute(m_b, 'lat', near_lat)  8.15 us
    ppermute x1, starting transfers between devices, body(): row_d = lax.ppermute(m_d, 'lat', low_lat)  7.96 us
    all_gather x1, blocking collectives, body(): sums_in = lax.all_gather(sums_too, 'lon', axis_index_groups=chips)  7.88 us
    ppermute x1, starting transfers between devices, body(): col_x = lax.ppermute(m_x, 'lon', far_lon)  3.58 us
    pallas_call x1, Pallas kernels, body(): pl.pallas_call(functools.partial(own_kernel, rows, cols), out_shape=(arra...  3.09 us
    ppermute x1, waiting for transfers between devices, body(): row_b = lax.ppermute(m_b, 'lat', near_lat)  2.94 us
    ppermute x1, starting transfers between devices, body(): sums_far = lax.ppermute(sums, 'lon', far_lon)  1.92 us
  transfers between devices with their start and end apart: 6, of which 2 were waited for; matrix products, arithmetic and copies ran while one was open for 2% of the time, Pallas kernels for 8%

profile of v7, /device:TPU:1, one launch (start us, length us, event | category | flops | bytes accessed | tf_op | source)
XLA Modules:
  0.0 55.5 jit_solution(958314078709012672)
XLA Ops:
  0.0 0.0 copy-start
  0.0 1.1 %edges.1 = (bf16[18,32,256]{2,1,0:T(8,128)(2,1)S(1)}, bf16[18,32,256]{2,1,0:T(8,128)(2,1)S(1)}, bf16[1,32,256]{2,1,0:T(8,128)(2,1)S(1)}, bf16[1,32,256]{2,1,0:T(8,128)(2,1)S(1)}, bf16[16,32,256]{2,1,0:T(8,128)(2,1)S(1)}) custom-call(bf16[16,32,256]{2,1,0:T(8,128)(2,1)} %f1.1, bf16[16,32,256]{2,1,0:T(8,128)(2,1)} %f2.1), custom_call_target="tpu_custom_call" | custom-call | tf_op jit(solution)/shard_map/edges/pallas_call | solution.py:469
  1.2 0.7 %collective-permute-start = (bf16[18,32,256]{2,1,0:T(8,128)(2,1)S(1)}, bf16[18,32,256]{2,1,0:T(8,128)(2,1)S(1)}, u32[]{:S(2)}, u32[]{:S(2)}) collective-permute-start(bf16[18,32,256]{2,1,0:T(8,128)(2,1)S(1)} %get-tuple-element.27), channel_id=1, source_target_pairs={{32,64},{64,32},{96,128},{128,96},{160,192},{192,160},{224,256},{2... | collective-permute-start | bytes 884744 | tf_op jit(solution)/shard_map/ppermute | solution.py:481
  1.8 8.2 %collective-permute-start.1 = (bf16[18,32,256]{2,1,0:T(8,128)(2,1)S(1)}, bf16[18,32,256]{2,1,0:T(8,128)(2,1)S(1)}, u32[]{:S(2)}, u32[]{:S(2)}) collective-permute-start(bf16[18,32,256]{2,1,0:T(8,128)(2,1)S(1)} %get-tuple-element.26.f2), channel_id=1, source_target_pairs={{0,32},{32,0},{64,96},{96,64},{128,160},{160,128},{192,224},{224,1... | collective-permute-start | bytes 884744 | tf_op jit(solution)/shard_map/ppermute | solution.py:482
  10.0 0.7 %collective-permute-start.2 = (bf16[1,32,256]{2,1,0:T(8,128)(2,1)S(1)}, bf16[1,32,256]{2,1,0:T(8,128)(2,1)S(1)}, u32[]{:S(2)}, u32[]{:S(2)}) collective-permute-start(bf16[1,32,256]{2,1,0:T(8,128)(2,1)S(1)} %get-tuple-element.28), channel_id=1, source_target_pairs={{64,128},{128,64},{96,160},{160,96},{192,256},{256,192},{224,288},... | collective-permute-start | bytes 49160 | tf_op jit(solution)/shard_map/ppermute | solution.py:483
  10.7 8.0 %collective-permute-start.3 = (bf16[1,32,256]{2,1,0:T(8,128)(2,1)S(1)}, bf16[1,32,256]{2,1,0:T(8,128)(2,1)S(1)}, u32[]{:S(2)}, u32[]{:S(2)}) collective-permute-start(bf16[1,32,256]{2,1,0:T(8,128)(2,1)S(1)} %get-tuple-element.29), channel_id=1, source_target_pairs={{0,64},{64,0},{32,96},{96,32},{128,192},{192,128},{160,224},{224,1... | collective-permute-start | bytes 49160 | tf_op jit(solution)/shard_map/ppermute | solution.py:484
  18.6 1.0 %copy.6 = bf16[256,9,8,8]{0,2,3,1:T(8,128)(2,1)S(1)} copy(bf16[256,9,8,8]{0,3,2,1:T(8,128)(2,1)} %bitcast.13) | data formatting | bytes 589824 | tf_op jit(solution)/shard_map/reshape | solution.py:565
  19.7 0.0 collective-permute-done.2.rc
  19.7 1.6 %collective-permute-done.3.rd = bf16[1,32,256]{2,1,0:T(8,128)(2,1)S(1)} collective-permute-done((bf16[1,32,256]{2,1,0:T(8,128)(2,1)S(1)}, bf16[1,32,256]{2,1,0:T(8,128)(2,1)S(1)}, u32[]{:S(2)}, u32[]{:S(2)}) %collective-permute-start.3) | collective-permute-done | bytes 16416 | tf_op jit(solution)/shard_map/ppermute | solution.py:484
  21.2 0.0 collective-permute-done.ra
  21.3 2.9 %collective-permute-done.1.rb = bf16[18,32,256]{2,1,0:T(8,128)(2,1)S(1)} collective-permute-done((bf16[18,32,256]{2,1,0:T(8,128)(2,1)S(1)}, bf16[18,32,256]{2,1,0:T(8,128)(2,1)S(1)}, u32[]{:S(2)}, u32[]{:S(2)}) %collective-permute-start.1) | collective-permute-done | bytes 294944 | tf_op jit(solution)/shard_map/ppermute | solution.py:482
  24.2 0.1 pack.1
  24.3 3.6 %collective-permute-start.4 = (bf16[26,16,256]{2,1,0:T(8,128)(2,1)S(1)}, bf16[26,16,256]{2,1,0:T(8,128)(2,1)S(1)}, u32[]{:S(2)}, u32[]{:S(2)}) collective-permute-start(bf16[26,16,256]{2,1,0:T(8,128)(2,1)S(1)} %pack.1), channel_id=1, source_target_pairs={{1,2},{2,1},{3,4},{4,3},{5,6},{6,5},{7,8},{8,7},{9,10},{10,9},{11,... | collective-permute-start | bytes 638984 | tf_op jit(solution)/shard_map/ppermute | solution.py:499
  27.9 0.0 copy-done
  27.9 3.1 %encode_own.1 = (bf16[48,32,256]{2,1,0:T(8,128)(2,1)S(1)}, bf16[18,32,256]{2,1,0:T(8,128)(2,1)S(1)}, f32[2,48,256]{2,1,0:T(8,128)S(1)}, f32[2,24,256]{2,1,0:T(8,...) custom-call(bf16[16,32,256]{2,1,0:T(8,128)(2,1)S(1)} %get-tuple-element.25.f1, ...), custom_call_target="tpu_custom_call" | custom-call | flops 2491416576 | bytes 4194304 | tf_op jit(solution)/shard_map/encode_own/pallas_call | solution.py:503
  31.0 10.5 %all-gather = bf16[52,16,256]{2,1,0:T(8,128)(2,1)S(1)} all-gather(bf16[26,16,256]{2,1,0:T(8,128)(2,1)S(1)} %get-tuple-element.35), channel_id=2, replica_groups={{0,1},{2,3},{4,5},{6,7},{8,9},{10,11},{12,13},{14,15},{16,17},{18,19},{..., dimensions={0}, use_global_device_ids=true | all-gather | bytes 638976 | tf_op jit(solution)/shard_map/all_gather | solution.py:529
  41.6 0.7 %strip.1 = (bf16[18,16,256]{2,1,0:T(8,128)(2,1)S(1)}, bf16[48,16,256]{2,1,0:T(8,128)(2,1)S(1)}, bf16[18,16,256]{2,1,0:T(8,128)(2,1)S(1)}, bf16[256,256]{1,0:T(8,128)(2,1)S(1)}) custom-call(bf16[48,32,256]{2,1,0:T(8,128)(2,1)S(1)} %get-tuple-element.30.o2, bf16[18,32,256]{2,1,0:T(8,128)(2,1)S(1)} %get-tuple-element.31.o1, ...), custom_call_target="tpu_custom_call" | custom-call | flops 339738624 | bytes 4194304 | tf_op jit(solution)/shard_map/strip/pallas_call | solution.py:534
  42.3 0.0 collective-permute-done.4.c_x
  42.3 1.7 %score.1 = (f32[8,640]{1,0:T(8,128)S(1)}, bf16[18,32,256]{2,1,0:T(8,128)(2,1)S(1)}) custom-call(bf16[48,32,256]{2,1,0:T(8,128)(2,1)S(1)} %get-tuple-element.30.o2, bf16[18,32,256]{2,1,0:T(8,128)(2,1)S(1)} %get-tuple-element.31.o1, f32[2,48,256]{2,1,0:T(8,128)S(1)} %get-tuple-element.32.ends2, f32[2,24,256]{2,1,0:T(8,128)S(1)} %get-tuple-element.33.ends1, ...), custom_call_target="tpu_custom_call" | custom-call | tf_op jit(solution)/shard_map/score/pallas_call | solution.py:553
  44.0 1.9 %collective-permute-start.5 = (f32[8,640]{1,0:T(8,128)S(1)}, f32[8,640]{1,0:T(8,128)S(1)}, u32[]{:S(2)}, u32[]{:S(2)}) collective-permute-start(f32[8,640]{1,0:T(8,128)S(1)} %get-tuple-element.39.sums.mine), channel_id=1, source_target_pairs={{1,2},{2,1},{3,4},{4,3},{5,6},{6,5},{7,8},{8,7},{9,10},{10,9},{11,... | collective-permute-start | bytes 61448 | tf_op jit(solution)/shard_map/ppermute | solution.py:563
  45.9 0.4 mix.1
  46.3 7.9 %all-gather.1 = f32[16,640]{1,0:T(8,128)S(1)} all-gather(f32[8,640]{1,0:T(8,128)S(1)} %get-tuple-element.41), channel_id=3, replica_groups={{0,1},{2,3},{4,5},{6,7},{8,9},{10,11},{12,13},{14,15},{16,17},{18,19},{..., dimensions={0}, use_global_device_ids=true | all-gather | bytes 61440 | tf_op jit(solution)/shard_map/all_gather | solution.py:581
  54.2 0.0 collective-permute-done.5.far
  54.2 1.3 %upsample.1 = f32[2,128,256]{2,1,0:T(8,128)} custom-call(f32[8,640]{1,0:T(8,128)S(1)} %get-tuple-element.39.sums.mine, f32[8,640]{1,0:T(8,128)S(1)} %collective-permute-done.5.far, f32[2,8,640]{2,1,0:T(8,128)S(1)} %bitcast.12, f32[9,8,8,512]{3,2,1,0:T(8,128)S(1)} %get-tuple-element.42.mix, f32[8,8,512]{2,1,0:T(8,128)S(1)} %get-tuple-element.43.inverse, ...), custom_call_target="tpu_custom_call" | custom-call | tf_op jit(solution)/shard_map/upsample/pallas_call | solution.py:582
Async XLA Ops:
  0.0 27.9 %copy-start = (bf16[3,3,256,256]{3,2,1,0:T(8,128)(2,1)S(1)}, bf16[3,3,256,256]{3,2,1,0:T(8,128)(2,1)}, u32[]{:S(2)}) copy-start(bf16[3,3,256,256]{3,2,1,0:T(8,128)(2,1)} %param.6) | copy-start | bytes 3538948
  1.2 20.1 %collective-permute-start = (bf16[18,32,256]{2,1,0:T(8,128)(2,1)S(1)}, bf16[18,32,256]{2,1,0:T(8,128)(2,1)S(1)}, u32[]{:S(2)}, u32[]{:S(2)}) collective-permute-start(bf16[18,32,256]{2,1,0:T(8,128)(2,1)S(1)} %get-tuple-element.27), channel_id=1, source_target_pairs={{32,64},{64,32},{96,128},{128,96},{160,192},{192,160},{224,256},{2... | collective-permute-start | bytes 884744 | tf_op jit(solution)/shard_map/ppermute | solution.py:481
  1.8 22.3 %collective-permute-start.1 = (bf16[18,32,256]{2,1,0:T(8,128)(2,1)S(1)}, bf16[18,32,256]{2,1,0:T(8,128)(2,1)S(1)}, u32[]{:S(2)}, u32[]{:S(2)}) collective-permute-start(bf16[18,32,256]{2,1,0:T(8,128)(2,1)S(1)} %get-tuple-element.26.f2), channel_id=1, source_target_pairs={{0,32},{32,0},{64,96},{96,64},{128,160},{160,128},{192,224},{224,1... | collective-permute-start | bytes 884744 | tf_op jit(solution)/shard_map/ppermute | solution.py:482
  10.0 9.7 %collective-permute-start.2 = (bf16[1,32,256]{2,1,0:T(8,128)(2,1)S(1)}, bf16[1,32,256]{2,1,0:T(8,128)(2,1)S(1)}, u32[]{:S(2)}, u32[]{:S(2)}) collective-permute-start(bf16[1,32,256]{2,1,0:T(8,128)(2,1)S(1)} %get-tuple-element.28), channel_id=1, source_target_pairs={{64,128},{128,64},{96,160},{160,96},{192,256},{256,192},{224,288},... | collective-permute-start | bytes 49160 | tf_op jit(solution)/shard_map/ppermute | solution.py:483
  10.7 10.6 %collective-permute-start.3 = (bf16[1,32,256]{2,1,0:T(8,128)(2,1)S(1)}, bf16[1,32,256]{2,1,0:T(8,128)(2,1)S(1)}, u32[]{:S(2)}, u32[]{:S(2)}) collective-permute-start(bf16[1,32,256]{2,1,0:T(8,128)(2,1)S(1)} %get-tuple-element.29), channel_id=1, source_target_pairs={{0,64},{64,0},{32,96},{96,32},{128,192},{192,128},{160,224},{224,1... | collective-permute-start | bytes 49160 | tf_op jit(solution)/shard_map/ppermute | solution.py:484
  24.3 18.0 %collective-permute-start.4 = (bf16[26,16,256]{2,1,0:T(8,128)(2,1)S(1)}, bf16[26,16,256]{2,1,0:T(8,128)(2,1)S(1)}, u32[]{:S(2)}, u32[]{:S(2)}) collective-permute-start(bf16[26,16,256]{2,1,0:T(8,128)(2,1)S(1)} %pack.1), channel_id=1, source_target_pairs={{1,2},{2,1},{3,4},{4,3},{5,6},{6,5},{7,8},{8,7},{9,10},{10,9},{11,... | collective-permute-start | bytes 638984 | tf_op jit(solution)/shard_map/ppermute | solution.py:499
  44.0 10.2 %collective-permute-start.5 = (f32[8,640]{1,0:T(8,128)S(1)}, f32[8,640]{1,0:T(8,128)S(1)}, u32[]{:S(2)}, u32[]{:S(2)}) collective-permute-start(f32[8,640]{1,0:T(8,128)S(1)} %get-tuple-element.39.sums.mine), channel_id=1, source_target_pairs={{1,2},{2,1},{3,4},{4,3},{5,6},{6,5},{7,8},{8,7},{9,10},{10,9},{11,... | collective-permute-start | bytes 61448 | tf_op jit(solution)/shard_map/ppermute | solution.py:563

commit v8 on v7

--- a/solution.py
+++ b/solution.py
@@ -65,12 +65,10 @@
 
 def edge(msg, main_cols, extra, rim, col):
     n1, n2 = main_cols.shape[0], rim.shape[0]
-    slots1, slots2 = -(-n1 // BC), -(-n2 // BC)
     msg[0:n1] = main_cols
     col[0:n1] = extra
-    msg[n1 : n1 + slots1] = col[0 : slots1 * BC].astype(BF16).reshape(slots1, BC, CH)
-    col[0:n2] = rim
-    msg[n1 + slots1 :] = col[0 : slots2 * BC].astype(BF16).reshape(slots2, BC, CH)
+    col[n1 : n1 + n2] = rim
+    msg[n1:] = col[...].astype(BF16).reshape(-1, BC, CH)
 
 
 def edge_places(cols, right):
@@ -167,11 +165,10 @@
 def finish_side(rows, cols, side, msg, w, o2, o1, ends2, ends1, edges, ext, xs, put):
     n2 = 3 * rows + 2
     n1 = rows + 4
-    slots2 = -(-n2 // BC)
-    slots1 = -(-n1 // BC)
     few, tall = rows + 2, 3 * rows
-    extra = msg[n1 : n1 + slots1].astype(F32).reshape(slots1 * BC, CH)[0:n1]
-    rim = msg[n1 + slots1 :].astype(F32).reshape(slots2 * BC, CH)[0:n2].astype(BF16)
+    singles = msg[n1:].astype(F32).reshape(-1, CH)
+    extra = singles[0:n1]
+    rim = singles[n1 : n1 + n2].astype(BF16)
     inner = edges[side, 0:n1]
     ext[:, BR : BR + BC] = msg[0:n1].astype(F32)
     ext[:, BR - 1 : BR] = (inner if side else extra)[:, None, :]
@@ -452,8 +449,8 @@
     rows, cols = frame_one.shape[0], frame_one.shape[1]
     cells = rows * cols
     n2, n1, few, tall = 3 * rows + 2, rows + 4, rows + 2, 3 * rows
-    n2_pad = -(-n2 // BC) * BC
-    slots = n1 + n2_pad // BC + -(-n1 // BC)
+    singles = -(-(n1 + n2) // BC) * BC
+    slots = n1 + singles // BC
     lats, lons = lax.axis_size("lat"), lax.axis_size("lon")
     far_lat = pair_perm(lats, 1, False)
     near_lat = pair_perm(lats, 0, False)
@@ -491,7 +488,7 @@
         scratch_shapes=[
             pltpu.VMEM((n1, cols, CH), BF16),
             pltpu.VMEM((n2, cols, CH), BF16),
-            pltpu.VMEM((n2_pad, CH), F32),
+            pltpu.VMEM((singles, CH), F32),
         ],
         compiler_params=params(16),
         name="pack",
@@ -517,7 +514,7 @@
             pltpu.VMEM((n1, cols + 2 * BR, CH), F32),
             pltpu.VMEM((3, n2, cols, CH), BF16),
             pltpu.VMEM((3, n1, cols, CH), BF16),
-            pltpu.VMEM((n2_pad, CH), F32),
+            pltpu.VMEM((singles, CH), F32),
         ],
         compiler_params=params(24),
         cost_estimate=pl.CostEstimate(

time: 55.8 us -> 55.7 us (level)
  no operation moved by 1% of the time
where the time goes in v8:
time: 55.7 us; the launch traced here: 55.3 us
  starting transfers between devices  22.9 us (41%)
  blocking collectives  18.3 us (33%)
  Pallas kernels  8.48 us (15%)
  waiting for transfers between devices  4.52 us (8%)
  local copies, waits for them, and re-layouts  1.03 us (2%)
    all_gather x1, blocking collectives, body(): col_in = lax.all_gather(m_in, 'lon', axis_index_groups=chips)  10.5 us
    ppermute x1, starting transfers between devices, body(): row_b = lax.ppermute(m_b, 'lat', near_lat)  8.15 us
    ppermute x1, starting transfers between devices, body(): row_d = lax.ppermute(m_d, 'lat', low_lat)  7.96 us
    all_gather x1, blocking collectives, body(): sums_in = lax.all_gather(sums_too, 'lon', axis_index_groups=chips)  7.71 us
    ppermute x1, starting transfers between devices, body(): col_x = lax.ppermute(m_x, 'lon', far_lon)  3.58 us
    pallas_call x1, Pallas kernels, body(): pl.pallas_call(functools.partial(own_kernel, rows, cols), out_shape=(arra...  3.09 us
    ppermute x1, waiting for transfers between devices, body(): row_b = lax.ppermute(m_b, 'lat', near_lat)  2.94 us
    ppermute x1, starting transfers between devices, body(): sums_far = lax.ppermute(sums, 'lon', far_lon)  1.92 us
  transfers between devices with their start and end apart: 6, of which 2 were waited for; matrix products, arithmetic and copies ran while one was open for 2% of the time, Pallas kernels for 8%

profile of v8, /device:TPU:1, one launch (start us, length us, event | category | flops | bytes accessed | tf_op | source)
XLA Modules:
  0.0 55.3 jit_solution(5778035986127213595)
XLA Ops:
  0.0 0.0 copy-start
  0.0 1.1 %edges.1 = (bf16[18,32,256]{2,1,0:T(8,128)(2,1)S(1)}, bf16[18,32,256]{2,1,0:T(8,128)(2,1)S(1)}, bf16[1,32,256]{2,1,0:T(8,128)(2,1)S(1)}, bf16[1,32,256]{2,1,0:T(8,128)(2,1)S(1)}, bf16[16,32,256]{2,1,0:T(8,128)(2,1)S(1)}) custom-call(bf16[16,32,256]{2,1,0:T(8,128)(2,1)} %f1.1, bf16[16,32,256]{2,1,0:T(8,128)(2,1)} %f2.1), custom_call_target="tpu_custom_call" | custom-call | tf_op jit(solution)/shard_map/edges/pallas_call | solution.py:466
  1.2 0.7 %collective-permute-start = (bf16[18,32,256]{2,1,0:T(8,128)(2,1)S(1)}, bf16[18,32,256]{2,1,0:T(8,128)(2,1)S(1)}, u32[]{:S(2)}, u32[]{:S(2)}) collective-permute-start(bf16[18,32,256]{2,1,0:T(8,128)(2,1)S(1)} %get-tuple-element.27), channel_id=1, source_target_pairs={{32,64},{64,32},{96,128},{128,96},{160,192},{192,160},{224,256},{2... | collective-permute-start | bytes 884744 | tf_op jit(solution)/shard_map/ppermute | solution.py:478
  1.8 8.2 %collective-permute-start.1 = (bf16[18,32,256]{2,1,0:T(8,128)(2,1)S(1)}, bf16[18,32,256]{2,1,0:T(8,128)(2,1)S(1)}, u32[]{:S(2)}, u32[]{:S(2)}) collective-permute-start(bf16[18,32,256]{2,1,0:T(8,128)(2,1)S(1)} %get-tuple-element.26.f2), channel_id=1, source_target_pairs={{0,32},{32,0},{64,96},{96,64},{128,160},{160,128},{192,224},{224,1... | collective-permute-start | bytes 884744 | tf_op jit(solution)/shard_map/ppermute | solution.py:479
  10.0 0.7 %collective-permute-start.2 = (bf16[1,32,256]{2,1,0:T(8,128)(2,1)S(1)}, bf16[1,32,256]{2,1,0:T(8,128)(2,1)S(1)}, u32[]{:S(2)}, u32[]{:S(2)}) collective-permute-start(bf16[1,32,256]{2,1,0:T(8,128)(2,1)S(1)} %get-tuple-element.28), channel_id=1, source_target_pairs={{64,128},{128,64},{96,160},{160,96},{192,256},{256,192},{224,288},... | collective-permute-start | bytes 49160 | tf_op jit(solution)/shard_map/ppermute | solution.py:480
  10.7 8.0 %collective-permute-start.3 = (bf16[1,32,256]{2,1,0:T(8,128)(2,1)S(1)}, bf16[1,32,256]{2,1,0:T(8,128)(2,1)S(1)}, u32[]{:S(2)}, u32[]{:S(2)}) collective-permute-start(bf16[1,32,256]{2,1,0:T(8,128)(2,1)S(1)} %get-tuple-element.29), channel_id=1, source_target_pairs={{0,64},{64,0},{32,96},{96,32},{128,192},{192,128},{160,224},{224,1... | collective-permute-start | bytes 49160 | tf_op jit(solution)/shard_map/ppermute | solution.py:481
  18.6 1.0 %copy.6 = bf16[256,9,8,8]{0,2,3,1:T(8,128)(2,1)S(1)} copy(bf16[256,9,8,8]{0,3,2,1:T(8,128)(2,1)} %bitcast.13) | data formatting | bytes 589824 | tf_op jit(solution)/shard_map/reshape | solution.py:562
  19.7 0.0 collective-permute-done.2.rc
  19.7 1.6 %collective-permute-done.3.rd = bf16[1,32,256]{2,1,0:T(8,128)(2,1)S(1)} collective-permute-done((bf16[1,32,256]{2,1,0:T(8,128)(2,1)S(1)}, bf16[1,32,256]{2,1,0:T(8,128)(2,1)S(1)}, u32[]{:S(2)}, u32[]{:S(2)}) %collective-permute-start.3) | collective-permute-done | bytes 16416 | tf_op jit(solution)/shard_map/ppermute | solution.py:481
  21.2 0.0 collective-permute-done.ra
  21.3 2.9 %collective-permute-done.1.rb = bf16[18,32,256]{2,1,0:T(8,128)(2,1)S(1)} collective-permute-done((bf16[18,32,256]{2,1,0:T(8,128)(2,1)S(1)}, bf16[18,32,256]{2,1,0:T(8,128)(2,1)S(1)}, u32[]{:S(2)}, u32[]{:S(2)}) %collective-permute-start.1) | collective-permute-done | bytes 294944 | tf_op jit(solution)/shard_map/ppermute | solution.py:479
  24.2 0.1 pack.1
  24.3 3.6 %collective-permute-start.4 = (bf16[25,16,256]{2,1,0:T(8,128)(2,1)S(1)}, bf16[25,16,256]{2,1,0:T(8,128)(2,1)S(1)}, u32[]{:S(2)}, u32[]{:S(2)}) collective-permute-start(bf16[25,16,256]{2,1,0:T(8,128)(2,1)S(1)} %pack.1), channel_id=1, source_target_pairs={{1,2},{2,1},{3,4},{4,3},{5,6},{6,5},{7,8},{8,7},{9,10},{10,9},{11,... | collective-permute-start | bytes 614408 | tf_op jit(solution)/shard_map/ppermute | solution.py:496
  27.9 0.0 copy-done
  27.9 3.1 %encode_own.1 = (bf16[48,32,256]{2,1,0:T(8,128)(2,1)S(1)}, bf16[18,32,256]{2,1,0:T(8,128)(2,1)S(1)}, f32[2,48,256]{2,1,0:T(8,128)S(1)}, f32[2,24,256]{2,1,0:T(8,...) custom-call(bf16[16,32,256]{2,1,0:T(8,128)(2,1)S(1)} %get-tuple-element.25.f1, ...), custom_call_target="tpu_custom_call" | custom-call | flops 2491416576 | bytes 4194304 | tf_op jit(solution)/shard_map/encode_own/pallas_call | solution.py:500
  31.0 10.5 %all-gather = bf16[50,16,256]{2,1,0:T(8,128)(2,1)S(1)} all-gather(bf16[25,16,256]{2,1,0:T(8,128)(2,1)S(1)} %get-tuple-element.35), channel_id=2, replica_groups={{0,1},{2,3},{4,5},{6,7},{8,9},{10,11},{12,13},{14,15},{16,17},{18,19},{..., dimensions={0}, use_global_device_ids=true | all-gather | bytes 614400 | tf_op jit(solution)/shard_map/all_gather | solution.py:526
  41.6 0.7 %strip.1 = (bf16[18,16,256]{2,1,0:T(8,128)(2,1)S(1)}, bf16[48,16,256]{2,1,0:T(8,128)(2,1)S(1)}, bf16[18,16,256]{2,1,0:T(8,128)(2,1)S(1)}, bf16[256,256]{1,0:T(8,128)(2,1)S(1)}) custom-call(bf16[48,32,256]{2,1,0:T(8,128)(2,1)S(1)} %get-tuple-element.30.o2, bf16[18,32,256]{2,1,0:T(8,128)(2,1)S(1)} %get-tuple-element.31.o1, ...), custom_call_target="tpu_custom_call" | custom-call | flops 339738624 | bytes 4194304 | tf_op jit(solution)/shard_map/strip/pallas_call | solution.py:531
  42.3 0.0 collective-permute-done.4.c_x
  42.3 1.7 %score.1 = (f32[8,640]{1,0:T(8,128)S(1)}, bf16[18,32,256]{2,1,0:T(8,128)(2,1)S(1)}) custom-call(bf16[48,32,256]{2,1,0:T(8,128)(2,1)S(1)} %get-tuple-element.30.o2, bf16[18,32,256]{2,1,0:T(8,128)(2,1)S(1)} %get-tuple-element.31.o1, f32[2,48,256]{2,1,0:T(8,128)S(1)} %get-tuple-element.32.ends2, f32[2,24,256]{2,1,0:T(8,128)S(1)} %get-tuple-element.33.ends1, ...), custom_call_target="tpu_custom_call" | custom-call | tf_op jit(solution)/shard_map/score/pallas_call | solution.py:550
  44.0 1.9 %collective-permute-start.5 = (f32[8,640]{1,0:T(8,128)S(1)}, f32[8,640]{1,0:T(8,128)S(1)}, u32[]{:S(2)}, u32[]{:S(2)}) collective-permute-start(f32[8,640]{1,0:T(8,128)S(1)} %get-tuple-element.39.sums.mine), channel_id=1, source_target_pairs={{1,2},{2,1},{3,4},{4,3},{5,6},{6,5},{7,8},{8,7},{9,10},{10,9},{11,... | collective-permute-start | bytes 61448 | tf_op jit(solution)/shard_map/ppermute | solution.py:560
  45.9 0.4 mix.1
  46.3 7.7 %all-gather.1 = f32[16,640]{1,0:T(8,128)S(1)} all-gather(f32[8,640]{1,0:T(8,128)S(1)} %get-tuple-element.41), channel_id=3, replica_groups={{0,1},{2,3},{4,5},{6,7},{8,9},{10,11},{12,13},{14,15},{16,17},{18,19},{..., dimensions={0}, use_global_device_ids=true | all-gather | bytes 61440 | tf_op jit(solution)/shard_map/all_gather | solution.py:578
  54.0 0.0 collective-permute-done.5.far
  54.0 1.3 %upsample.1 = f32[2,128,256]{2,1,0:T(8,128)} custom-call(f32[8,640]{1,0:T(8,128)S(1)} %get-tuple-element.39.sums.mine, f32[8,640]{1,0:T(8,128)S(1)} %collective-permute-done.5.far, f32[2,8,640]{2,1,0:T(8,128)S(1)} %bitcast.12, f32[9,8,8,512]{3,2,1,0:T(8,128)S(1)} %get-tuple-element.42.mix, f32[8,8,512]{2,1,0:T(8,128)S(1)} %get-tuple-element.43.inverse, ...), custom_call_target="tpu_custom_call" | custom-call | tf_op jit(solution)/shard_map/upsample/pallas_call | solution.py:579
Async XLA Ops:
  0.0 27.9 %copy-start = (bf16[3,3,256,256]{3,2,1,0:T(8,128)(2,1)S(1)}, bf16[3,3,256,256]{3,2,1,0:T(8,128)(2,1)}, u32[]{:S(2)}) copy-start(bf16[3,3,256,256]{3,2,1,0:T(8,128)(2,1)} %param.6) | copy-start | bytes 3538948
  1.2 20.1 %collective-permute-start = (bf16[18,32,256]{2,1,0:T(8,128)(2,1)S(1)}, bf16[18,32,256]{2,1,0:T(8,128)(2,1)S(1)}, u32[]{:S(2)}, u32[]{:S(2)}) collective-permute-start(bf16[18,32,256]{2,1,0:T(8,128)(2,1)S(1)} %get-tuple-element.27), channel_id=1, source_target_pairs={{32,64},{64,32},{96,128},{128,96},{160,192},{192,160},{224,256},{2... | collective-permute-start | bytes 884744 | tf_op jit(solution)/shard_map/ppermute | solution.py:478
  1.8 22.3 %collective-permute-start.1 = (bf16[18,32,256]{2,1,0:T(8,128)(2,1)S(1)}, bf16[18,32,256]{2,1,0:T(8,128)(2,1)S(1)}, u32[]{:S(2)}, u32[]{:S(2)}) collective-permute-start(bf16[18,32,256]{2,1,0:T(8,128)(2,1)S(1)} %get-tuple-element.26.f2), channel_id=1, source_target_pairs={{0,32},{32,0},{64,96},{96,64},{128,160},{160,128},{192,224},{224,1... | collective-permute-start | bytes 884744 | tf_op jit(solution)/shard_map/ppermute | solution.py:479
  10.0 9.7 %collective-permute-start.2 = (bf16[1,32,256]{2,1,0:T(8,128)(2,1)S(1)}, bf16[1,32,256]{2,1,0:T(8,128)(2,1)S(1)}, u32[]{:S(2)}, u32[]{:S(2)}) collective-permute-start(bf16[1,32,256]{2,1,0:T(8,128)(2,1)S(1)} %get-tuple-element.28), channel_id=1, source_target_pairs={{64,128},{128,64},{96,160},{160,96},{192,256},{256,192},{224,288},... | collective-permute-start | bytes 49160 | tf_op jit(solution)/shard_map/ppermute | solution.py:480
  10.7 10.6 %collective-permute-start.3 = (bf16[1,32,256]{2,1,0:T(8,128)(2,1)S(1)}, bf16[1,32,256]{2,1,0:T(8,128)(2,1)S(1)}, u32[]{:S(2)}, u32[]{:S(2)}) collective-permute-start(bf16[1,32,256]{2,1,0:T(8,128)(2,1)S(1)} %get-tuple-element.29), channel_id=1, source_target_pairs={{0,64},{64,0},{32,96},{96,32},{128,192},{192,128},{160,224},{224,1... | collective-permute-start | bytes 49160 | tf_op jit(solution)/shard_map/ppermute | solution.py:481
  24.3 18.0 %collective-permute-start.4 = (bf16[25,16,256]{2,1,0:T(8,128)(2,1)S(1)}, bf16[25,16,256]{2,1,0:T(8,128)(2,1)S(1)}, u32[]{:S(2)}, u32[]{:S(2)}) collective-permute-start(bf16[25,16,256]{2,1,0:T(8,128)(2,1)S(1)} %pack.1), channel_id=1, source_target_pairs={{1,2},{2,1},{3,4},{4,3},{5,6},{6,5},{7,8},{8,7},{9,10},{10,9},{11,... | collective-permute-start | bytes 614408 | tf_op jit(solution)/shard_map/ppermute | solution.py:496
  44.0 10.0 %collective-permute-start.5 = (f32[8,640]{1,0:T(8,128)S(1)}, f32[8,640]{1,0:T(8,128)S(1)}, u32[]{:S(2)}, u32[]{:S(2)}) collective-permute-start(f32[8,640]{1,0:T(8,128)S(1)} %get-tuple-element.39.sums.mine), channel_id=1, source_target_pairs={{1,2},{2,1},{3,4},{4,3},{5,6},{6,5},{7,8},{8,7},{9,10},{10,9},{11,... | collective-permute-start | bytes 61448 | tf_op jit(solution)/shard_map/ppermute | solution.py:560

commit v9 on v8

--- a/solution.py
+++ b/solution.py
@@ -316,10 +316,11 @@
             row = float((kb - 1) * BR + kr)
             both = [jnp.where(below, under[kr, i], over[kr, i]) for i in range(4)]
             now = [jnp.exp(jnp.where(of_right, both[2 + i], both[i])) for i in range(2)]
-            now += [jnp.where(is_own, jnp.exp(both[i]), 0.0) for i in range(2, 4)]
-            now += [row * ((now[0] + now[1]) + (now[2] + now[3]))]
+            now += [jnp.exp(both[i]) for i in range(2, 4)]
+            now += [row * (now[0] + now[1]), row * (now[2] + now[3])]
             acc = add(acc, now)
-    values = triple(acc[0:4], acc[4], sub, base)
+    acc[2], acc[3], acc[5] = (jnp.where(is_own, acc[i], 0.0) for i in (2, 3, 5))
+    values = triple(acc[0:4], acc[4] + acc[5], sub, base)
     for k, at in enumerate((0, cols + rows * cols)):
         for m in range(2):
             lo = (2 * k + m) * quarter

time: 55.7 us -> 55.7 us (level)
  no operation moved by 1% of the time
where the time goes in v9:
time: 55.7 us; the launch traced here: 55.3 us
  starting transfers between devices  22.9 us (41%)
  blocking collectives  18.3 us (33%)
  Pallas kernels  8.48 us (15%)
  waiting for transfers between devices  4.52 us (8%)
  local copies, waits for them, and re-layouts  1.03 us (2%)
    all_gather x1, blocking collectives, body(): col_in = lax.all_gather(m_in, 'lon', axis_index_groups=chips)  10.5 us
    ppermute x1, starting transfers between devices, body(): row_b = lax.ppermute(m_b, 'lat', near_lat)  8.15 us
    ppermute x1, starting transfers between devices, body(): row_d = lax.ppermute(m_d, 'lat', low_lat)  7.96 us
    all_gather x1, blocking collectives, body(): sums_in = lax.all_gather(sums_too, 'lon', axis_index_groups=chips)  7.72 us
    ppermute x1, starting transfers between devices, body(): col_x = lax.ppermute(m_x, 'lon', far_lon)  3.58 us
    pallas_call x1, Pallas kernels, body(): pl.pallas_call(functools.partial(own_kernel, rows, cols), out_shape=(arra...  3.09 us
    ppermute x1, waiting for transfers between devices, body(): row_b = lax.ppermute(m_b, 'lat', near_lat)  2.94 us
    ppermute x1, starting transfers between devices, body(): sums_far = lax.ppermute(sums, 'lon', far_lon)  1.92 us
  transfers between devices with their start and end apart: 6, of which 2 were waited for; matrix products, arithmetic and copies ran while one was open for 2% of the time, Pallas kernels for 8%

profile of v9, /device:TPU:1, one launch (start us, length us, event | category | flops | bytes accessed | tf_op | source)
XLA Modules:
  0.0 55.3 jit_solution(9893504672854582059)
XLA Ops:
  0.0 0.0 copy-start
  0.0 1.1 %edges.1 = (bf16[18,32,256]{2,1,0:T(8,128)(2,1)S(1)}, bf16[18,32,256]{2,1,0:T(8,128)(2,1)S(1)}, bf16[1,32,256]{2,1,0:T(8,128)(2,1)S(1)}, bf16[1,32,256]{2,1,0:T(8,128)(2,1)S(1)}, bf16[16,32,256]{2,1,0:T(8,128)(2,1)S(1)}) custom-call(bf16[16,32,256]{2,1,0:T(8,128)(2,1)} %f1.1, bf16[16,32,256]{2,1,0:T(8,128)(2,1)} %f2.1), custom_call_target="tpu_custom_call" | custom-call | tf_op jit(solution)/shard_map/edges/pallas_call | solution.py:467
  1.2 0.7 %collective-permute-start = (bf16[18,32,256]{2,1,0:T(8,128)(2,1)S(1)}, bf16[18,32,256]{2,1,0:T(8,128)(2,1)S(1)}, u32[]{:S(2)}, u32[]{:S(2)}) collective-permute-start(bf16[18,32,256]{2,1,0:T(8,128)(2,1)S(1)} %get-tuple-element.27), channel_id=1, source_target_pairs={{32,64},{64,32},{96,128},{128,96},{160,192},{192,160},{224,256},{2... | collective-permute-start | bytes 884744 | tf_op jit(solution)/shard_map/ppermute | solution.py:479
  1.8 8.2 %collective-permute-start.1 = (bf16[18,32,256]{2,1,0:T(8,128)(2,1)S(1)}, bf16[18,32,256]{2,1,0:T(8,128)(2,1)S(1)}, u32[]{:S(2)}, u32[]{:S(2)}) collective-permute-start(bf16[18,32,256]{2,1,0:T(8,128)(2,1)S(1)} %get-tuple-element.26.f2), channel_id=1, source_target_pairs={{0,32},{32,0},{64,96},{96,64},{128,160},{160,128},{192,224},{224,1... | collective-permute-start | bytes 884744 | tf_op jit(solution)/shard_map/ppermute | solution.py:480
  10.0 0.7 %collective-permute-start.2 = (bf16[1,32,256]{2,1,0:T(8,128)(2,1)S(1)}, bf16[1,32,256]{2,1,0:T(8,128)(2,1)S(1)}, u32[]{:S(2)}, u32[]{:S(2)}) collective-permute-start(bf16[1,32,256]{2,1,0:T(8,128)(2,1)S(1)} %get-tuple-element.28), channel_id=1, source_target_pairs={{64,128},{128,64},{96,160},{160,96},{192,256},{256,192},{224,288},... | collective-permute-start | bytes 49160 | tf_op jit(solution)/shard_map/ppermute | solution.py:481
  10.7 8.0 %collective-permute-start.3 = (bf16[1,32,256]{2,1,0:T(8,128)(2,1)S(1)}, bf16[1,32,256]{2,1,0:T(8,128)(2,1)S(1)}, u32[]{:S(2)}, u32[]{:S(2)}) collective-permute-start(bf16[1,32,256]{2,1,0:T(8,128)(2,1)S(1)} %get-tuple-element.29), channel_id=1, source_target_pairs={{0,64},{64,0},{32,96},{96,32},{128,192},{192,128},{160,224},{224,1... | collective-permute-start | bytes 49160 | tf_op jit(solution)/shard_map/ppermute | solution.py:482
  18.6 1.0 %copy.6 = bf16[256,9,8,8]{0,2,3,1:T(8,128)(2,1)S(1)} copy(bf16[256,9,8,8]{0,3,2,1:T(8,128)(2,1)} %bitcast.13) | data formatting | bytes 589824 | tf_op jit(solution)/shard_map/reshape | solution.py:563
  19.7 0.0 collective-permute-done.2.rc
  19.7 1.6 %collective-permute-done.3.rd = bf16[1,32,256]{2,1,0:T(8,128)(2,1)S(1)} collective-permute-done((bf16[1,32,256]{2,1,0:T(8,128)(2,1)S(1)}, bf16[1,32,256]{2,1,0:T(8,128)(2,1)S(1)}, u32[]{:S(2)}, u32[]{:S(2)}) %collective-permute-start.3) | collective-permute-done | bytes 16416 | tf_op jit(solution)/shard_map/ppermute | solution.py:482
  21.2 0.0 collective-permute-done.ra
  21.3 2.9 %collective-permute-done.1.rb = bf16[18,32,256]{2,1,0:T(8,128)(2,1)S(1)} collective-permute-done((bf16[18,32,256]{2,1,0:T(8,128)(2,1)S(1)}, bf16[18,32,256]{2,1,0:T(8,128)(2,1)S(1)}, u32[]{:S(2)}, u32[]{:S(2)}) %collective-permute-start.1) | collective-permute-done | bytes 294944 | tf_op jit(solution)/shard_map/ppermute | solution.py:480
  24.2 0.1 pack.1
  24.3 3.6 %collective-permute-start.4 = (bf16[25,16,256]{2,1,0:T(8,128)(2,1)S(1)}, bf16[25,16,256]{2,1,0:T(8,128)(2,1)S(1)}, u32[]{:S(2)}, u32[]{:S(2)}) collective-permute-start(bf16[25,16,256]{2,1,0:T(8,128)(2,1)S(1)} %pack.1), channel_id=1, source_target_pairs={{1,2},{2,1},{3,4},{4,3},{5,6},{6,5},{7,8},{8,7},{9,10},{10,9},{11,... | collective-permute-start | bytes 614408 | tf_op jit(solution)/shard_map/ppermute | solution.py:497
  27.9 0.0 copy-done
  27.9 3.1 %encode_own.1 = (bf16[48,32,256]{2,1,0:T(8,128)(2,1)S(1)}, bf16[18,32,256]{2,1,0:T(8,128)(2,1)S(1)}, f32[2,48,256]{2,1,0:T(8,128)S(1)}, f32[2,24,256]{2,1,0:T(8,...) custom-call(bf16[16,32,256]{2,1,0:T(8,128)(2,1)S(1)} %get-tuple-element.25.f1, ...), custom_call_target="tpu_custom_call" | custom-call | flops 2491416576 | bytes 4194304 | tf_op jit(solution)/shard_map/encode_own/pallas_call | solution.py:501
  31.0 10.5 %all-gather = bf16[50,16,256]{2,1,0:T(8,128)(2,1)S(1)} all-gather(bf16[25,16,256]{2,1,0:T(8,128)(2,1)S(1)} %get-tuple-element.35), channel_id=2, replica_groups={{0,1},{2,3},{4,5},{6,7},{8,9},{10,11},{12,13},{14,15},{16,17},{18,19},{..., dimensions={0}, use_global_device_ids=true | all-gather | bytes 614400 | tf_op jit(solution)/shard_map/all_gather | solution.py:527
  41.6 0.7 %strip.1 = (bf16[18,16,256]{2,1,0:T(8,128)(2,1)S(1)}, bf16[48,16,256]{2,1,0:T(8,128)(2,1)S(1)}, bf16[18,16,256]{2,1,0:T(8,128)(2,1)S(1)}, bf16[256,256]{1,0:T(8,128)(2,1)S(1)}) custom-call(bf16[48,32,256]{2,1,0:T(8,128)(2,1)S(1)} %get-tuple-element.30.o2, bf16[18,32,256]{2,1,0:T(8,128)(2,1)S(1)} %get-tuple-element.31.o1, ...), custom_call_target="tpu_custom_call" | custom-call | flops 339738624 | bytes 4194304 | tf_op jit(solution)/shard_map/strip/pallas_call | solution.py:532
  42.3 0.0 collective-permute-done.4.c_x
  42.3 1.7 %score.1 = (f32[8,640]{1,0:T(8,128)S(1)}, bf16[18,32,256]{2,1,0:T(8,128)(2,1)S(1)}) custom-call(bf16[48,32,256]{2,1,0:T(8,128)(2,1)S(1)} %get-tuple-element.30.o2, bf16[18,32,256]{2,1,0:T(8,128)(2,1)S(1)} %get-tuple-element.31.o1, f32[2,48,256]{2,1,0:T(8,128)S(1)} %get-tuple-element.32.ends2, f32[2,24,256]{2,1,0:T(8,128)S(1)} %get-tuple-element.33.ends1, ...), custom_call_target="tpu_custom_call" | custom-call | tf_op jit(solution)/shard_map/score/pallas_call | solution.py:551
  44.0 1.9 %collective-permute-start.5 = (f32[8,640]{1,0:T(8,128)S(1)}, f32[8,640]{1,0:T(8,128)S(1)}, u32[]{:S(2)}, u32[]{:S(2)}) collective-permute-start(f32[8,640]{1,0:T(8,128)S(1)} %get-tuple-element.39.sums.mine), channel_id=1, source_target_pairs={{1,2},{2,1},{3,4},{4,3},{5,6},{6,5},{7,8},{8,7},{9,10},{10,9},{11,... | collective-permute-start | bytes 61448 | tf_op jit(solution)/shard_map/ppermute | solution.py:561
  45.9 0.4 mix.1
  46.3 7.7 %all-gather.1 = f32[16,640]{1,0:T(8,128)S(1)} all-gather(f32[8,640]{1,0:T(8,128)S(1)} %get-tuple-element.41), channel_id=3, replica_groups={{0,1},{2,3},{4,5},{6,7},{8,9},{10,11},{12,13},{14,15},{16,17},{18,19},{..., dimensions={0}, use_global_device_ids=true | all-gather | bytes 61440 | tf_op jit(solution)/shard_map/all_gather | solution.py:579
  54.0 0.0 collective-permute-done.5.far
  54.0 1.3 %upsample.1 = f32[2,128,256]{2,1,0:T(8,128)} custom-call(f32[8,640]{1,0:T(8,128)S(1)} %get-tuple-element.39.sums.mine, f32[8,640]{1,0:T(8,128)S(1)} %collective-permute-done.5.far, f32[2,8,640]{2,1,0:T(8,128)S(1)} %bitcast.12, f32[9,8,8,512]{3,2,1,0:T(8,128)S(1)} %get-tuple-element.42.mix, f32[8,8,512]{2,1,0:T(8,128)S(1)} %get-tuple-element.43.inverse, ...), custom_call_target="tpu_custom_call" | custom-call | tf_op jit(solution)/shard_map/upsample/pallas_call | solution.py:580
Async XLA Ops:
  0.0 27.9 %copy-start = (bf16[3,3,256,256]{3,2,1,0:T(8,128)(2,1)S(1)}, bf16[3,3,256,256]{3,2,1,0:T(8,128)(2,1)}, u32[]{:S(2)}) copy-start(bf16[3,3,256,256]{3,2,1,0:T(8,128)(2,1)} %param.6) | copy-start | bytes 3538948
  1.2 20.1 %collective-permute-start = (bf16[18,32,256]{2,1,0:T(8,128)(2,1)S(1)}, bf16[18,32,256]{2,1,0:T(8,128)(2,1)S(1)}, u32[]{:S(2)}, u32[]{:S(2)}) collective-permute-start(bf16[18,32,256]{2,1,0:T(8,128)(2,1)S(1)} %get-tuple-element.27), channel_id=1, source_target_pairs={{32,64},{64,32},{96,128},{128,96},{160,192},{192,160},{224,256},{2... | collective-permute-start | bytes 884744 | tf_op jit(solution)/shard_map/ppermute | solution.py:479
  1.8 22.3 %collective-permute-start.1 = (bf16[18,32,256]{2,1,0:T(8,128)(2,1)S(1)}, bf16[18,32,256]{2,1,0:T(8,128)(2,1)S(1)}, u32[]{:S(2)}, u32[]{:S(2)}) collective-permute-start(bf16[18,32,256]{2,1,0:T(8,128)(2,1)S(1)} %get-tuple-element.26.f2), channel_id=1, source_target_pairs={{0,32},{32,0},{64,96},{96,64},{128,160},{160,128},{192,224},{224,1... | collective-permute-start | bytes 884744 | tf_op jit(solution)/shard_map/ppermute | solution.py:480
  10.0 9.7 %collective-permute-start.2 = (bf16[1,32,256]{2,1,0:T(8,128)(2,1)S(1)}, bf16[1,32,256]{2,1,0:T(8,128)(2,1)S(1)}, u32[]{:S(2)}, u32[]{:S(2)}) collective-permute-start(bf16[1,32,256]{2,1,0:T(8,128)(2,1)S(1)} %get-tuple-element.28), channel_id=1, source_target_pairs={{64,128},{128,64},{96,160},{160,96},{192,256},{256,192},{224,288},... | collective-permute-start | bytes 49160 | tf_op jit(solution)/shard_map/ppermute | solution.py:481
  10.7 10.6 %collective-permute-start.3 = (bf16[1,32,256]{2,1,0:T(8,128)(2,1)S(1)}, bf16[1,32,256]{2,1,0:T(8,128)(2,1)S(1)}, u32[]{:S(2)}, u32[]{:S(2)}) collective-permute-start(bf16[1,32,256]{2,1,0:T(8,128)(2,1)S(1)} %get-tuple-element.29), channel_id=1, source_target_pairs={{0,64},{64,0},{32,96},{96,32},{128,192},{192,128},{160,224},{224,1... | collective-permute-start | bytes 49160 | tf_op jit(solution)/shard_map/ppermute | solution.py:482
  24.3 18.0 %collective-permute-start.4 = (bf16[25,16,256]{2,1,0:T(8,128)(2,1)S(1)}, bf16[25,16,256]{2,1,0:T(8,128)(2,1)S(1)}, u32[]{:S(2)}, u32[]{:S(2)}) collective-permute-start(bf16[25,16,256]{2,1,0:T(8,128)(2,1)S(1)} %pack.1), channel_id=1, source_target_pairs={{1,2},{2,1},{3,4},{4,3},{5,6},{6,5},{7,8},{8,7},{9,10},{10,9},{11,... | collective-permute-start | bytes 614408 | tf_op jit(solution)/shard_map/ppermute | solution.py:497
  44.0 10.0 %collective-permute-start.5 = (f32[8,640]{1,0:T(8,128)S(1)}, f32[8,640]{1,0:T(8,128)S(1)}, u32[]{:S(2)}, u32[]{:S(2)}) collective-permute-start(f32[8,640]{1,0:T(8,128)S(1)} %get-tuple-element.39.sums.mine), channel_id=1, source_target_pairs={{1,2},{2,1},{3,4},{4,3},{5,6},{6,5},{7,8},{8,7},{9,10},{10,9},{11,... | collective-permute-start | bytes 61448 | tf_op jit(solution)/shard_map/ppermute | solution.py:561
